TPU v7x, 256 devices: a whole 4x4x8 slice. The times are simulated.
256 devices in a mesh: lat: 16 (over y, x), lon: 4 (over z_hi, core), ch: 4 (over z_lo).
Axes of the slice: x: 4, y: 4, z: 8 (z_hi: 2, z_lo: 4; z = z_hi * 4 + z_lo), core: 2. Of those that a mesh axis runs over, the one named last changes fastest.
Arguments:
- tokens: bfloat16 [384, 768, 512], P('lat', 'ch', 'lon'), may hold values from -6 to 6
- gain_first: float32 [768], P('ch'), may hold values from 0.25 to 1.75
- mode_first: float32 [8, 18432], P('ch'), may hold values from -0.4375 to 0.4375
- mode_second: float32 [8, 18432], P('ch'), may hold values from -0.4375 to 0.4375
- kept_lat: int32 [288], replicated, may hold values from 0 to 383, as said below
- gain_second: float32 [768], replicated, may hold values from 0.25 to 1.75
- w_up: bfloat16 [768, 3072], P(None, 'ch'), may hold values from -0.21875 to 0.21875
- w_down: bfloat16 [3072, 768], P('ch'), may hold values from -0.109375 to 0.109375
Outputs:
- result: bfloat16 [384, 768, 512], P('lat', 'ch', 'lon')
Inputs may be any that keep to these rules, and one draw needn't show every extreme that they name: `kept_lat`: 288 distinct latitude wavenumbers in any order; 0 and 383 are always among them.
All inputs are finite; a program needn't handle non-finite values.
Results may differ from a plain program's by a relative error of at most 0.015.
Values may be sent and summed in bfloat16 or wider, within the bound.
No kernel may reach another device: no remote copies, remote signals or barrier semaphores. Data moves between devices by JAX's collectives and lax.ppermute only.
A program may use at most 128 MiB of HBM per device.

v0:
```python
import math

import jax
import jax.numpy as jnp
from jax import lax
from jax.sharding import PartitionSpec as P

BS = 96
KW = 256


SHRINK = 0.01
EPSILON = 1e-05
HIGH = lax.Precision.HIGH


def twiddle(first, second, length):
    phase = first[:, None] * second[None, :] % length
    angle = phase.astype(jnp.float32) * (2.0 * math.pi / length)
    return (jnp.cos(angle), jnp.sin(angle))


def complex_block(real, imag, weight):
    w_real = weight[:, 0]
    w_imag = weight[:, 1]

    def product(left, right):
        return jnp.einsum("pkbi,bio->pkbo", left, right, precision=HIGH)

    return (
        product(real, w_real) - product(imag, w_imag),
        product(real, w_imag) + product(imag, w_real),
    )


def shrink(values):
    return jnp.where(
        values > SHRINK, values - SHRINK, jnp.where(values < -SHRINK, values + SHRINK, 0.0)
    )


def along(table, values):
    return jnp.einsum("ph,hkc->pkc", table, values, precision=HIGH)


def spectral(columns, kept_lat, mode_first, mode_second):
    height, parts, mode_cols, chans = columns.shape
    cosine, sine = twiddle(kept_lat, jnp.arange(height, dtype=jnp.int32), height)
    factor = 1.0 / math.sqrt(height)
    cosine = cosine * factor
    sine = sine * factor
    real = columns[:, 0]
    imag = columns[:, 1]
    fwd_real = along(cosine, real) + along(sine, imag)
    fwd_imag = along(cosine, imag) - along(sine, real)
    blocks = mode_first.shape[0]
    first_w = mode_first.reshape(blocks, 2, BS, BS)
    second_w = mode_second.reshape(blocks, 2, BS, BS)
    shape = (fwd_real.shape[0], mode_cols, blocks, BS)
    inner_real, inner_imag = complex_block(
        fwd_real.reshape(shape), fwd_imag.reshape(shape), first_w
    )
    inner_real = jnp.maximum(inner_real, 0.0)
    inner_imag = jnp.maximum(inner_imag, 0.0)
    out_real, out_imag = complex_block(inner_real, inner_imag, second_w)
    out_real = shrink(out_real).reshape(fwd_real.shape)
    out_imag = shrink(out_imag).reshape(fwd_real.shape)
    back_real = along(cosine.T, out_real) - along(sine.T, out_imag)
    back_imag = along(cosine.T, out_imag) + along(sine.T, out_real)
    return jnp.stack([back_real, back_imag], axis=1)


def norm_middle(block, gain):
    values = block.astype(jnp.float32)
    mean = jnp.mean(values, axis=1, keepdims=True)
    spread = jnp.mean((values - mean) * (values - mean), axis=1, keepdims=True)
    return ((values - mean) * lax.rsqrt(spread + EPSILON) * gain[None, :, None]).astype(
        jnp.bfloat16
    )


def on_device(tokens, gain_first, mode_first, mode_second, kept_lat, gain_second, w_up, w_down):
    rows, chans, cols = tokens.shape
    lon_count = lax.axis_size("lon")
    full_chans = chans * lax.axis_size("ch")
    width = cols * lon_count
    values = tokens.astype(jnp.float32)
    total, square = lax.psum((jnp.sum(values, axis=1), jnp.sum(values * values, axis=1)), "ch")
    mean = total / full_chans
    spread = square / full_chans - mean * mean
    normed = (
        (values - mean[:, None, :])
        * lax.rsqrt(spread + EPSILON)[:, None, :]
        * gain_first[None, :, None]
    ).astype(jnp.bfloat16)
    strips = lax.all_to_all(normed, "lon", split_axis=0, concat_axis=2, tiled=True)
    cos_lon, sin_lon = twiddle(
        jnp.arange(width, dtype=jnp.int32), jnp.arange(KW, dtype=jnp.int32), width
    )
    factor = 1.0 / math.sqrt(width)
    forward_table = jnp.stack([cos_lon, -sin_lon], axis=1) * factor
    spec = jnp.einsum("rcw,wtk->rtkc", strips.astype(jnp.float32), forward_table, precision=HIGH)
    columns = lax.all_to_all(
        spec.astype(jnp.bfloat16), ("lat", "lon"), split_axis=2, concat_axis=0, tiled=True
    ).astype(spec.dtype)
    mixed = spectral(columns, kept_lat, mode_first, mode_second)
    returned = lax.all_to_all(
        mixed.astype(jnp.bfloat16), ("lat", "lon"), split_axis=0, concat_axis=2, tiled=True
    ).astype(mixed.dtype)
    weights_k = jnp.where(jnp.arange(KW) == 0, 1.0, 2.0).astype(jnp.float32) * factor
    inverse_table = jnp.stack(
        [cos_lon.T * weights_k[:, None], -sin_lon.T * weights_k[:, None]], axis=0
    )
    field = jnp.einsum("rtkc,tkw->rcw", returned, inverse_table, precision=HIGH).astype(
        jnp.bfloat16
    )
    restored = lax.all_to_all(field, "lon", split_axis=2, concat_axis=0, tiled=True)
    first = (values + normed.astype(jnp.float32) + restored.astype(jnp.float32)).astype(
        jnp.bfloat16
    )
    feats = lax.all_gather(first, "ch", axis=1, tiled=True)
    ready = norm_middle(feats, gain_second)
    hidden = jax.nn.gelu(
        jnp.einsum("rcw,cf->rwf", ready, w_up, preferred_element_type=jnp.float32)
    ).astype(jnp.bfloat16)
    partial_terms = jnp.einsum("rwf,fc->rcw", hidden, w_down, preferred_element_type=jnp.float32)
    summed = lax.psum_scatter(
        partial_terms.astype(jnp.bfloat16), "ch", scatter_dimension=1, tiled=True
    ).astype(jnp.float32)
    output = (first.astype(jnp.float32) + summed).astype(jnp.bfloat16)
    return output


def solution(mesh):
    return jax.shard_map(
        on_device,
        mesh=mesh,
        in_specs=(
            P("lat", "ch", "lon"),
            P("ch"),
            P("ch", None),
            P("ch", None),
            P(),
            P(),
            P(None, "ch"),
            P("ch", None),
        ),
        out_specs=P("lat", "ch", "lon"),
        check_vma=False,
    )
```

profile of v0, /device:TPU:96, one launch (start us, length us, event | category | flops | bytes accessed | tf_op | source)
XLA Modules:
  0.0 505.7 jit_solution(1830508166985267767)
XLA Ops:
  6.5 1.8 convert_reduce_fusion.1
  8.3 15.4 %all-reduce = (f32[24,128]{1,0:T(8,128)S(1)}, f32[24,128]{1,0:T(8,128)S(1)}) all-reduce(f32[24,128]{1,0:T(8,128)S(1)} %get-tuple-element.6, f32[24,128]{1,0:T(8,128)S(1)} %get-tuple-element.5), channel_id=1, replica_groups=mesh['lat'=16,'lon'=4,'ch'=4] {'ch'}, use_global_device_ids=true, to_apply=%region_3.0 | all-reduce | flops 6144 | bytes 49152 | tf_op jit(solution)/shard_map/psum | solution.py:88
  23.8 0.6 copy-done.20
  24.4 1.5 fusion.25
  25.9 5.9 %all-to-all-start = ((bf16[24,192,128]{2,1,0:T(8,128)(2,1)}), bf16[24,192,128]{2,1,0:T(8,128)(2,1)S(1)}, u32[]{:S(2)}, u32[]{:S(2)}) async-start(bf16[24,192,128]{2,1,0:T(8,128)(2,1)} %fusion.25), calls=%async_computation | async-start | bytes 2359296 | tf_op jit(solution)/shard_map/all_to_all | solution.py:96
  31.8 2.9 sine_negate_fusion
  34.7 27.7 %all-to-all-done = bf16[24,192,128]{2,1,0:T(8,128)(2,1)S(1)} async-done(((bf16[24,192,128]{2,1,0:T(8,128)(2,1)}), bf16[24,192,128]{2,1,0:T(8,128)(2,1)S(1)}, u32[]{:S(2)}, u32[]{:S(2)}) %all-to-all-start) | async-done | bytes 1179680 | tf_op jit(solution)/shard_map/all_to_all | solution.py:96
  62.5 1.9 copy.149
  64.4 2.5 reshape.238
  66.9 3.6 fusion.34
  70.5 4.9 copy.78
  75.4 8.5 %all-to-all-start.1 = ((bf16[6,2,256,192]{3,1,0,2:T(2,128)(2,1)}), bf16[6,2,256,192]{3,1,0,2:T(2,128)(2,1)}, u32[]{:S(2)}, u32[]{:S(2)}) async-start(bf16[6,2,256,192]{3,1,0,2:T(2,128)(2,1)} %copy.78), calls=%async_computation.1 | async-start | bytes 3145728 | tf_op jit(solution)/shard_map/all_to_all | solution.py:103
  83.9 0.2 reshape.230
  84.1 0.2 reshape.232
  84.3 28.0 %all-to-all-done.1 = bf16[6,2,256,192]{3,1,0,2:T(2,128)(2,1)} async-done(((bf16[6,2,256,192]{3,1,0,2:T(2,128)(2,1)}), bf16[6,2,256,192]{3,1,0,2:T(2,128)(2,1)}, u32[]{:S(2)}, u32[]{:S(2)}) %all-to-all-start.1) | async-done | bytes 1179680 | tf_op jit(solution)/shard_map/all_to_all | solution.py:103
  112.3 2.2 copy.80
  114.5 1.4 fusion.165
  115.9 2.2 copy.125
  118.1 4.7 fusion.80
  122.8 3.5 fusion.77
  126.3 1.8 copy.126
  128.2 3.7 fusion.76
  131.9 2.5 fusion.81
  134.4 0.1 add.112
  134.5 1.3 fusion.44
  135.8 1.3 fusion.46
  137.2 1.3 fusion.38
  138.5 1.6 fusion.124
  140.2 0.6 fusion.123
  140.8 0.3 copy-done.11
  141.1 1.3 fusion.36
  142.4 2.1 select_bitcast_fusion.1
  144.5 2.7 copy.93
  147.3 5.3 %fusion.78 = f32[384,768]{0,1} fusion(f32[288,768]{0,1:T(8,128)} %bitcast.131, s32[288]{0:T(512)S(1)} %copy-done.21), kind=kOutput, calls=%fused_computation.105 | convolution fusion | flops 510713856 | bytes 2065536
  152.6 3.9 fusion.75
  156.5 1.9 select_bitcast_fusion
  158.4 1.7 copy.96
  160.1 2.9 fusion.74
  163.1 3.2 fusion.79
  166.3 0.2 fusion.54
  166.5 1.1 copy-done.5
  167.5 0.2 fusion.55
  167.7 0.1 pad_maximum_fusion
  167.8 2.5 copy.97
  170.4 5.5 %all-to-all-start.2 = ((bf16[384,2,4,192]{3,2,1,0:T(4,128)(2,1)}), bf16[384,2,4,192]{3,2,1,0:T(4,128)(2,1)}, u32[]{:S(2)}, u32[]{:S(2)}) async-start(bf16[384,2,4,192]{3,2,1,0:T(4,128)(2,1)} %copy.97), calls=%async_computation.2 | async-start | bytes 3145728 | tf_op jit(solution)/shard_map/all_to_all | solution.py:107
  175.9 3.0 cosine_multiply_fusion
  179.0 24.7 %all-to-all-done.2 = bf16[384,2,4,192]{3,2,1,0:T(4,128)(2,1)} async-done(((bf16[384,2,4,192]{3,2,1,0:T(4,128)(2,1)}), bf16[384,2,4,192]{3,2,1,0:T(4,128)(2,1)}, u32[]{:S(2)}, u32[]{:S(2)}) %all-to-all-start.2) | async-done | bytes 1179680 | tf_op jit(solution)/shard_map/all_to_all | solution.py:107
  203.7 3.1 copy.98
  206.9 1.6 bitcast_convert_fusion
  208.4 3.0 copy.100
  211.4 56.5 %all_to_all.63 = bf16[6,192,512]{1,0,2:T(8,128)(2,1)} all-to-all(bf16[6,192,512]{1,0,2:T(8,128)(2,1)} %copy.100), channel_id=1, replica_groups=mesh['lat'=16,'lon'=4,'ch'=4] {'lon'}, dimensions={2} | all-to-all | bytes 2359296 | tf_op jit(solution)/shard_map/all_to_all | solution.py:117
  267.9 4.5 copy.101
  272.4 2.3 fusion.28
  274.7 1.8 copy.102
  276.5 0.3 reduce-scatter.2.cloned.1.call-start
  276.8 97.9 %all-gather.2.cloned.1.call-done = bf16[24,768,128]{2,0,1:T(8,128)(2,1)} async-done(((bf16[24,192,128]{2,0,1:T(8,128)(2,1)}), bf16[24,768,128]{2,0,1:T(8,128)(2,1)}) %all-gather.2.cloned.1.call-update) | async-done | bytes 4718608 | tf_op jit(solution)/shard_map/all_gather | solution.py:121
  374.7 3.3 convert_reduce_fusion
  378.0 0.4 copy-done.1
  378.5 1.3 fusion.2
  379.8 4.0 fusion.4
  383.8 13.7 %convert_bitcast_fusion = bf16[24,768,128]{1,2,0:T(8,128)(2,1)} fusion(bf16[24,768,128]{2,0,1:T(8,128)(2,1)} %fusion.4, bf16[768,768]{1,0:T(8,128)(2,1)S(1)} %copy-done, bf16[768,768]{1,0:T(8,128)(2,1)} %param.14), kind=kOutput, calls=%fused_computation.19 | convolution fusion | flops 7271350272 | bytes 11796480 | tf_op jit(solution)/shard_map/rwf,fc->rcw/dot_general | solution.py:126
  397.5 6.9 %copy.104 = bf16[24,768,128]{2,0,1:T(8,128)(2,1)} copy(bf16[24,768,128]{1,2,0:T(8,128)(2,1)} %convert_bitcast_fusion) | data formatting | bytes 9437184 | tf_op jit(solution)/shard_map/convert_element_type | solution.py:128
  404.5 91.3 %reduce-scatter.2.cloned.1.call-done = bf16[24,192,128]{2,0,1:T(8,128)(2,1)} async-done(((bf16[24,768,128]{2,0,1:T(8,128)(2,1)}), bf16[24,192,128]{2,0,1:T(8,128)(2,1)}) %reduce-scatter.2.cloned.1.call-update) | async-done | bytes 1179664 | tf_op jit(solution)/shard_map/reduce_scatter | solution.py:127
  495.8 2.6 add_convert_fusion
  (54 shorter events, 0.3 us)
Async XLA Ops:
  6.5 377.2 %copy-start = (bf16[768,768]{1,0:T(8,128)(2,1)S(1)}, bf16[768,768]{1,0:T(8,128)(2,1)}, u32[]{:S(2)}) copy-start(bf16[768,768]{1,0:T(8,128)(2,1)} %param.15) | copy-start | bytes 3538948
  6.5 17.8 %copy-start.2 = (bf16[24,192,128]{2,1,0:T(8,128)(2,1)S(1)}, bf16[24,192,128]{2,1,0:T(8,128)(2,1)}, u32[]{:S(2)}) copy-start(bf16[24,192,128]{2,1,0:T(8,128)(2,1)} %param.8) | copy-start | bytes 3538948
  6.5 17.8 %copy-start.23 = (f32[192]{0:T(256)S(1)}, f32[192]{0:T(256)}, u32[]{:S(2)}) copy-start(f32[192]{0:T(256)} %param.9) | copy-start | bytes 2308
  23.8 0.6 copy-start.20
  25.9 36.6 %all-to-all-start = ((bf16[24,192,128]{2,1,0:T(8,128)(2,1)}), bf16[24,192,128]{2,1,0:T(8,128)(2,1)S(1)}, u32[]{:S(2)}, u32[]{:S(2)}) async-start(bf16[24,192,128]{2,1,0:T(8,128)(2,1)} %fusion.25), calls=%async_computation | async-start | bytes 2359296 | tf_op jit(solution)/shard_map/all_to_all | solution.py:96
  75.4 8.5 %copy-start.18 = (f32[2,18432]{1,0:T(2,128)S(1)}, f32[2,18432]{1,0:T(2,128)}, u32[]{:S(2)}) copy-start(f32[2,18432]{1,0:T(2,128)} %param.10) | copy-start | bytes 442372
  75.4 8.7 %copy-start.19 = (f32[2,18432]{1,0:T(2,128)S(1)}, f32[2,18432]{1,0:T(2,128)}, u32[]{:S(2)}) copy-start(f32[2,18432]{1,0:T(2,128)} %param.11) | copy-start | bytes 442372
  75.4 36.9 %all-to-all-start.1 = ((bf16[6,2,256,192]{3,1,0,2:T(2,128)(2,1)}), bf16[6,2,256,192]{3,1,0,2:T(2,128)(2,1)}, u32[]{:S(2)}, u32[]{:S(2)}) async-start(bf16[6,2,256,192]{3,1,0,2:T(2,128)(2,1)} %copy.78), calls=%async_computation.1 | async-start | bytes 3145728 | tf_op jit(solution)/shard_map/all_to_all | solution.py:103
  84.1 53.1 %copy-start.10 = (f32[2,2,96,96]{3,2,1,0:T(8,128)}, f32[2,2,96,96]{3,2,1,0:T(8,128)S(1)}, u32[]{:S(2)}) copy-start(f32[2,2,96,96]{3,2,1,0:T(8,128)S(1)} %reshape.230) | copy-start | bytes 442372
  84.3 55.9 %copy-start.7 = (f32[2,2,96,96]{3,2,1,0:T(8,128)}, f32[2,2,96,96]{3,2,1,0:T(8,128)S(1)}, u32[]{:S(2)}) copy-start(f32[2,2,96,96]{3,2,1,0:T(8,128)S(1)} %reshape.232) | copy-start | bytes 442372
  115.9 2.2 copy-start.21
  118.1 4.7 copy-start.14
  128.2 3.7 copy-start.15
  131.8 2.6 copy-start.13
  135.8 1.3 copy-start.12
  140.2 0.9 copy-start.11
  141.1 1.3 copy-start.8
  147.2 5.3 %copy-start.3 = (f32[288,4,2,96]{0,3,2,1:T(8,128)S(1)}, f32[288,4,2,96]{0,3,2,1:T(8,128)}, u32[]{:S(2)}) copy-start(f32[288,4,2,96]{0,3,2,1:T(8,128)} %copy.93) | copy-start | bytes 2654212
  152.6 3.9 copy-start.4
  152.6 3.9 copy-start.9
  163.1 3.2 copy-start.6
  166.3 1.3 copy-start.5
  170.4 33.3 %all-to-all-start.2 = ((bf16[384,2,4,192]{3,2,1,0:T(4,128)(2,1)}), bf16[384,2,4,192]{3,2,1,0:T(4,128)(2,1)}, u32[]{:S(2)}, u32[]{:S(2)}) async-start(bf16[384,2,4,192]{3,2,1,0:T(4,128)(2,1)} %copy.97), calls=%async_computation.2 | async-start | bytes 3145728 | tf_op jit(solution)/shard_map/all_to_all | solution.py:107
  175.9 198.8 %all-gather.2.cloned.1.call-start = ((), (), s32[]{:S(2)}) async-start(), calls=%async_computation.5 | async-start | bytes 5898240 | tf_op jit(solution)/shard_map/all_gather | solution.py:121
  203.7 3.1 copy-start.16
  203.7 3.1 copy-start.17
  267.9 4.5 copy-start.24
  276.5 219.3 %reduce-scatter.2.cloned.1.call-start = ((), (), s32[]{:S(2)}) async-start(), calls=%async_computation.6 | async-start | bytes 5898240 | tf_op jit(solution)/shard_map/reduce_scatter | solution.py:127
  374.7 3.8 copy-start.1
  378.5 1.3 copy-start.22
Sparse Core Ops, SparseCore 0:
  276.6 98.0 all-gather.1
  404.6 91.1 reduce-scatter.1
where the time goes:
time: 515 us; the launch traced here: 506 us
  waiting for transfers between devices  270 us (52%)
  blocking collectives  72 us (14%)
  matrix products  60.1 us (12%)
  local copies, waits for them, and re-layouts  46 us (9%)
  other arithmetic  23.5 us (5%)
  starting transfers between devices  20.3 us (4%)
  between operations  14.2 us (3%)
    all_gather x1, waiting for transfers between devices, on_device(): feats = lax.all_gather(first, 'ch', axis=1, tiled=True)  97.9 us
    reduce_scatter x1, waiting for transfers between devices, on_device(): lax.psum_scatter(partial_terms.astype(jnp.bfloat16), 'ch', scatter_dimens...  91.3 us
    all_to_all x1, blocking collectives, on_device(): lax.all_to_all(field, 'lon', split_axis=2, concat_axis=0, tiled=True)  56.5 us
    unnamed x8, matrix products  29.8 us
    all_to_all x1, waiting for transfers between devices, on_device(): lax.all_to_all(spec.astype(jnp.bfloat16), ('lat', 'lon'), split_axis=2, c...  28 us
    all_to_all x1, waiting for transfers between devices, on_device(): lax.all_to_all(normed, 'lon', split_axis=0, concat_axis=2, tiled=True)  27.7 us
    all_to_all x1, waiting for transfers between devices, on_device(): lax.all_to_all(mixed.astype(jnp.bfloat16), ('lat', 'lon'), split_axis=0,...  24.7 us
    psum x1, blocking collectives, on_device(): lax.psum((jnp.sum(values, axis=1), jnp.sum(values * values, axis=1)), 'ch')  15.4 us
  transfers between devices with their start and end apart: 5, of which 5 were waited for; matrix products, arithmetic and copies ran while one was open for 1% of the time, Pallas kernels for 0%

commit v1 on v0

v1 whole, which is shorter than its diff:
```python
import math

import jax
import jax.numpy as jnp
import numpy as np
from jax import lax
from jax.sharding import Mesh, PartitionSpec as P

BS = 96
KW = 256
SHRINK = 0.01
EPSILON = 1e-05
BF16 = jnp.bfloat16
F32 = jnp.float32


def dot(left, right, dims):
    return lax.dot_general(left, right, (dims, ((), ())), preferred_element_type=F32)


def lon_tables(width, dests):
    k = np.arange(KW)
    angle = 2.0 * np.pi * (k[:, None] * np.arange(width)[None, :] % width) / width
    both = np.stack([np.cos(angle), -np.sin(angle)]) / math.sqrt(width)
    forward = both.reshape(2, dests, KW // dests, width).transpose(1, 0, 2, 3)
    weights = np.where(k == 0, 1.0, 2.0)
    inverse = (both * weights[None, :, None]).reshape(2, dests, KW // dests, width)
    inverse = inverse.transpose(1, 0, 2, 3)
    return forward.reshape(2 * KW, width), inverse.reshape(2 * KW, width)


def lat_tables(kept_lat, height):
    h = np.arange(height)
    angle = 2.0 * np.pi * (h[:, None] * h[None, :] % height) / height
    table = np.stack([np.cos(angle), np.sin(angle)], axis=1) / math.sqrt(height)
    table = jnp.asarray(table.reshape(height, 2 * height), BF16)
    pick = (kept_lat[:, None] == jnp.arange(height)[None, :]).astype(BF16)
    kept = dot(pick, table, ((1,), (0,))).astype(BF16)
    return kept[:, :height], kept[:, height:]


def shrink(values):
    return jnp.where(
        values > SHRINK, values - SHRINK, jnp.where(values < -SHRINK, values + SHRINK, 0.0)
    )


def mode_product(values, weight):
    full = jnp.concatenate(
        [
            jnp.concatenate([weight[0], weight[1]], axis=1),
            jnp.concatenate([-weight[1], weight[0]], axis=1),
        ],
        axis=0,
    ).astype(BF16)
    return dot(values.astype(BF16), full, ((2,), (0,)))


def on_device(tokens, gain_first, mode_first, mode_second, kept_lat, gain_second, w_up, w_down):
    rows, chans, cols = tokens.shape
    lat_n, zh_n, co_n, ch_n = (lax.axis_size(a) for a in ("lat", "zh", "co", "ch"))
    lon_n = zh_n * co_n
    width = cols * lon_n
    height = rows * lat_n
    full = chans * ch_n
    dests = lat_n * co_n
    half = rows // co_n
    trip = half // ch_n
    hidden_n = w_up.shape[1]
    zh, co = lax.axis_index("zh"), lax.axis_index("co")

    piece_n = hidden_n // dests
    piece_at = (co * lat_n + lax.axis_index("lat")) * piece_n
    up_piece = lax.dynamic_slice_in_dim(w_up.T, piece_at, piece_n, axis=0)
    down_piece = lax.dynamic_slice_in_dim(w_down.T, piece_at, piece_n, axis=0)
    weights = jnp.stack([up_piece, down_piece])
    weights = lax.all_gather(weights, "ch")
    weights = lax.all_gather(weights, "lat")
    weights = lax.all_gather(weights, "co")

    values = tokens.astype(F32)
    sums = jnp.stack([jnp.sum(values, axis=1), jnp.sum(values * values, axis=1)])
    sums = lax.all_gather(sums, ("zh", "co", "ch"))
    sums = sums.reshape(lon_n, ch_n, 2, ch_n, co_n, trip, cols).sum(axis=1)
    sums = lax.dynamic_index_in_dim(sums, co, axis=3, keepdims=False)
    sums = sums.reshape(lon_n, 2, half, cols) / full
    mean = sums[:, 0]
    scale = lax.rsqrt(sums[:, 1] - mean * mean + EPSILON)

    parts = tokens.reshape(ch_n, co_n, trip, zh_n, BS, cols).transpose(3, 1, 0, 2, 4, 5)
    parts = parts.reshape(lon_n, half, BS, cols)
    strips = lax.all_to_all(parts, ("zh", "co"), split_axis=0, concat_axis=0, tiled=True)
    gain = lax.dynamic_slice_in_dim(gain_first, zh * BS, BS)
    strips = strips.astype(F32)
    normed = (
        (strips - mean[:, :, None, :]) * scale[:, :, None, :] * gain[None, None, :, None]
    ).astype(BF16)

    forward, inverse = lon_tables(width, dests)
    forward = jnp.asarray(forward, BF16).reshape(2 * KW, lon_n, cols)
    inverse = jnp.asarray(inverse, BF16)
    spec = jnp.einsum("mlw,lrcw->mrc", forward, normed, preferred_element_type=F32)
    spec = spec.astype(BF16).reshape(dests, 2 * KW // dests, half * BS)
    columns = lax.all_to_all(spec, ("lat", "co"), split_axis=0, concat_axis=0, tiled=True)

    modes = KW // dests
    columns = columns.reshape(lat_n, co_n, 2, modes, ch_n, trip, BS)
    columns = columns.transpose(2, 0, 4, 1, 5, 3, 6).reshape(2, height, modes * BS)
    cosine, sine = lat_tables(kept_lat, height)
    left = jnp.concatenate(
        [jnp.concatenate([cosine, sine], axis=1), jnp.concatenate([-sine, cosine], axis=1)], axis=0
    )
    kept = kept_lat.shape[0]
    moved = dot(left, columns.reshape(2 * height, modes * BS), ((1,), (0,)))
    moved = moved.reshape(2, kept, modes, BS).transpose(1, 2, 0, 3).reshape(kept, modes, 2 * BS)
    first_w = lax.dynamic_index_in_dim(mode_first, zh, axis=0, keepdims=False).reshape(2, BS, BS)
    second_w = lax.dynamic_index_in_dim(mode_second, zh, axis=0, keepdims=False).reshape(2, BS, BS)
    inner = jnp.maximum(mode_product(moved, first_w), 0.0)
    outer = shrink(mode_product(inner, second_w)).astype(BF16)
    outer = outer.reshape(kept, modes, 2, BS).transpose(2, 0, 1, 3).reshape(2 * kept, modes * BS)
    back = dot(left, outer, ((0,), (0,))).astype(BF16)
    back = back.reshape(2, lat_n, ch_n, co_n, trip, modes, BS).transpose(1, 3, 0, 5, 2, 4, 6)
    back = back.reshape(dests, 2 * modes, half * BS)
    returned = lax.all_to_all(back, ("lat", "co"), split_axis=0, concat_axis=0, tiled=True)

    returned = returned.reshape(2 * KW, half * BS)
    field = dot(returned, inverse, ((0,), (0,))).astype(BF16)
    field = field.reshape(half, BS, lon_n, cols).transpose(2, 0, 1, 3)
    first = (strips + normed.astype(F32) + field.astype(F32)).astype(BF16)
    first = first.reshape(lon_n, ch_n, trip, BS, cols)
    first = first.reshape(lon_n * ch_n, trip, BS, cols)
    whole = lax.all_to_all(first, ("zh", "co", "ch"), split_axis=0, concat_axis=0, tiled=True)
    whole = whole.reshape(zh_n, co_n, ch_n, trip, BS, cols).transpose(1, 3, 2, 0, 4, 5)
    whole = whole.reshape(co_n * trip, full, cols).astype(F32)

    center = jnp.mean(whole, axis=1, keepdims=True)
    spread = jnp.mean((whole - center) * (whole - center), axis=1, keepdims=True)
    ready = ((whole - center) * lax.rsqrt(spread + EPSILON) * gain_second[None, :, None]).astype(
        BF16
    )
    weights = weights.transpose(3, 2, 0, 1, 4, 5).reshape(2, ch_n, -1, full)
    hidden = jnp.einsum("gfc,rcw->gfrw", weights[0], ready, preferred_element_type=F32)
    hidden = jax.nn.gelu(hidden).astype(BF16)
    mixed = jnp.einsum("gcf,gfrw->rcw", weights[1], hidden, preferred_element_type=F32)
    result = (whole + mixed).astype(BF16)
    result = result.reshape(co_n * trip, ch_n, chans, cols).transpose(1, 0, 2, 3)
    result = lax.all_to_all(result, "ch", split_axis=0, concat_axis=0, tiled=True)
    return result.reshape(rows, chans, cols)


def solution(mesh):
    grid = mesh.devices
    lat_n, lon_n, ch_n = grid.shape
    split = Mesh(grid.reshape(lat_n, 2, lon_n // 2, ch_n), ("lat", "zh", "co", "ch"))
    lon = ("zh", "co")
    return jax.shard_map(
        on_device,
        mesh=split,
        in_specs=(
            P("lat", "ch", lon),
            P("ch"),
            P("ch", None),
            P("ch", None),
            P(),
            P(),
            P(None, "ch"),
            P("ch", None),
        ),
        out_specs=P("lat", "ch", lon),
        check_vma=False,
    )
```

time: 515 us -> 326 us (0.63)
  waiting for transfers between devices: 270 us -> 91.9 us
  matrix products: 60.1 us -> 25.3 us
  blocking collectives: 72 us -> 99.8 us
  local copies, waits for them, and re-layouts: 46 us -> 63.1 us
  other arithmetic: 23.5 us -> 6.93 us
    reduce_scatter x1 -> x0, waiting for transfers between devices: 91.3 us -> none  [on_device(): lax.psum_scatter(partial_terms.astype(jnp.bfloat16), 'ch', scatter_dimens...]
    all_gather x1 -> x2, waiting for transfers between devices: 97.9 us -> 54.1 us  [the longest x1 54.1 us: on_device(): weights = lax.all_gather(weights, 'lat')]
    all_gather x0 -> x2, blocking collectives: none -> 43.6 us  [the longest x1 28.2 us: on_device(): sums = lax.all_gather(sums, ('zh', 'co', 'ch'))]
    all_to_all x3, waiting for transfers between devices: 80.4 us -> 37.8 us  [the longest x1 26.2 us: on_device(): lax.all_to_all(first, ('zh', 'co', 'ch'), split_axis=0, concat_axis=0, ti...]
    unnamed x8 -> x0, matrix products: 29.8 us -> none
    reshape x2 -> x9, local copies, waits for them, and re-layouts: 0.37 us -> 21.9 us  [the longest x2 5.17 us: on_device(): back.reshape(2, lat_n, ch_n, co_n, trip, modes, BS)]
    psum x1 -> x0, blocking collectives: 15.4 us -> none  [on_device(): lax.psum((jnp.sum(values, axis=1), jnp.sum(values * values, axis=1)), 'ch')]
    convert_element_type x5 -> x8, local copies, waits for them, and re-layouts: 21 us -> 10.5 us  [the longest x1 3.26 us: on_device(): spec = spec.astype(BF16).reshape(dests, 2 * KW // dests, half * BS)]
  transfers between devices with their start and end apart: 5 -> 5, of which waited for: 5 -> 3; matrix products, arithmetic and copies ran while one was open for 1% -> 18% of each run, Pallas kernels for 0% -> 0%
where the time goes in v1:
time: 326 us; the launch traced here: 320 us
  blocking collectives  99.8 us (31%)
  waiting for transfers between devices  91.9 us (28%)
  local copies, waits for them, and re-layouts  63.1 us (19%)
  matrix products  25.3 us (8%)
  starting transfers between devices  19.4 us (6%)
  between operations  13.8 us (4%)
  other arithmetic  6.93 us (2%)
    all_gather x1, waiting for transfers between devices, on_device(): weights = lax.all_gather(weights, 'lat')  54.1 us
    all_to_all x1, blocking collectives, on_device(): lax.all_to_all(result, 'ch', split_axis=0, concat_axis=0, tiled=True)  33.1 us
    all_gather x1, blocking collectives, on_device(): sums = lax.all_gather(sums, ('zh', 'co', 'ch'))  28.2 us
    all_to_all x1, waiting for transfers between devices, on_device(): lax.all_to_all(first, ('zh', 'co', 'ch'), split_axis=0, concat_axis=0, ti...  26.2 us
    all_to_all x1, blocking collectives, on_device(): lax.all_to_all(back, ('lat', 'co'), split_axis=0, concat_axis=0, tiled=True)  23.1 us
    all_gather x1, blocking collectives, on_device(): weights = lax.all_gather(weights, 'ch')  15.4 us
    dot_general x1, matrix products, on_device(): jnp.einsum('gcf,gfrw->rcw', weights[1], hidden, preferred_element_type=F32)  14.4 us
    all_to_all x1, waiting for transfers between devices, on_device(): lax.all_to_all(spec, ('lat', 'co'), split_axis=0, concat_axis=0, tiled=True)  11.6 us
  transfers between devices with their start and end apart: 5, of which 3 were waited for; matrix products, arithmetic and copies ran while one was open for 18% of the time, Pallas kernels for 0%

profile of v1, /device:TPU:96, one launch (start us, length us, event | category | flops | bytes accessed | tf_op | source)
XLA Modules:
  0.0 320.2 jit_solution(9067917880620035343)
XLA Ops:
  6.5 1.4 constant_dynamic-slice_fusion
  7.9 0.1 copy.174
  8.0 0.1 copy.173
  8.2 15.4 %all-gather.1 = bf16[8,24,768]{2,1,0:T(8,128)(2,1)} all-gather(bf16[2,24,768]{2,1,0:T(8,128)(2,1)S(1)} %pad_maximum_fusion), channel_id=3, replica_groups=mesh['lat'=16,'zh'=2,'co'=2,'ch'=4] {'ch'}, dimensions={0}, use_global_device_ids=true | all-gather | bytes 368640 | tf_op jit(solution)/shard_map/all_gather | solution.py:77
  23.6 1.1 copy.141
  24.7 5.1 %all-to-all-start = ((bf16[4,12,96,128]{3,2,1,0:T(8,128)(2,1)}), bf16[4,12,96,128]{3,2,1,0:T(8,128)(2,1)S(1)}, u32[]{:S(2)}, u32[]{:S(2)}) async-start(bf16[4,12,96,128]{3,2,1,0:T(8,128)(2,1)} %bitcast.2), calls=%async_computation | async-start | bytes 2359296 | tf_op jit(solution)/shard_map/all_to_all | solution.py:92
  29.8 54.1 %all-gather.7.cloned.1.call-done = bf16[64,2,24,768]{3,2,1,0:T(8,128)(2,1)} async-done(((bf16[4,2,24,768]{3,2,1,0:T(8,128)(2,1)}), bf16[64,2,24,768]{3,2,1,0:T(8,128)(2,1)}) %all-gather.7.cloned.1.call-update) | async-done | bytes 4718608 | tf_op jit(solution)/shard_map/all_gather | solution.py:78
  84.0 0.3 convert_reduce_fusion
  84.3 28.2 %all-gather = f32[32,24,128]{2,1,0:T(8,128)S(1)} all-gather(f32[2,24,128]{2,1,0:T(8,128)S(1)} %pad_maximum_fusion.1), channel_id=2, replica_groups=mesh['lat'=16,'zh'=2,'co'=2,'ch'=4] {'zh','co','ch'}, dimensions={0}, use_global_device_ids=true | all-gather | bytes 417792 | tf_op jit(solution)/shard_map/all_gather | solution.py:83
  112.5 0.1 copy.142
  112.6 0.3 reduce_sum.47
  113.2 0.1 dynamic_slice.21
  113.2 0.4 copy-done.7
  113.7 1.8 fusion.24
  115.6 3.3 %copy.149 = bf16[512,12,96]{2,1,0:T(8,128)(2,1)S(1)} copy(bf16[512,12,96]{0,2,1:T(8,128)(2,1)} %fusion.24) | data formatting | bytes 2359296 | tf_op jit(solution)/shard_map/convert_element_type | solution.py:103
  118.9 2.7 reshape.123
  121.6 6.0 %all-to-all-start.1 = ((bf16[32,16,1152]{2,1,0:T(8,128)(2,1)}), bf16[32,16,1152]{2,1,0:T(8,128)(2,1)}, u32[]{:S(2)}, u32[]{:S(2)}) async-start(bf16[32,16,1152]{2,1,0:T(8,128)(2,1)} %reshape.123), calls=%async_computation.1 | async-start | bytes 2359296 | tf_op jit(solution)/shard_map/all_to_all | solution.py:104
  127.6 0.6 convert_reduce_fusion.3
  128.3 0.7 reshape.136
  129.0 0.7 reshape.135
  129.7 0.7 reshape.140
  130.4 0.7 reshape.139
  131.0 0.7 reshape.132
  131.7 0.7 reshape.133
  132.4 0.4 convolution_convert_fusion.3
  133.0 0.7 copy-done.1
  133.8 1.0 maximum_maximum_fusion
  134.8 11.6 %all-to-all-done.1 = bf16[32,16,1152]{2,1,0:T(8,128)(2,1)} async-done(((bf16[32,16,1152]{2,1,0:T(8,128)(2,1)}), bf16[32,16,1152]{2,1,0:T(8,128)(2,1)}, u32[]{:S(2)}, u32[]{:S(2)}) %all-to-all-start.1) | async-done | bytes 1179680 | tf_op jit(solution)/shard_map/all_to_all | solution.py:104
  146.4 5.1 %reshape.124 = bf16[16,2,2,8,4,3,96]{6,5,4,3,2,1,0:T(4,128)(2,1)S(1)} reshape(bf16[32,16,1152]{2,1,0:T(8,128)(2,1)} %all-to-all-done.1) | data formatting | bytes 2359296 | tf_op jit(solution)/shard_map/reshape | solution.py:107
  151.6 1.8 copy.150
  153.4 2.9 reshape_reshape.6
  156.3 0.6 copy.151
  157.0 2.3 fusion.23
  159.3 0.1 copy.152
  159.4 1.2 copy.153
  160.6 2.8 select_convert_fusion
  163.5 3.1 reshape.125
  166.6 0.2 copy.186
  166.8 1.9 reshape.126
  168.7 2.7 convolution_convert_fusion.1
  171.3 2.6 reshape.127
  173.9 2.5 copy.185
  176.5 2.6 reshape.128
  179.1 23.1 %all_to_all.25 = bf16[32,16,1152]{2,1,0:T(8,128)(2,1)S(1)} all-to-all(bf16[32,16,1152]{2,1,0:T(8,128)(2,1)} %reshape.128), channel_id=1, replica_groups=mesh['lat'=16,'zh'=2,'co'=2,'ch'=4] {'lat','co'}, dimensions={0} | all-to-all | bytes 2359296 | tf_op jit(solution)/shard_map/all_to_all | solution.py:124
  202.2 0.8 fusion.10
  203.0 1.9 reshape.141
  204.9 3.4 %fusion.15 = bf16[4,12,96,128]{3,2,1,0:T(8,128)(2,1)} fusion(bf16[4,12,96,128]{3,2,1,0:T(8,128)(2,1)S(1)} %all-to-all-done, f32[12,96,4,128]{3,2,1,0:T(4,128)} %reshape.141, f32[96]{0:T(128)S(1)} %dynamic_slice.21, f32[4,12,128]{2,1,0:T(8,128)} %copy-done.8, f32[4,12,128]{2,1,0:T(8,128)} %copy-done.7), kind=kLoop, calls=%fused_computation.21 | loop fusion | flops 5308416 | bytes 4768128 | tf_op jit(solution)/shard_map/convert_element_type | solution.py:129
  208.3 8.3 %all-to-all-start.3 = ((bf16[16,3,96,128]{3,2,1,0:T(8,128)(2,1)}), bf16[16,3,96,128]{3,2,1,0:T(8,128)(2,1)S(1)}, u32[]{:S(2)}, u32[]{:S(2)}) async-start(bf16[16,3,96,128]{3,2,1,0:T(8,128)(2,1)} %bitcast.28), calls=%async_computation.3 | async-start | bytes 2359296 | tf_op jit(solution)/shard_map/all_to_all | solution.py:132
  216.6 0.1 mul.92
  216.6 26.2 %all-to-all-done.3 = bf16[16,3,96,128]{3,2,1,0:T(8,128)(2,1)S(1)} async-done(((bf16[16,3,96,128]{3,2,1,0:T(8,128)(2,1)}), bf16[16,3,96,128]{3,2,1,0:T(8,128)(2,1)S(1)}, u32[]{:S(2)}, u32[]{:S(2)}) %all-to-all-start.3) | async-done | bytes 1179680 | tf_op jit(solution)/shard_map/all_to_all | solution.py:132
  242.8 0.2 fusion.18
  243.0 0.3 multiply_reduce_fusion
  243.3 0.4 multiply_convert_fusion
  243.7 0.1 copy.162
  243.9 0.3 convert_bitcast_fusion
  244.1 0.2 copy.157
  244.4 2.0 copy.164
  246.3 8.3 %copy.184 = bf16[2,16,4,2,24,768]{5,4,1,0,2,3:T(8,128)(2,1)} copy(bf16[2,16,4,2,24,768]{5,4,3,2,1,0:T(8,128)(2,1)} %bitcast.124) | data formatting | bytes 18874368 | tf_op jit(solution)/shard_map/all_gather | solution.py:79
  254.6 8.4 %fusion.57 = (bf16[1,4,2,16,24,768]{5,4,3,2,1,0:T(8,128)(2,1)}, bf16[1,4,2,16,24,768]{5,4,3,2,1,0:T(8,128)(2,1)}) fusion(bf16[2,4,2,16,24,768]{5,4,3,2,1,0:T(8,128)(2,1)} %bitcast.121), kind=kLoop, calls=%fused_computation.85 | loop fusion | bytes 18874368 | tf_op jit(solution)/shard_map/slice | solution.py:142
  263.0 14.4 %fusion.17 = bf16[6,768,128]{1,2,0:T(8,128)(2,1)} fusion(f32[6,768,128]{1,2,0:T(8,128)S(1)} %copy-done.2, bf16[4,768,768,1]{2,1,3,0:T(8,128)(2,1)} %bitcast.137, bf16[4,768,768,1]{2,1,3,0:T(8,128)(2,1)} %bitcast.136, bf16[6,768,128,1]{2,1,0,3:T(8,128)(2,1)S(1)} %bitcast.139), kind=kOutput, calls=%fused_computation.24 | convolution fusion | flops 7270170624 | bytes 14155776 | tf_op jit(solution)/shard_map/gcf,gfrw->rcw/dot_general | solution.py:144
  277.4 1.7 copy.165
  279.1 0.1 copy.166
  279.2 33.1 %all_to_all.26 = bf16[4,6,192,128]{3,2,1,0:T(8,128)(2,1)S(1)} all-to-all(bf16[4,6,192,128]{3,2,1,0:T(8,128)(2,1)S(1)} %copy.166), channel_id=1, replica_groups=mesh['lat'=16,'zh'=2,'co'=2,'ch'=4] {'ch'}, dimensions={0} | all-to-all | bytes 2359296 | tf_op jit(solution)/shard_map/all_to_all | solution.py:147
  312.4 1.0 copy.189
  (48 shorter events, 0.5 us)
Async XLA Ops:
  6.5 17.0 %copy-start = (bf16[24,192,128]{2,1,0:T(8,128)(2,1)S(1)}, bf16[24,192,128]{2,1,0:T(8,128)(2,1)}, u32[]{:S(2)}) copy-start(bf16[24,192,128]{2,1,0:T(8,128)(2,1)} %param.11) | copy-start | bytes 3538948
  6.5 77.4 %all-gather.7.cloned.1.call-start = ((), (), s32[]{:S(2)}) async-start(), calls=%async_computation.5 | async-start | bytes 5013504 | tf_op jit(solution)/shard_map/all_gather | solution.py:78
  24.7 88.5 %all-to-all-start = ((bf16[4,12,96,128]{3,2,1,0:T(8,128)(2,1)}), bf16[4,12,96,128]{3,2,1,0:T(8,128)(2,1)S(1)}, u32[]{:S(2)}, u32[]{:S(2)}) async-start(bf16[4,12,96,128]{3,2,1,0:T(8,128)(2,1)} %bitcast.2), calls=%async_computation | async-start | bytes 2359296 | tf_op jit(solution)/shard_map/all_to_all | solution.py:92
  29.8 216.5 %all-gather.9.cloned.1.call-start = ((), (), s32[]{:S(2)}) async-start(), calls=%async_computation.6 | async-start | bytes 14155776 | tf_op jit(solution)/shard_map/all_gather | solution.py:79
  83.9 29.2 %copy-start.13 = (f32[192]{0:T(256)S(1)}, f32[192]{0:T(256)}, u32[]{:S(2)}) copy-start(f32[192]{0:T(256)} %param.12) | copy-start | bytes 2308
  83.9 29.8 %copy-start.14 = (bf16[512,4,128,1]{2,0,3,1:T(8,128)(2,1)S(1)}, bf16[512,4,128,1]{2,0,3,1:T(8,128)(2,1)}, u32[]{:S(2)}) copy-start(bf16[512,4,128,1]{2,0,3,1:T(8,128)(2,1)} %constant.76) | copy-start | bytes 1572868
  113.1 0.6 copy-start.7
  113.1 0.6 copy-start.8
  118.9 8.8 %copy-start.9 = (f32[2,18432]{1,0:T(2,128)S(1)}, f32[2,18432]{1,0:T(2,128)}, u32[]{:S(2)}) copy-start(f32[2,18432]{1,0:T(2,128)} %param.14) | copy-start | bytes 442372
  118.9 13.6 %copy-start.12 = (s32[288]{0:T(512)S(1)}, s32[288]{0:T(512)}, u32[]{:S(2)}) copy-start(s32[288]{0:T(512)} %param.15) | copy-start | bytes 3460
  121.6 6.0 %copy-start.10 = (f32[2,18432]{1,0:T(2,128)S(1)}, f32[2,18432]{1,0:T(2,128)}, u32[]{:S(2)}) copy-start(f32[2,18432]{1,0:T(2,128)} %param.13) | copy-start | bytes 442372
  121.6 10.8 %copy-start.5 = (bf16[384,768]{1,0:T(8,128)(2,1)S(1)}, bf16[384,768]{1,0:T(8,128)(2,1)}, u32[]{:S(2)}) copy-start(bf16[384,768]{1,0:T(8,128)(2,1)} %constant.71.clone) | copy-start | bytes 1769476
  121.6 24.8 %all-to-all-start.1 = ((bf16[32,16,1152]{2,1,0:T(8,128)(2,1)}), bf16[32,16,1152]{2,1,0:T(8,128)(2,1)}, u32[]{:S(2)}, u32[]{:S(2)}) async-start(bf16[32,16,1152]{2,1,0:T(8,128)(2,1)} %reshape.123), calls=%async_computation.1 | async-start | bytes 2359296 | tf_op jit(solution)/shard_map/all_to_all | solution.py:104
  132.9 0.8 copy-start.1
  132.9 0.8 copy-start.3
  132.9 0.9 copy-start.4
  179.1 23.1 %copy-start.6 = (bf16[512,512]{1,0:T(8,128)(2,1)S(1)}, bf16[512,512]{1,0:T(8,128)(2,1)}, u32[]{:S(2)}) copy-start(bf16[512,512]{1,0:T(8,128)(2,1)} %constant.70.clone) | copy-start | bytes 1572868
  208.3 8.3 %copy-start.11 = (f32[768]{0:T(1024)S(1)}, f32[768]{0:T(1024)}, u32[]{:S(2)}) copy-start(f32[768]{0:T(1024)} %param.16) | copy-start | bytes 9220
  208.3 34.5 %all-to-all-start.3 = ((bf16[16,3,96,128]{3,2,1,0:T(8,128)(2,1)}), bf16[16,3,96,128]{3,2,1,0:T(8,128)(2,1)S(1)}, u32[]{:S(2)}, u32[]{:S(2)}) async-start(bf16[16,3,96,128]{3,2,1,0:T(8,128)(2,1)} %bitcast.28), calls=%async_computation.3 | async-start | bytes 2359296 | tf_op jit(solution)/shard_map/all_to_all | solution.py:132
  254.6 8.4 %copy-start.2 = (f32[6,768,128]{1,2,0:T(8,128)S(1)}, f32[6,768,128]{1,2,0:T(8,128)}, u32[]{:S(2)}) copy-start(f32[6,768,128]{1,2,0:T(8,128)} %copy.164) | copy-start | bytes 7077892
Sparse Core Ops, SparseCore 0:
  23.7 60.1 all-gather.6
  85.7 26.9 all-gather.8

commit v2 on v1

v2 whole, which is shorter than its diff:
```python
import functools
import math

import jax
import jax.numpy as jnp
import numpy as np
from jax import lax
from jax.experimental import pallas as pl
from jax.experimental.pallas import tpu as pltpu
from jax.sharding import Mesh, PartitionSpec as P

BS = 96
KW = 256
LANES = 128
SHRINK = 0.01
EPSILON = 1e-05
BF16 = jnp.bfloat16
F32 = jnp.float32
VMEM_LIMIT = 40 * 1024 * 1024


def dot(left, right, dims=((1,), (0,))):
    return lax.dot_general(left, right, (dims, ((), ())), preferred_element_type=F32)


def whole(shape):
    return pl.BlockSpec(shape, lambda *_: (0,) * len(shape))


def call(kernel, scalars, args, outs, scratch, flops):
    moved = sum(a.size * a.dtype.itemsize for a in (*args, *outs))
    return pl.pallas_call(
        kernel,
        grid_spec=pltpu.PrefetchScalarGridSpec(
            num_scalar_prefetch=1,
            grid=(1,),
            in_specs=[whole(a.shape) for a in args],
            out_specs=[whole(o.shape) for o in outs],
            scratch_shapes=scratch,
        ),
        out_shape=outs,
        compiler_params=pltpu.CompilerParams(vmem_limit_bytes=VMEM_LIMIT),
        cost_estimate=pl.CostEstimate(flops=flops, bytes_accessed=moved, transcendentals=0),
    )(scalars, *args)


def lon_tables(width, dests):
    k = np.arange(KW)
    angle = 2.0 * np.pi * (k[:, None] * np.arange(width)[None, :] % width) / width
    both = np.stack([np.cos(angle), -np.sin(angle)]) / math.sqrt(width)
    forward = both.reshape(2, dests, KW // dests, width).transpose(1, 0, 2, 3)
    weights = np.where(k == 0, 1.0, 2.0)
    inverse = (both * weights[None, :, None]).reshape(2, dests, KW // dests, width)
    inverse = inverse.transpose(1, 0, 2, 3)
    return forward.reshape(2 * KW, width), inverse.reshape(2 * KW, width)


def lat_table(kept_lat, height, order):
    h = np.arange(height)
    angle = 2.0 * np.pi * (h[:, None] * h[order][None, :] % height) / height
    cosine, sine = np.cos(angle) / math.sqrt(height), np.sin(angle) / math.sqrt(height)
    table = np.concatenate([cosine, sine, -sine, cosine], axis=1)
    pick = (kept_lat[:, None] == jnp.arange(height)[None, :]).astype(BF16)
    kept = dot(pick, jnp.asarray(table, BF16)).astype(BF16)
    return jnp.concatenate([kept[:, : 2 * height], kept[:, 2 * height :]], axis=0)


def mode_weight(flat):
    weight = flat.reshape(2, BS, BS)
    weight = jnp.pad(weight, ((0, 0), (0, LANES - BS), (0, LANES - BS)))
    return jnp.concatenate(
        [
            jnp.concatenate([weight[0], weight[1]], axis=1),
            jnp.concatenate([-weight[1], weight[0]], axis=1),
        ],
        axis=0,
    ).astype(BF16)


def forward_kernel(full, at, own, near, far, across, stats, gain, table, spec, base, normed):
    core, lon = at[0], at[2]
    parts = (
        lambda c, t: own[c, core, t, at[1]],
        lambda c, t: near[c, t],
        lambda c, t: far[c, core, t],
        lambda c, t: across[c, t],
    )
    groups, trip = near.shape[0], near.shape[1]
    for d, part in enumerate(parts):
        lanes = pl.ds(pl.multiple_of((lon ^ d) * LANES, LANES), LANES)
        mean = stats[d, 0] / full
        scale = lax.rsqrt(stats[d, 1] / full - mean * mean + EPSILON)
        for c in range(groups):
            for t in range(trip):
                r = c * trip + t
                values = part(c, t).astype(F32)
                value = (values - mean[r : r + 1]) * scale[r : r + 1] * gain[...]
                value = value.astype(BF16)
                rows = slice(r * BS, (r + 1) * BS)
                normed[rows, lanes] = value
                base[rows, lanes] = values + value.astype(F32)
    result = dot(table[...], normed[...], ((1,), (1,)))
    spec[...] = result.astype(BF16).reshape(spec.shape)


def middle_kernel(at, columns, left, right, first_w, second_w, out, wide, stacked, mid):
    srcs, pairs, inner = columns.shape
    modes = pairs // 2
    local = inner // BS
    height = srcs * local
    kept = left.shape[0] // 2
    tiles = inner // LANES
    for j in range(tiles):
        part = columns[:, :, j * LANES : (j + 1) * LANES]
        wide[j] = part.reshape(srcs * pairs, LANES).astype(F32)
    blank = jnp.zeros((srcs, LANES), F32)
    for t in range(2):
        for k in range(modes):
            take = pl.ds(t * modes + k, srcs, stride=pairs)
            one = jnp.concatenate([wide[j, take, :] for j in range(tiles)] + [blank], axis=1)
            for r in range(local):
                rows = slice(t * height + r * srcs, t * height + (r + 1) * srcs)
                stacked[rows, k * LANES : (k + 1) * LANES] = one[
                    :, r * BS : r * BS + LANES
                ].astype(BF16)
    moved = dot(left[...], stacked[...]).astype(BF16)
    for k in range(modes):
        lanes = slice(k * LANES, (k + 1) * LANES)
        both = jnp.concatenate([moved[:kept, lanes], moved[kept:, lanes]], axis=1)
        both = jnp.maximum(dot(both, first_w[...]), 0.0).astype(BF16)
        both = dot(both, second_w[...])
        both = jnp.where(
            both > SHRINK, both - SHRINK, jnp.where(both < -SHRINK, both + SHRINK, 0.0)
        ).astype(BF16)
        mid[:kept, lanes] = both[:, :LANES]
        mid[kept:, lanes] = both[:, LANES:]
    back = dot(right[...], mid[...])
    for t in range(2):
        for k in range(modes):
            lanes = slice(k * LANES, k * LANES + BS)
            one = jnp.concatenate(
                [
                    back[t * height + r * srcs : t * height + (r + 1) * srcs, lanes]
                    for r in range(local)
                ],
                axis=1,
            )
            for j in range(tiles):
                put = pl.ds(t * modes + k, srcs, stride=pairs)
                wide[j, put, :] = one[:, j * LANES : (j + 1) * LANES]
    for j in range(tiles):
        part = wide[j].astype(BF16).reshape(srcs, pairs, LANES)
        out[:, :, j * LANES : (j + 1) * LANES] = part


def inverse_kernel(at, returned, table, base, *refs):
    outs, first = refs[:-1], refs[-1]
    field = dot(returned[...], table[...], ((0,), (0,))).astype(BF16).astype(F32)
    first[...] = (base[...] + field).astype(BF16)
    count = len(outs)
    cores, trip = outs[0].shape[0], outs[0].shape[1]
    groups = first.shape[0] // (trip * BS)
    for d, out in enumerate(outs):
        place = lax.rem(at[0] + d, count)
        high, low = place // groups, lax.rem(place, groups)
        rows = pl.ds(pl.multiple_of(low * (trip * BS), trip * BS), trip * BS)
        for c in range(cores):
            lanes = pl.ds(pl.multiple_of((high * cores + c) * LANES, LANES), LANES)
            out[c] = first[rows, lanes].reshape(trip, BS, LANES)


def token_kernel(at, *refs):
    mine, theirs, gain, up, down = refs[:8], refs[8], refs[9], refs[10], refs[11]
    outs, (first, ready, total) = refs[12:16], refs[16:]
    step = pl.program_id(0)
    core = at[1]
    trip = theirs.shape[1]
    groups = len(outs)
    count = len(mine)

    @pl.when(step == 0)
    def _():
        for d, ref in enumerate(mine):
            place = lax.rem(at[0] - d + count, count)
            row = (lax.rem(place, groups) * (count // groups) + place // groups) * BS
            rows = pl.ds(pl.multiple_of(row, BS), BS)
            for t in range(trip):
                own = pl.ds(pl.multiple_of((core * trip + t) * LANES, LANES), LANES)
                first[rows, own] = ref[core, t]
                other = pl.ds(pl.multiple_of(((1 - core) * trip + t) * LANES, LANES), LANES)
                first[rows, other] = theirs[d, t]
        values = first[...].astype(F32)
        mean = jnp.mean(values, axis=0, keepdims=True)
        values = values - mean
        spread = jnp.mean(values * values, axis=0, keepdims=True)
        ready[...] = (values * lax.rsqrt(spread + EPSILON) * gain[...]).astype(BF16)
        total[...] = first[...].astype(F32)

    side = first.shape[0]
    hidden = dot(up[...].reshape(-1, side), ready[...])
    hidden = jax.nn.gelu(hidden).astype(BF16)
    total[...] += dot(down[...].reshape(side, -1), hidden)

    @pl.when(step == pl.num_programs(0) - 1)
    def _():
        chans = outs[0].shape[1]
        for d, out in enumerate(outs):
            low = lax.rem(lax.rem(at[0], groups) + d, groups)
            rows = pl.ds(pl.multiple_of(low * chans, chans), chans)
            for r in range(out.shape[0]):
                out[r] = total[rows, r * LANES : (r + 1) * LANES].astype(BF16)


def on_device(tokens, gain_first, mode_first, mode_second, kept_lat, gain_second, w_up, w_down):
    rows, chans, cols = tokens.shape
    lat_n, zh_n, co_n, ch_n = (lax.axis_size(a) for a in ("lat", "zh", "co", "ch"))
    lon_n, z_n = zh_n * co_n, zh_n * ch_n
    width = cols * lon_n
    height = rows * lat_n
    full = chans * ch_n
    dests = lat_n * co_n
    half = rows // co_n
    trip = half // ch_n
    lat, zh, co, ch = (lax.axis_index(a) for a in ("lat", "zh", "co", "ch"))
    lon = zh * co_n + co
    z = zh * ch_n + ch
    swap = [(0, 1), (1, 0)]

    def ring(array, axes, count, step):
        return lax.ppermute(array, axes, [(i, (i + step) % count) for i in range(count)])

    values = tokens.astype(F32)
    sums = jnp.stack([jnp.sum(values, axis=1), jnp.sum(values * values, axis=1)])
    sums = sums + sum(ring(sums, "ch", ch_n, d) for d in range(1, ch_n))
    shared = [sums] + [
        lax.ppermute(sums, ("zh", "co"), [(i, i ^ d) for i in range(lon_n)])
        for d in range(1, lon_n)
    ]
    stats = jnp.stack(shared).reshape(lon_n, 2, ch_n, co_n, trip, cols)
    stats = lax.dynamic_index_in_dim(stats, co, axis=3, keepdims=False)
    stats = stats.reshape(lon_n, 2, half, cols)

    own = tokens.reshape(ch_n, co_n, trip, zh_n, BS, cols)
    far = lax.ppermute(
        lax.dynamic_index_in_dim(own, 1 - zh, axis=3, keepdims=False), "zh", swap
    )
    near = lax.dynamic_index_in_dim(own, zh, axis=3, keepdims=False)
    near = lax.dynamic_index_in_dim(near, 1 - co, axis=1, keepdims=False)
    near = lax.ppermute(near, "co", swap)
    across = lax.dynamic_index_in_dim(far, 1 - co, axis=1, keepdims=False)
    across = lax.ppermute(across, "co", swap)

    picked = jnp.where(co == 0, w_up, w_down).T
    piece_n = picked.shape[0] // lat_n
    piece = lax.dynamic_slice_in_dim(picked, lat * piece_n, piece_n, axis=0)
    pieces = jnp.stack([piece] + [ring(piece, "ch", ch_n, d) for d in range(1, ch_n)])
    weights = lax.all_gather(pieces, ("lat", "co"))
    weights = weights.reshape(lat_n, co_n, ch_n, piece_n, full)

    forward, inverse = lon_tables(width, dests)
    gain = lax.dynamic_slice_in_dim(gain_first, zh * BS, BS)
    gain = jnp.broadcast_to(gain[:, None], (BS, cols))
    at = jnp.stack([co, zh, lon]).astype(jnp.int32)
    wide_n = half * BS
    spec, base = call(
        functools.partial(forward_kernel, float(full)),
        at,
        (own, near, far, across, stats, gain, jnp.asarray(forward, BF16)),
        (
            jax.ShapeDtypeStruct((dests, 2 * KW // dests, wide_n), BF16),
            jax.ShapeDtypeStruct((wide_n, width), F32),
        ),
        [pltpu.VMEM((wide_n, width), BF16)],
        4 * KW * width * wide_n,
    )
    columns = lax.all_to_all(spec, ("lat", "co"), split_axis=0, concat_axis=0, tiled=True)

    modes = KW // dests
    order = np.arange(height).reshape(lat_n, ch_n, co_n, trip).transpose(1, 3, 0, 2).reshape(-1)
    left = lat_table(kept_lat, height, order)
    kept = kept_lat.shape[0]
    first_w = mode_weight(lax.dynamic_index_in_dim(mode_first, zh, axis=0, keepdims=False))
    second_w = mode_weight(lax.dynamic_index_in_dim(mode_second, zh, axis=0, keepdims=False))
    (back,) = call(
        middle_kernel,
        at,
        (columns, left, left.T, first_w, second_w),
        (jax.ShapeDtypeStruct(columns.shape, BF16),),
        [
            pltpu.VMEM((wide_n // LANES, dests * 2 * modes, LANES), F32),
            pltpu.VMEM((2 * height, modes * LANES), BF16),
            pltpu.VMEM((2 * kept, modes * LANES), BF16),
        ],
        16 * height * kept * modes * LANES,
    )
    returned = lax.all_to_all(back, ("lat", "co"), split_axis=0, concat_axis=0, tiled=True)

    at = jnp.stack([z, co]).astype(jnp.int32)
    firsts = call(
        inverse_kernel,
        at,
        (returned.reshape(2 * KW, wide_n), jnp.asarray(inverse, BF16), base),
        tuple(jax.ShapeDtypeStruct((co_n, trip, BS, cols), BF16) for _ in range(z_n)),
        [pltpu.VMEM((wide_n, width), BF16)],
        4 * KW * width * wide_n,
    )
    mine = [firsts[0]] + [ring(firsts[d], ("zh", "ch"), z_n, d) for d in range(1, z_n)]
    theirs = jnp.stack(
        [lax.dynamic_index_in_dim(m, 1 - co, axis=0, keepdims=False) for m in mine]
    )
    theirs = lax.ppermute(theirs, "co", swap)

    tokens_n = co_n * trip * cols
    gain = jnp.broadcast_to(gain_second[:, None], (full, tokens_n))
    once = [whole(m.shape) for m in mine] + [whole(theirs.shape), whole(gain.shape)]
    weight_block = (lat_n, None, None, piece_n, full)
    results = pl.pallas_call(
        token_kernel,
        grid_spec=pltpu.PrefetchScalarGridSpec(
            num_scalar_prefetch=1,
            grid=(ch_n,),
            in_specs=once
            + [
                pl.BlockSpec(weight_block, lambda i, at: (0, 0, i, 0, 0)),
                pl.BlockSpec(weight_block, lambda i, at: (0, 1, i, 0, 0)),
            ],
            out_specs=[whole((co_n * trip, chans, cols))] * ch_n,
            scratch_shapes=[
                pltpu.VMEM((full, tokens_n), BF16),
                pltpu.VMEM((full, tokens_n), BF16),
                pltpu.VMEM((full, tokens_n), F32),
            ],
        ),
        out_shape=[jax.ShapeDtypeStruct((co_n * trip, chans, cols), BF16)] * ch_n,
        compiler_params=pltpu.CompilerParams(vmem_limit_bytes=VMEM_LIMIT),
        cost_estimate=pl.CostEstimate(
            flops=4 * full * full * ch_n * tokens_n,
            bytes_accessed=weights.size * 2,
            transcendentals=full * ch_n * tokens_n,
        ),
    )(at, *mine, theirs, gain, weights, weights)
    output = jnp.zeros((ch_n, co_n * trip, chans, cols), BF16)
    for d, piece in enumerate(results):
        piece = piece if d == 0 else ring(piece, "ch", ch_n, d)
        output = lax.dynamic_update_index_in_dim(output, piece, lax.rem(ch - d + ch_n, ch_n), 0)
    return output.reshape(rows, chans, cols)


def solution(mesh):
    grid = mesh.devices
    lat_n, lon_n, ch_n = grid.shape
    split = Mesh(grid.reshape(lat_n, 2, lon_n // 2, ch_n), ("lat", "zh", "co", "ch"))
    lon = ("zh", "co")
    return jax.shard_map(
        on_device,
        mesh=split,
        in_specs=(
            P("lat", "ch", lon),
            P("ch"),
            P("ch", None),
            P("ch", None),
            P(),
            P(),
            P(None, "ch"),
            P("ch", None),
        ),
        out_specs=P("lat", "ch", lon),
        check_vma=False,
    )
```

time: 326 us -> 225 us (0.69)
  blocking collectives: 99.8 us -> 0 us
  local copies, waits for them, and re-layouts: 63.1 us -> 28.5 us
  starting transfers between devices: 19.4 us -> 49.4 us
  matrix products: 25.3 us -> 2 us
  Pallas kernels: 0 us -> 20.4 us
  waiting for transfers between devices: 91.9 us -> 96.6 us
  other arithmetic: 6.93 us -> 10.5 us
    ppermute x0 -> x23, waiting for transfers between devices: none -> 73.4 us  [the longest x16 63.8 us: ring(): lax.ppermute(array, axes, [(i, (i + step) % count) for i in range(count)])]
    all_to_all x2 -> x0, blocking collectives: 56.2 us -> none  [the longest x1 33.1 us: on_device(): lax.all_to_all(result, 'ch', split_axis=0, concat_axis=0, tiled=True)]
    all_gather x2 -> x1, waiting for transfers between devices: 54.1 us -> 0.01 us  [on_device(): weights = lax.all_gather(pieces, ('lat', 'co'))]
    all_gather x2 -> x0, blocking collectives: 43.6 us -> none  [the longest x1 28.2 us: on_device(): sums = lax.all_gather(sums, ('zh', 'co', 'ch'))]
    ppermute x0 -> x23, starting transfers between devices: none -> 37.9 us  [the longest x16 26.2 us: ring(): lax.ppermute(array, axes, [(i, (i + step) % count) for i in range(count)])]
    reshape x9 -> x3, local copies, waits for them, and re-layouts: 21.9 us -> 1.47 us  [the longest x2 1.46 us: mode_weight(): weight = flat.reshape(2, BS, BS)]
    pallas_call x0 -> x4, Pallas kernels: none -> 20.4 us  [the longest x1 12 us: on_device(): pl.pallas_call(token_kernel, grid_spec=pltpu.PrefetchScalarGridSpec(num_s...]
    dot_general x2 -> x0, matrix products: 16.3 us -> none  [the longest x1 14.4 us: on_device(): jnp.einsum('gcf,gfrw->rcw', weights[1], hidden, preferred_element_type=F32)]
  transfers between devices with their start and end apart: 5 -> 26, of which waited for: 3 -> 15; matrix products, arithmetic and copies ran while one was open for 18% -> 10% of each run, Pallas kernels for 0% -> 4%
where the time goes in v2:
time: 225 us; the launch traced here: 221 us
  waiting for transfers between devices  96.6 us (43%)
  starting transfers between devices  49.4 us (22%)
  local copies, waits for them, and re-layouts  28.5 us (13%)
  Pallas kernels  20.4 us (9%)
  between operations  13.8 us (6%)
  other arithmetic  10.5 us (5%)
    ppermute x16, waiting for transfers between devices, ring(): lax.ppermute(array, axes, [(i, (i + step) % count) for i in range(count)])  63.8 us
    ppermute x16, starting transfers between devices, ring(): lax.ppermute(array, axes, [(i, (i + step) % count) for i in range(count)])  26.2 us
    all_to_all x1, waiting for transfers between devices, on_device(): lax.all_to_all(back, ('lat', 'co'), split_axis=0, concat_axis=0, tiled=True)  18.9 us
    unnamed x61, local copies, waits for them, and re-layouts  16.3 us
    pallas_call x1, Pallas kernels, on_device(): pl.pallas_call(token_kernel, grid_spec=pltpu.PrefetchScalarGridSpec(num_s...  12 us
    pallas_call x3, Pallas kernels, call(): pl.pallas_call(kernel, grid_spec=pltpu.PrefetchScalarGridSpec(num_scalar_...  8.43 us
    ppermute x1, waiting for transfers between devices, on_device(): lax.ppermute(lax.dynamic_index_in_dim(own, 1 - zh, axis=3, keepdims=False...  7.6 us
    all_to_all x1, starting transfers between devices, on_device(): lax.all_to_all(spec, ('lat', 'co'), split_axis=0, concat_axis=0, tiled=True)  7.55 us
  transfers between devices with their start and end apart: 26, of which 15 were waited for; matrix products, arithmetic and copies ran while one was open for 10% of the time, Pallas kernels for 4%

profile of v2, /device:TPU:96, one launch (start us, length us, event | category | flops | bytes accessed | tf_op | source)
XLA Modules:
  0.0 221.2 jit_solution(10602253864441703417)
XLA Ops:
  6.5 1.4 constant_dynamic-slice_fusion
  8.2 1.0 collective-permute-start.17
  10.3 3.0 %collective-permute-done.17 = bf16[48,768]{1,0:T(8,128)(2,1)S(1)} collective-permute-done((bf16[48,768]{1,0:T(8,128)(2,1)S(1)}, bf16[48,768]{1,0:T(8,128)(2,1)S(1)}, u32[]{:S(2)}, u32[]{:S(2)}) %collective-permute-start.17) | collective-permute-done | bytes 73760 | tf_op jit(solution)/shard_map/ppermute | solution.py:230
  13.3 3.6 %collective-permute-done.18 = bf16[48,768]{1,0:T(8,128)(2,1)S(1)} collective-permute-done((bf16[48,768]{1,0:T(8,128)(2,1)S(1)}, bf16[48,768]{1,0:T(8,128)(2,1)S(1)}, u32[]{:S(2)}, u32[]{:S(2)}) %collective-permute-start.18) | collective-permute-done | bytes 73760 | tf_op jit(solution)/shard_map/ppermute | solution.py:230
  16.9 0.8 pad_maximum_fusion.1
  17.7 0.9 dynamic-slice_bitcast_fusion
  18.6 5.4 %collective-permute-start.1 = (bf16[4,2,3,96,128]{4,3,2,1,0:T(8,128)(2,1)}, bf16[4,2,3,96,128]{4,3,2,1,0:T(8,128)(2,1)S(1)}, u32[]{:S(2)}, u32[]{:S(2)}) collective-permute-start(bf16[4,2,3,96,128]{4,3,2,1,0:T(8,128)(2,1)} %dynamic-slice_bitcast_fusion), channel_id=1, source_target_pairs={{0,8},{8,0},{1,9},{9,1},{2,10},{10,2},{3,11},{11,3},{4,12},{12,4},... | collective-permute-start | bytes 1769480 | tf_op jit(solution)/shard_map/ppermute | solution.py:244
  25.0 1.4 collective-permute-start.3
  26.8 2.0 collective-permute-start.5
  29.0 2.0 convolution_convert_fusion
  31.0 7.6 %collective-permute-done.1.far = bf16[4,2,3,96,128]{4,3,2,1,0:T(8,128)(2,1)S(1)} collective-permute-done((bf16[4,2,3,96,128]{4,3,2,1,0:T(8,128)(2,1)}, bf16[4,2,3,96,128]{4,3,2,1,0:T(8,128)(2,1)S(1)}, u32[]{:S(2)}, u32[]{:S(2)}) %collective-permute-start.1) | collective-permute-done | bytes 589856 | tf_op jit(solution)/shard_map/ppermute | solution.py:244
  38.8 12.0 %collective-permute-done.3 = f32[2,24,128]{2,0,1:T(2,128)} collective-permute-done((f32[2,24,128]{2,0,1:T(2,128)}, f32[2,24,128]{2,0,1:T(2,128)}, u32[]{:S(2)}, u32[]{:S(2)}) %collective-permute-start.3) | collective-permute-done | bytes 24608 | tf_op jit(solution)/shard_map/ppermute | solution.py:230
  50.8 1.0 collective-permute-done.4
  51.8 0.8 add_add_fusion
  52.8 5.7 %collective-permute-start.8 = (f32[2,24,128]{2,0,1:T(2,128)S(1)}, f32[2,24,128]{2,0,1:T(2,128)S(1)}, u32[]{:S(2)}, u32[]{:S(2)}) collective-permute-start(f32[2,24,128]{2,0,1:T(2,128)S(1)} %add_add_fusion), channel_id=1, source_target_pairs={{0,12},{4,8},{8,4},{12,0},{1,13},{5,9},{9,5},{13,1},{2,14},{6,10},... | collective-permute-start | bytes 73736 | tf_op jit(solution)/shard_map/ppermute | solution.py:236
  58.6 1.4 dynamic-slice_reduce_fusion
  60.0 0.7 reshape.40
  60.7 0.7 reshape.41
  62.3 0.7 copy-done.11
  63.1 1.1 copy-done.2
  64.2 1.1 copy-done.8
  65.3 1.0 copy-done.10
  66.2 1.0 copy-done.12
  67.2 2.2 shard_map.109
  69.4 1.0 copy-done.3
  70.4 7.6 %all-to-all-start = ((bf16[32,16,1152]{2,1,0:T(8,128)(2,1)}), bf16[32,16,1152]{2,1,0:T(8,128)(2,1)S(1)}, u32[]{:S(2)}, u32[]{:S(2)}) async-start(bf16[32,16,1152]{2,1,0:T(8,128)(2,1)} %copy-done.3), calls=%async_computation | async-start | bytes 2359296 | tf_op jit(solution)/shard_map/all_to_all | solution.py:276
  77.9 2.3 %fusion.17 = (bf16[288,768]{0,1:T(8,128)(2,1)S(1)}, bf16[288,768]{0,1:T(8,128)(2,1)}) fusion(bf16[288,1536]{0,1:T(8,128)(2,1)} %convolution_convert_fusion), kind=kLoop, calls=%fused_computation.59 | loop fusion | bytes 1769472 | tf_op jit(solution)/shard_map/slice | solution.py:65
  80.2 0.9 copy-done.17
  81.1 2.3 %pad_maximum_fusion = bf16[576,768]{0,1:T(8,128)(2,1)} fusion(bf16[288,768]{0,1:T(8,128)(2,1)} %get-tuple-element.36, bf16[288,768]{0,1:T(8,128)(2,1)S(1)} %get-tuple-element.35), kind=kLoop, calls=%fused_computation.4 | loop fusion | flops 1769472 | bytes 1769472 | tf_op jit(solution)/shard_map/concatenate | solution.py:65
  83.4 2.2 %copy.21.left = bf16[576,768]{1,0:T(8,128)(2,1)} copy(bf16[576,768]{0,1:T(8,128)(2,1)} %pad_maximum_fusion) | data formatting | bytes 1769472 | tf_op jit(solution)/shard_map/concatenate | solution.py:65
  85.7 0.9 fusion.11
  86.5 0.8 fusion.12
  87.3 0.8 fusion.10
  88.2 0.8 fusion.9
  90.4 2.3 %fusion.19.right = bf16[768,576]{1,0:T(8,128)(2,1)} fusion(bf16[288,768]{0,1:T(8,128)(2,1)} %get-tuple-element.36, bf16[288,768]{0,1:T(8,128)(2,1)S(1)} %copy-done.18), kind=kLoop, calls=%fused_computation.60 | loop fusion | flops 1769472 | bytes 1769472 | tf_op jit(solution)/shard_map/transpose | solution.py:287
  92.7 4.3 %all-to-all-done.columns = bf16[32,16,1152]{2,1,0:T(8,128)(2,1)S(1)} async-done(((bf16[32,16,1152]{2,1,0:T(8,128)(2,1)}), bf16[32,16,1152]{2,1,0:T(8,128)(2,1)S(1)}, u32[]{:S(2)}, u32[]{:S(2)}) %all-to-all-start) | async-done | bytes 1179680 | tf_op jit(solution)/shard_map/all_to_all | solution.py:276
  97.0 1.2 copy-done.5
  98.2 1.2 copy-done.6
  99.3 0.9 copy-done.13
  100.2 0.9 copy-done.14
  101.1 4.7 %shard_map.110 = bf16[32,16,1152]{2,1,0:T(8,128)(2,1)S(1)} custom-call(s32[3]{0:T(128)S(1)} %pad_add_fusion.1.at, bf16[32,16,1152]{2,1,0:T(8,128)(2,1)S(1)} %all-to-all-done.columns, bf16[576,768]{1,0:T(8,128)(2,1)S(1)} %copy-done.6, bf16[768,576]{1,0:T(8,128)(2,1)S(1)} %copy-done.5, bf16[256,256]{1,0:T(8,128)(2,1)S(1)} %copy-done.13, ...), custom_call_target="tpu_custom_call" | custom-call | flops 1811939328 | bytes 4390912 | tf_op jit(solution)/shard_map/pallas_call | solution.py:32
  105.9 1.0 copy-done.4
  106.9 3.9 %all-to-all-start.1 = ((bf16[32,16,1152]{2,1,0:T(8,128)(2,1)}), bf16[32,16,1152]{2,1,0:T(8,128)(2,1)S(1)}, u32[]{:S(2)}, u32[]{:S(2)}) async-start(bf16[32,16,1152]{2,1,0:T(8,128)(2,1)} %copy-done.4), calls=%async_computation.1 | async-start | bytes 2359296 | tf_op jit(solution)/shard_map/all_to_all | solution.py:296
  110.9 18.9 %all-to-all-done.1 = bf16[32,16,1152]{2,1,0:T(8,128)(2,1)S(1)} async-done(((bf16[32,16,1152]{2,1,0:T(8,128)(2,1)}), bf16[32,16,1152]{2,1,0:T(8,128)(2,1)S(1)}, u32[]{:S(2)}, u32[]{:S(2)}) %all-to-all-start.1) | async-done | bytes 1179680 | tf_op jit(solution)/shard_map/all_to_all | solution.py:296
  129.8 1.0 copy-done.7
  130.9 1.6 shard_map.111
  132.5 4.0 %collective-permute-start.9 = (bf16[2,3,96,128]{3,2,1,0:T(8,128)(2,1)S(1)}, bf16[2,3,96,128]{3,2,1,0:T(8,128)(2,1)S(1)}, u32[]{:S(2)}, u32[]{:S(2)}) collective-permute-start(bf16[2,3,96,128]{3,2,1,0:T(8,128)(2,1)S(1)} %get-tuple-element.22), channel_id=1, source_target_pairs={{0,1},{1,2},{2,3},{3,8},{8,9},{9,10},{10,11},{11,0},{4,5},{5,6},{6... | collective-permute-start | bytes 442376 | tf_op jit(solution)/shard_map/ppermute | solution.py:230
  136.5 1.2 collective-permute-start.10
  138.3 5.1 %collective-permute-start.11 = (bf16[2,3,96,128]{3,2,1,0:T(8,128)(2,1)S(1)}, bf16[2,3,96,128]{3,2,1,0:T(8,128)(2,1)S(1)}, u32[]{:S(2)}, u32[]{:S(2)}) collective-permute-start(bf16[2,3,96,128]{3,2,1,0:T(8,128)(2,1)S(1)} %get-tuple-element.24), channel_id=1, source_target_pairs={{0,3},{1,8},{2,9},{3,10},{8,11},{9,0},{10,1},{11,2},{4,7},{5,12},{... | collective-permute-start | bytes 442376 | tf_op jit(solution)/shard_map/ppermute | solution.py:230
  143.4 1.3 collective-permute-start.12
  144.7 2.0 collective-permute-start.13
  146.8 2.8 %collective-permute-start.14 = (bf16[2,3,96,128]{3,2,1,0:T(8,128)(2,1)S(1)}, bf16[2,3,96,128]{3,2,1,0:T(8,128)(2,1)S(1)}, u32[]{:S(2)}, u32[]{:S(2)}) collective-permute-start(bf16[2,3,96,128]{3,2,1,0:T(8,128)(2,1)S(1)} %get-tuple-element.27), channel_id=1, source_target_pairs={{0,10},{1,11},{2,0},{3,1},{8,2},{9,3},{10,8},{11,9},{4,14},{5,15},... | collective-permute-start | bytes 442376 | tf_op jit(solution)/shard_map/ppermute | solution.py:230
  149.6 5.6 %collective-permute-done.10.refs_2_ = bf16[2,3,96,128]{3,2,1,0:T(8,128)(2,1)S(1)} collective-permute-done((bf16[2,3,96,128]{3,2,1,0:T(8,128)(2,1)S(1)}, bf16[2,3,96,128]{3,2,1,0:T(8,128)(2,1)S(1)}, u32[]{:S(2)}, u32[]{:S(2)}) %collective-permute-start.10) | collective-permute-done | bytes 147488 | tf_op jit(solution)/shard_map/ppermute | solution.py:230
  155.4 7.9 %collective-permute-done.11.refs_3_ = bf16[2,3,96,128]{3,2,1,0:T(8,128)(2,1)S(1)} collective-permute-done((bf16[2,3,96,128]{3,2,1,0:T(8,128)(2,1)S(1)}, bf16[2,3,96,128]{3,2,1,0:T(8,128)(2,1)S(1)}, u32[]{:S(2)}, u32[]{:S(2)}) %collective-permute-start.11) | collective-permute-done | bytes 147488 | tf_op jit(solution)/shard_map/ppermute | solution.py:230
  163.3 1.9 collective-permute-done.13.refs_5_
  165.2 2.4 %collective-permute-done.14.refs_6_ = bf16[2,3,96,128]{3,2,1,0:T(8,128)(2,1)S(1)} collective-permute-done((bf16[2,3,96,128]{3,2,1,0:T(8,128)(2,1)S(1)}, bf16[2,3,96,128]{3,2,1,0:T(8,128)(2,1)S(1)}, u32[]{:S(2)}, u32[]{:S(2)}) %collective-permute-start.14) | collective-permute-done | bytes 147488 | tf_op jit(solution)/shard_map/ppermute | solution.py:230
  167.6 2.4 %collective-permute-done.15.refs_7_ = bf16[2,3,96,128]{3,2,1,0:T(8,128)(2,1)S(1)} collective-permute-done((bf16[2,3,96,128]{3,2,1,0:T(8,128)(2,1)S(1)}, bf16[2,3,96,128]{3,2,1,0:T(8,128)(2,1)S(1)}, u32[]{:S(2)}, u32[]{:S(2)}) %collective-permute-start.15) | collective-permute-done | bytes 147488 | tf_op jit(solution)/shard_map/ppermute | solution.py:230
  170.3 2.0 collective-permute-done.16.refs_8_
  173.2 12.0 %shard_map.112 = (bf16[6,192,128]{2,1,0:T(8,128)(2,1)S(1)}, bf16[6,192,128]{2,1,0:T(8,128)(2,1)S(1)}, bf16[6,192,128]{2,1,0:T(8,128)(2,1)S(1)}, bf16[6,192,128]{2,1,0:T(8,128)(2,1)S(1)}) custom-call(s32[2]{0:T(128)S(1)} %pad_add_fusion.at, bf16[2,3,96,128]{3,2,1,0:T(8,128)(2,1)S(1)} %copy-done.16, ...), custom_call_target="tpu_custom_call" | custom-call | flops 7247757312 | bytes 9437184 | tf_op jit(solution)/shard_map/pallas_call | solution.py:317
  185.2 1.6 collective-permute-start.20
  187.2 1.6 collective-permute-start.22
  189.1 5.9 %collective-permute-done.20 = bf16[6,192,128]{2,1,0:T(8,128)(2,1)S(1)} collective-permute-done((bf16[6,192,128]{2,1,0:T(8,128)(2,1)S(1)}, bf16[6,192,128]{2,1,0:T(8,128)(2,1)S(1)}, u32[]{:S(2)}, u32[]{:S(2)}) %collective-permute-start.20) | collective-permute-done | bytes 294944 | tf_op jit(solution)/shard_map/ppermute | solution.py:230
  195.0 18.2 %collective-permute-done.21 = bf16[6,192,128]{2,1,0:T(8,128)(2,1)S(1)} collective-permute-done((bf16[6,192,128]{2,1,0:T(8,128)(2,1)S(1)}, bf16[6,192,128]{2,1,0:T(8,128)(2,1)S(1)}, u32[]{:S(2)}, u32[]{:S(2)}) %collective-permute-start.21) | collective-permute-done | bytes 294944 | tf_op jit(solution)/shard_map/ppermute | solution.py:230
  213.3 1.0 copy-done.19
  (90 shorter events, 8.7 us)
Async XLA Ops:
  6.5 165.8 %all-gather.3.cloned.1.call-start = ((), (), s32[]{:S(2)}) async-start(), calls=%async_computation.2 | async-start | bytes 9732096 | tf_op jit(solution)/shard_map/all_gather | solution.py:257
  6.5 11.2 %copy-start = (bf16[24,192,128]{2,1,0:T(8,128)(2,1)S(1)}, bf16[24,192,128]{2,1,0:T(8,128)(2,1)}, u32[]{:S(2)}) copy-start(bf16[24,192,128]{2,1,0:T(8,128)(2,1)} %param.11) | copy-start | bytes 3538948
  8.2 5.1 %collective-permute-start.17 = (bf16[48,768]{1,0:T(8,128)(2,1)S(1)}, bf16[48,768]{1,0:T(8,128)(2,1)S(1)}, u32[]{:S(2)}, u32[]{:S(2)}) collective-permute-start(bf16[48,768]{1,0:T(8,128)(2,1)S(1)} %get-tuple-element.38), channel_id=1, source_target_pairs={{0,1},{1,2},{2,3},{3,0},{4,5},{5,6},{6,7},{7,4},{8,9},{9,10},{10,1... | collective-permute-start | bytes 221192 | tf_op jit(solution)/shard_map/ppermute | solution.py:230
  9.2 7.7 %collective-permute-start.18 = (bf16[48,768]{1,0:T(8,128)(2,1)S(1)}, bf16[48,768]{1,0:T(8,128)(2,1)S(1)}, u32[]{:S(2)}, u32[]{:S(2)}) collective-permute-start(bf16[48,768]{1,0:T(8,128)(2,1)S(1)} %get-tuple-element.38), channel_id=1, source_target_pairs={{0,2},{1,3},{2,0},{3,1},{4,6},{5,7},{6,4},{7,5},{8,10},{9,11},{10,... | collective-permute-start | bytes 221192 | tf_op jit(solution)/shard_map/ppermute | solution.py:230
  9.9 7.1 %collective-permute-start.19 = (bf16[48,768]{1,0:T(8,128)(2,1)S(1)}, bf16[48,768]{1,0:T(8,128)(2,1)S(1)}, u32[]{:S(2)}, u32[]{:S(2)}) collective-permute-start(bf16[48,768]{1,0:T(8,128)(2,1)S(1)} %get-tuple-element.38), channel_id=1, source_target_pairs={{0,3},{1,0},{2,1},{3,2},{4,7},{5,4},{6,5},{7,6},{8,11},{9,8},{10,9... | collective-permute-start | bytes 221192 | tf_op jit(solution)/shard_map/ppermute | solution.py:230
  18.6 10.4 %copy-start.20 = (bf16[384,1536]{1,0:T(8,128)(2,1)S(1)}, bf16[384,1536]{1,0:T(8,128)(2,1)}, u32[]{:S(2)}) copy-start(bf16[384,1536]{1,0:T(8,128)(2,1)} %constant.141.clone) | copy-start | bytes 3538948
  18.6 10.4 %copy-start.24 = (s32[288]{0:T(512)S(1)}, s32[288]{0:T(512)}, u32[]{:S(2)}) copy-start(s32[288]{0:T(512)} %param.15) | copy-start | bytes 3460
  18.6 20.0 %collective-permute-start.1 = (bf16[4,2,3,96,128]{4,3,2,1,0:T(8,128)(2,1)}, bf16[4,2,3,96,128]{4,3,2,1,0:T(8,128)(2,1)S(1)}, u32[]{:S(2)}, u32[]{:S(2)}) collective-permute-start(bf16[4,2,3,96,128]{4,3,2,1,0:T(8,128)(2,1)} %dynamic-slice_bitcast_fusion), channel_id=1, source_target_pairs={{0,8},{8,0},{1,9},{9,1},{2,10},{10,2},{3,11},{11,3},{4,12},{12,4},... | collective-permute-start | bytes 1769480 | tf_op jit(solution)/shard_map/ppermute | solution.py:244
  24.3 4.5 %copy-start.21 = (f32[24,128]{1,0:T(8,128)}, f32[24,128]{1,0:T(8,128)S(1)}, u32[]{:S(2)}) copy-start(f32[24,128]{1,0:T(8,128)S(1)} %get-tuple-element.34) | copy-start | bytes 36868
  25.0 25.8 %collective-permute-start.3 = (f32[2,24,128]{2,0,1:T(2,128)}, f32[2,24,128]{2,0,1:T(2,128)}, u32[]{:S(2)}, u32[]{:S(2)}) collective-permute-start(f32[2,24,128]{2,0,1:T(2,128)} %pad_maximum_fusion.2), channel_id=1, source_target_pairs={{0,1},{1,2},{2,3},{3,0},{4,5},{5,6},{6,7},{7,4},{8,9},{9,10},{10,1... | collective-permute-start | bytes 73736 | tf_op jit(solution)/shard_map/ppermute | solution.py:230
  26.4 25.4 %collective-permute-start.4 = (f32[2,24,128]{2,0,1:T(2,128)}, f32[2,24,128]{2,0,1:T(2,128)}, u32[]{:S(2)}, u32[]{:S(2)}) collective-permute-start(f32[2,24,128]{2,0,1:T(2,128)} %pad_maximum_fusion.2), channel_id=1, source_target_pairs={{0,2},{1,3},{2,0},{3,1},{4,6},{5,7},{6,4},{7,5},{8,10},{9,11},{10,... | collective-permute-start | bytes 73736 | tf_op jit(solution)/shard_map/ppermute | solution.py:230
  26.8 25.0 %collective-permute-start.5 = (f32[2,24,128]{2,0,1:T(2,128)}, f32[2,24,128]{2,0,1:T(2,128)}, u32[]{:S(2)}, u32[]{:S(2)}) collective-permute-start(f32[2,24,128]{2,0,1:T(2,128)} %pad_maximum_fusion.2), channel_id=1, source_target_pairs={{0,3},{1,0},{2,1},{3,2},{4,7},{5,4},{6,5},{7,6},{8,11},{9,8},{10,9... | collective-permute-start | bytes 73736 | tf_op jit(solution)/shard_map/ppermute | solution.py:230
  28.9 32.7 %collective-permute-start = (bf16[4,3,96,128]{3,2,1,0:T(8,128)(2,1)S(1)}, bf16[4,3,96,128]{3,2,1,0:T(8,128)(2,1)S(1)}, u32[]{:S(2)}, u32[]{:S(2)}) collective-permute-start(bf16[4,3,96,128]{3,2,1,0:T(8,128)(2,1)S(1)} %dynamic-slice_bitcast_fusion.2), channel_id=1, source_target_pairs={{0,4},{4,0},{1,5},{5,1},{2,6},{6,2},{3,7},{7,3},{8,12},{12,8},{9,1... | collective-permute-start | bytes 884744 | tf_op jit(solution)/shard_map/ppermute | solution.py:249
  29.0 22.8 %copy-start.22 = (f32[24,128]{1,0:T(8,128)S(1)}, f32[24,128]{1,0:T(8,128)}, u32[]{:S(2)}) copy-start(f32[24,128]{1,0:T(8,128)} %copy-done.21) | copy-start | bytes 36868
  31.0 30.4 %copy-start.25 = (f32[192]{0:T(256)S(1)}, f32[192]{0:T(256)}, u32[]{:S(2)}) copy-start(f32[192]{0:T(256)} %param.12) | copy-start | bytes 2308
  38.6 23.7 %copy-start.1 = (bf16[4,2,3,96,128]{4,3,2,1,0:T(8,128)(2,1)}, bf16[4,2,3,96,128]{4,3,2,1,0:T(8,128)(2,1)S(1)}, u32[]{:S(2)}) copy-start(bf16[4,2,3,96,128]{4,3,2,1,0:T(8,128)(2,1)S(1)} %collective-permute-done.1.far) | copy-start | bytes 1769476
  38.7 23.7 %collective-permute-start.2 = (bf16[4,3,96,128]{3,2,1,0:T(8,128)(2,1)S(1)}, bf16[4,3,96,128]{3,2,1,0:T(8,128)(2,1)S(1)}, u32[]{:S(2)}, u32[]{:S(2)}) collective-permute-start(bf16[4,3,96,128]{3,2,1,0:T(8,128)(2,1)S(1)} %dynamic-slice_bitcast_fusion.1), channel_id=1, source_target_pairs={{0,4},{4,0},{1,5},{5,1},{2,6},{6,2},{3,7},{7,3},{8,12},{12,8},{9,1... | collective-permute-start | bytes 884744 | tf_op jit(solution)/shard_map/ppermute | solution.py:251
  52.6 8.9 %collective-permute-start.6 = (f32[2,24,128]{2,0,1:T(2,128)S(1)}, f32[2,24,128]{2,0,1:T(2,128)S(1)}, u32[]{:S(2)}, u32[]{:S(2)}) collective-permute-start(f32[2,24,128]{2,0,1:T(2,128)S(1)} %add_add_fusion), channel_id=1, source_target_pairs={{0,4},{4,0},{8,12},{12,8},{1,5},{5,1},{9,13},{13,9},{2,6},{6,2},{1... | collective-permute-start | bytes 73736 | tf_op jit(solution)/shard_map/ppermute | solution.py:236
  52.7 8.8 %collective-permute-start.7 = (f32[2,24,128]{2,0,1:T(2,128)S(1)}, f32[2,24,128]{2,0,1:T(2,128)S(1)}, u32[]{:S(2)}, u32[]{:S(2)}) collective-permute-start(f32[2,24,128]{2,0,1:T(2,128)S(1)} %add_add_fusion), channel_id=1, source_target_pairs={{0,8},{4,12},{8,0},{12,4},{1,9},{5,13},{9,1},{13,5},{2,10},{6,14},... | collective-permute-start | bytes 73736 | tf_op jit(solution)/shard_map/ppermute | solution.py:236
  52.8 8.7 %collective-permute-start.8 = (f32[2,24,128]{2,0,1:T(2,128)S(1)}, f32[2,24,128]{2,0,1:T(2,128)S(1)}, u32[]{:S(2)}, u32[]{:S(2)}) collective-permute-start(f32[2,24,128]{2,0,1:T(2,128)S(1)} %add_add_fusion), channel_id=1, source_target_pairs={{0,12},{4,8},{8,4},{12,0},{1,13},{5,9},{9,5},{13,1},{2,14},{6,10},... | collective-permute-start | bytes 73736 | tf_op jit(solution)/shard_map/ppermute | solution.py:236
  61.6 0.7 copy-start.9
  62.3 0.7 copy-start.11
  63.1 1.1 copy-start.2
  64.2 1.1 copy-start.8
  65.3 1.0 copy-start.10
  66.2 1.0 copy-start.12
  69.4 1.0 copy-start.3
  70.4 26.6 %all-to-all-start = ((bf16[32,16,1152]{2,1,0:T(8,128)(2,1)}), bf16[32,16,1152]{2,1,0:T(8,128)(2,1)S(1)}, u32[]{:S(2)}, u32[]{:S(2)}) async-start(bf16[32,16,1152]{2,1,0:T(8,128)(2,1)} %copy-done.3), calls=%async_computation | async-start | bytes 2359296 | tf_op jit(solution)/shard_map/all_to_all | solution.py:276
  80.2 0.9 copy-start.17
  85.6 4.7 %copy-start.18 = (bf16[288,768]{0,1:T(8,128)(2,1)S(1)}, bf16[288,768]{0,1:T(8,128)(2,1)}, u32[]{:S(2)}) copy-start(bf16[288,768]{0,1:T(8,128)(2,1)} %copy-done.17) | copy-start | bytes 1327108
  97.0 1.2 copy-start.5
  98.2 1.2 copy-start.6
  99.3 0.9 copy-start.13
  100.2 0.9 copy-start.14
  105.9 1.0 copy-start.4
  106.9 23.0 %all-to-all-start.1 = ((bf16[32,16,1152]{2,1,0:T(8,128)(2,1)}), bf16[32,16,1152]{2,1,0:T(8,128)(2,1)S(1)}, u32[]{:S(2)}, u32[]{:S(2)}) async-start(bf16[32,16,1152]{2,1,0:T(8,128)(2,1)} %copy-done.4), calls=%async_computation.1 | async-start | bytes 2359296 | tf_op jit(solution)/shard_map/all_to_all | solution.py:296
  129.8 1.0 copy-start.7
  132.4 39.9 %copy-start.23 = (f32[768]{0:T(1024)S(1)}, f32[768]{0:T(1024)}, u32[]{:S(2)}) copy-start(f32[768]{0:T(1024)} %param.16) | copy-start | bytes 9220
  132.5 14.3 %collective-permute-start.9 = (bf16[2,3,96,128]{3,2,1,0:T(8,128)(2,1)S(1)}, bf16[2,3,96,128]{3,2,1,0:T(8,128)(2,1)S(1)}, u32[]{:S(2)}, u32[]{:S(2)}) collective-permute-start(bf16[2,3,96,128]{3,2,1,0:T(8,128)(2,1)S(1)} %get-tuple-element.22), channel_id=1, source_target_pairs={{0,1},{1,2},{2,3},{3,8},{8,9},{9,10},{10,11},{11,0},{4,5},{5,6},{6... | collective-permute-start | bytes 442376 | tf_op jit(solution)/shard_map/ppermute | solution.py:230
  136.5 18.7 %collective-permute-start.10 = (bf16[2,3,96,128]{3,2,1,0:T(8,128)(2,1)S(1)}, bf16[2,3,96,128]{3,2,1,0:T(8,128)(2,1)S(1)}, u32[]{:S(2)}, u32[]{:S(2)}) collective-permute-start(bf16[2,3,96,128]{3,2,1,0:T(8,128)(2,1)S(1)} %get-tuple-element.23), channel_id=1, source_target_pairs={{0,2},{1,3},{2,8},{3,9},{8,10},{9,11},{10,0},{11,1},{4,6},{5,7},{6... | collective-permute-start | bytes 442376 | tf_op jit(solution)/shard_map/ppermute | solution.py:230
  137.7 0.7 copy-start.15
  138.3 24.9 %collective-permute-start.11 = (bf16[2,3,96,128]{3,2,1,0:T(8,128)(2,1)S(1)}, bf16[2,3,96,128]{3,2,1,0:T(8,128)(2,1)S(1)}, u32[]{:S(2)}, u32[]{:S(2)}) collective-permute-start(bf16[2,3,96,128]{3,2,1,0:T(8,128)(2,1)S(1)} %get-tuple-element.24), channel_id=1, source_target_pairs={{0,3},{1,8},{2,9},{3,10},{8,11},{9,0},{10,1},{11,2},{4,7},{5,12},{... | collective-permute-start | bytes 442376 | tf_op jit(solution)/shard_map/ppermute | solution.py:230
  143.4 19.9 %collective-permute-start.12 = (bf16[2,3,96,128]{3,2,1,0:T(8,128)(2,1)S(1)}, bf16[2,3,96,128]{3,2,1,0:T(8,128)(2,1)S(1)}, u32[]{:S(2)}, u32[]{:S(2)}) collective-permute-start(bf16[2,3,96,128]{3,2,1,0:T(8,128)(2,1)S(1)} %get-tuple-element.25), channel_id=1, source_target_pairs={{0,8},{1,9},{2,10},{3,11},{8,0},{9,1},{10,2},{11,3},{4,12},{5,13},... | collective-permute-start | bytes 442376 | tf_op jit(solution)/shard_map/ppermute | solution.py:230
  144.7 20.4 %collective-permute-start.13 = (bf16[2,3,96,128]{3,2,1,0:T(8,128)(2,1)S(1)}, bf16[2,3,96,128]{3,2,1,0:T(8,128)(2,1)S(1)}, u32[]{:S(2)}, u32[]{:S(2)}) collective-permute-start(bf16[2,3,96,128]{3,2,1,0:T(8,128)(2,1)S(1)} %get-tuple-element.26), channel_id=1, source_target_pairs={{0,9},{1,10},{2,11},{3,0},{8,1},{9,2},{10,3},{11,8},{4,13},{5,14},... | collective-permute-start | bytes 442376 | tf_op jit(solution)/shard_map/ppermute | solution.py:230
  146.8 20.8 %collective-permute-start.14 = (bf16[2,3,96,128]{3,2,1,0:T(8,128)(2,1)S(1)}, bf16[2,3,96,128]{3,2,1,0:T(8,128)(2,1)S(1)}, u32[]{:S(2)}, u32[]{:S(2)}) collective-permute-start(bf16[2,3,96,128]{3,2,1,0:T(8,128)(2,1)S(1)} %get-tuple-element.27), channel_id=1, source_target_pairs={{0,10},{1,11},{2,0},{3,1},{8,2},{9,3},{10,8},{11,9},{4,14},{5,15},... | collective-permute-start | bytes 442376 | tf_op jit(solution)/shard_map/ppermute | solution.py:230
  155.2 14.8 %collective-permute-start.15 = (bf16[2,3,96,128]{3,2,1,0:T(8,128)(2,1)S(1)}, bf16[2,3,96,128]{3,2,1,0:T(8,128)(2,1)S(1)}, u32[]{:S(2)}, u32[]{:S(2)}) collective-permute-start(bf16[2,3,96,128]{3,2,1,0:T(8,128)(2,1)S(1)} %get-tuple-element.28), channel_id=1, source_target_pairs={{0,11},{1,0},{2,1},{3,2},{8,3},{9,8},{10,9},{11,10},{4,15},{5,4},{... | collective-permute-start | bytes 442376 | tf_op jit(solution)/shard_map/ppermute | solution.py:230
  170.0 2.3 %collective-permute-start.16 = (bf16[8,3,96,128]{3,2,1,0:T(8,128)(2,1)S(1)}, bf16[8,3,96,128]{3,2,1,0:T(8,128)(2,1)S(1)}, u32[]{:S(2)}, u32[]{:S(2)}) collective-permute-start(bf16[8,3,96,128]{3,2,1,0:T(8,128)(2,1)S(1)} %dynamic-slice_dynamic-update-slice_fusion), channel_id=1, source_target_pairs={{0,4},{4,0},{1,5},{5,1},{2,6},{6,2},{3,7},{7,3},{8,12},{12,8},{9,1... | collective-permute-start | bytes 1769480 | tf_op jit(solution)/shard_map/ppermute | solution.py:311
  172.3 0.9 copy-start.16
  185.2 9.8 %collective-permute-start.20 = (bf16[6,192,128]{2,1,0:T(8,128)(2,1)S(1)}, bf16[6,192,128]{2,1,0:T(8,128)(2,1)S(1)}, u32[]{:S(2)}, u32[]{:S(2)}) collective-permute-start(bf16[6,192,128]{2,1,0:T(8,128)(2,1)S(1)} %get-tuple-element.30), channel_id=1, source_target_pairs={{0,1},{1,2},{2,3},{3,0},{4,5},{5,6},{6,7},{7,4},{8,9},{9,10},{10,1... | collective-permute-start | bytes 884744 | tf_op jit(solution)/shard_map/ppermute | solution.py:230
  186.8 26.4 %collective-permute-start.21 = (bf16[6,192,128]{2,1,0:T(8,128)(2,1)S(1)}, bf16[6,192,128]{2,1,0:T(8,128)(2,1)S(1)}, u32[]{:S(2)}, u32[]{:S(2)}) collective-permute-start(bf16[6,192,128]{2,1,0:T(8,128)(2,1)S(1)} %get-tuple-element.31), channel_id=1, source_target_pairs={{0,2},{1,3},{2,0},{3,1},{4,6},{5,7},{6,4},{7,5},{8,10},{9,11},{10,... | collective-permute-start | bytes 884744 | tf_op jit(solution)/shard_map/ppermute | solution.py:230
  187.2 26.0 %collective-permute-start.22 = (bf16[6,192,128]{2,1,0:T(8,128)(2,1)S(1)}, bf16[6,192,128]{2,1,0:T(8,128)(2,1)S(1)}, u32[]{:S(2)}, u32[]{:S(2)}) collective-permute-start(bf16[6,192,128]{2,1,0:T(8,128)(2,1)S(1)} %get-tuple-element.32), channel_id=1, source_target_pairs={{0,3},{1,0},{2,1},{3,2},{4,7},{5,4},{6,5},{7,6},{8,11},{9,8},{10,9... | collective-permute-start | bytes 884744 | tf_op jit(solution)/shard_map/ppermute | solution.py:230
  213.3 1.0 copy-start.19
Sparse Core Ops, SparseCore 0:
  17.8 63.1 all-gather.2

commit v3 on v2

--- a/solution.py
+++ b/solution.py
@@ -16,7 +16,8 @@
 EPSILON = 1e-05
 BF16 = jnp.bfloat16
 F32 = jnp.float32
-VMEM_LIMIT = 40 * 1024 * 1024
+SMALL = 32 * 1024 * 1024
+LARGE = 56 * 1024 * 1024
 
 
 def dot(left, right, dims=((1,), (0,))):
@@ -27,7 +28,7 @@
     return pl.BlockSpec(shape, lambda *_: (0,) * len(shape))
 
 
-def call(kernel, scalars, args, outs, scratch, flops):
+def call(kernel, scalars, args, outs, scratch, flops, limit=SMALL):
     moved = sum(a.size * a.dtype.itemsize for a in (*args, *outs))
     return pl.pallas_call(
         kernel,
@@ -39,7 +40,7 @@
             scratch_shapes=scratch,
         ),
         out_shape=outs,
-        compiler_params=pltpu.CompilerParams(vmem_limit_bytes=VMEM_LIMIT),
+        compiler_params=pltpu.CompilerParams(vmem_limit_bytes=limit),
         cost_estimate=pl.CostEstimate(flops=flops, bytes_accessed=moved, transcendentals=0),
     )(scalars, *args)
 
@@ -77,33 +78,44 @@
     ).astype(BF16)
 
 
-def forward_kernel(full, at, own, near, far, across, stats, gain, table, spec, base, normed):
-    core, lon = at[0], at[2]
+def strips(at, own, near, far, across):
+    core, high, lon = at[0], at[1], at[2]
+    trip = near.shape[1]
     parts = (
-        lambda c, t: own[c, core, t, at[1]],
+        lambda c, t: own[c, core, t, high],
         lambda c, t: near[c, t],
         lambda c, t: far[c, core, t],
         lambda c, t: across[c, t],
     )
-    groups, trip = near.shape[0], near.shape[1]
     for d, part in enumerate(parts):
         lanes = pl.ds(pl.multiple_of((lon ^ d) * LANES, LANES), LANES)
-        mean = stats[d, 0] / full
-        scale = lax.rsqrt(stats[d, 1] / full - mean * mean + EPSILON)
-        for c in range(groups):
-            for t in range(trip):
-                r = c * trip + t
-                values = part(c, t).astype(F32)
-                value = (values - mean[r : r + 1]) * scale[r : r + 1] * gain[...]
-                value = value.astype(BF16)
-                rows = slice(r * BS, (r + 1) * BS)
-                normed[rows, lanes] = value
-                base[rows, lanes] = values + value.astype(F32)
+        for r in range(near.shape[0] * trip):
+            yield r, lanes, part(r // trip, r % trip).astype(F32)
+
+
+def forward_kernel(full, at, own, near, far, across, chip, partner, gain, table, *refs):
+    spec, base, normed, mean, scale = refs
+    for d in range(4):
+        stats = (chip if d < 2 else partner)[d % 2] / full
+        mean[d] = stats[0]
+        scale[d] = lax.rsqrt(stats[1] - stats[0] * stats[0] + EPSILON)
+    count, trip = near.shape[0] * near.shape[1], near.shape[1]
+    for i, (r, lanes, values) in enumerate(strips(at, own, near, far, across)):
+        d = i // count
+        low = r + (r // trip) * trip
+        picked = []
+        for ref in (mean, scale):
+            rows = ref[d, low : low + 1], ref[d, low + trip : low + trip + 1]
+            picked.append(jnp.where(at[0] == 0, *rows))
+        value = ((values - picked[0]) * picked[1] * gain[...]).astype(BF16)
+        rows = slice(r * BS, (r + 1) * BS)
+        normed[rows, lanes] = value
+        base[rows, lanes] = values + value.astype(F32)
     result = dot(table[...], normed[...], ((1,), (1,)))
     spec[...] = result.astype(BF16).reshape(spec.shape)
 
 
-def middle_kernel(at, columns, left, right, first_w, second_w, out, wide, stacked, mid):
+def middle_kernel(at, columns, left, first_w, second_w, out, wide, stacked, mid):
     srcs, pairs, inner = columns.shape
     modes = pairs // 2
     local = inner // BS
@@ -134,7 +146,7 @@
         ).astype(BF16)
         mid[:kept, lanes] = both[:, :LANES]
         mid[kept:, lanes] = both[:, LANES:]
-    back = dot(right[...], mid[...])
+    back = dot(left[...], mid[...], ((0,), (0,)))
     for t in range(2):
         for k in range(modes):
             lanes = slice(k * LANES, k * LANES + BS)
@@ -169,46 +181,49 @@
             out[c] = first[rows, lanes].reshape(trip, BS, LANES)
 
 
-def token_kernel(at, *refs):
-    mine, theirs, gain, up, down = refs[:8], refs[8], refs[9], refs[10], refs[11]
-    outs, (first, ready, total) = refs[12:16], refs[16:]
-    step = pl.program_id(0)
+def token_kernel(order, at, *refs):
+    count = len(order)
+    mine, theirs, gain, weights = refs[:count], *refs[count : count + 3]
+    outs, (first, ready, total, held, done) = refs[count + 3 : -5], refs[-5:]
     core = at[1]
     trip = theirs.shape[1]
     groups = len(outs)
-    count = len(mine)
-
-    @pl.when(step == 0)
-    def _():
-        for d, ref in enumerate(mine):
-            place = lax.rem(at[0] - d + count, count)
-            row = (lax.rem(place, groups) * (count // groups) + place // groups) * BS
-            rows = pl.ds(pl.multiple_of(row, BS), BS)
-            for t in range(trip):
-                own = pl.ds(pl.multiple_of((core * trip + t) * LANES, LANES), LANES)
-                first[rows, own] = ref[core, t]
-                other = pl.ds(pl.multiple_of(((1 - core) * trip + t) * LANES, LANES), LANES)
-                first[rows, other] = theirs[d, t]
-        values = first[...].astype(F32)
-        mean = jnp.mean(values, axis=0, keepdims=True)
-        values = values - mean
+    steps = held.shape[0]
+    pair = weights.shape[2]
+    copies = [
+        pltpu.make_async_copy(weights.at[:, i // pair, i % pair], held.at[i], done.at[i])
+        for i in range(steps)
+    ]
+    for copy in copies:
+        copy.start()
+    for i, ref in enumerate(mine):
+        place = lax.rem(at[0] - order[i] + count, count)
+        row = (lax.rem(place, groups) * (count // groups) + place // groups) * BS
+        rows = pl.ds(pl.multiple_of(row, BS), BS)
+        for t in range(trip):
+            own = pl.ds(pl.multiple_of((core * trip + t) * LANES, LANES), LANES)
+            first[rows, own] = ref[core, t]
+            other = pl.ds(pl.multiple_of(((1 - core) * trip + t) * LANES, LANES), LANES)
+            first[rows, other] = theirs[i, t]
+    for r in range(2 * trip):
+        lanes = slice(r * LANES, (r + 1) * LANES)
+        values = first[:, lanes].astype(F32)
+        total[:, lanes] = values
+        values = values - jnp.mean(values, axis=0, keepdims=True)
         spread = jnp.mean(values * values, axis=0, keepdims=True)
-        ready[...] = (values * lax.rsqrt(spread + EPSILON) * gain[...]).astype(BF16)
-        total[...] = first[...].astype(F32)
-
+        ready[:, lanes] = (values * lax.rsqrt(spread + EPSILON) * gain[...]).astype(BF16)
     side = first.shape[0]
-    hidden = dot(up[...].reshape(-1, side), ready[...])
-    hidden = jax.nn.gelu(hidden).astype(BF16)
-    total[...] += dot(down[...].reshape(side, -1), hidden)
-
-    @pl.when(step == pl.num_programs(0) - 1)
-    def _():
-        chans = outs[0].shape[1]
-        for d, out in enumerate(outs):
-            low = lax.rem(lax.rem(at[0], groups) + d, groups)
-            rows = pl.ds(pl.multiple_of(low * chans, chans), chans)
-            for r in range(out.shape[0]):
-                out[r] = total[rows, r * LANES : (r + 1) * LANES].astype(BF16)
+    for i, copy in enumerate(copies):
+        copy.wait()
+        hidden = dot(held[i, :, 0].reshape(-1, side), ready[...])
+        hidden = jax.nn.gelu(hidden).astype(BF16)
+        total[...] += dot(held[i, :, 1].reshape(side, -1), hidden)
+    chans = outs[0].shape[1]
+    for d, out in enumerate(outs):
+        low = lax.rem(lax.rem(at[0], groups) + d, groups)
+        rows = pl.ds(pl.multiple_of(low * chans, chans), chans)
+        for r in range(out.shape[0]):
+            out[r] = total[rows, r * LANES : (r + 1) * LANES].astype(BF16)
 
 
 def on_device(tokens, gain_first, mode_first, mode_second, kept_lat, gain_second, w_up, w_down):
@@ -229,62 +244,83 @@
     def ring(array, axes, count, step):
         return lax.ppermute(array, axes, [(i, (i + step) % count) for i in range(count)])
 
+    piece_n = w_up.shape[1] // lat_n
+    piece = jnp.stack(
+        [
+            lax.dynamic_slice_in_dim(w, lat * piece_n, piece_n, axis=1).T
+            for w in (w_up, w_down)
+        ]
+    )
+    pieces = [
+        lax.ppermute(
+            piece,
+            ("co", "ch"),
+            [(c * ch_n + i, c * ch_n + (i + 2 * c + d) % ch_n) for c in range(co_n) for i in range(ch_n)],
+        )
+        for d in range(ch_n // co_n)
+    ]
+    pieces = jnp.stack(pieces)
+
     values = tokens.astype(F32)
     sums = jnp.stack([jnp.sum(values, axis=1), jnp.sum(values * values, axis=1)])
     sums = sums + sum(ring(sums, "ch", ch_n, d) for d in range(1, ch_n))
-    shared = [sums] + [
-        lax.ppermute(sums, ("zh", "co"), [(i, i ^ d) for i in range(lon_n)])
-        for d in range(1, lon_n)
-    ]
-    stats = jnp.stack(shared).reshape(lon_n, 2, ch_n, co_n, trip, cols)
-    stats = lax.dynamic_index_in_dim(stats, co, axis=3, keepdims=False)
-    stats = stats.reshape(lon_n, 2, half, cols)
-
-    own = tokens.reshape(ch_n, co_n, trip, zh_n, BS, cols)
+
+    block_gain = lax.dynamic_slice_in_dim(gain_first, zh * BS, BS)
+    block_gain = jnp.broadcast_to(block_gain[:, None], (BS, cols))
+    second_gain = jnp.broadcast_to(gain_second[:, None], (full, cols))
+    place = jnp.stack([co, zh, lon]).astype(jnp.int32)
+    column = jnp.stack([z, co]).astype(jnp.int32)
+    pieces, sums, sent, block_gain, second_gain, place, column = lax.optimization_barrier(
+        (pieces, sums, tokens, block_gain, second_gain, place, column)
+    )
+    weights = lax.all_gather(pieces, ("lat", "co"))
+    own = sent.reshape(ch_n, co_n, trip, zh_n, BS, cols)
     far = lax.ppermute(
         lax.dynamic_index_in_dim(own, 1 - zh, axis=3, keepdims=False), "zh", swap
     )
+    chip_sums = jnp.stack([sums, lax.ppermute(sums, "co", swap)])
+    partner_sums = lax.ppermute(chip_sums, "zh", swap)
+    order = np.arange(height).reshape(lat_n, ch_n, co_n, trip).transpose(1, 3, 0, 2).reshape(-1)
+    left = lat_table(kept_lat, height, order)
+    kept = kept_lat.shape[0]
+    first_w = mode_weight(lax.dynamic_index_in_dim(mode_first, zh, axis=0, keepdims=False))
+    second_w = mode_weight(lax.dynamic_index_in_dim(mode_second, zh, axis=0, keepdims=False))
+    (far, chip_sums, partner_sums), tables = lax.optimization_barrier(
+        (
+            (far, chip_sums, partner_sums),
+            (left, first_w, second_w),
+        )
+    )
+    left, first_w, second_w = tables
     near = lax.dynamic_index_in_dim(own, zh, axis=3, keepdims=False)
     near = lax.dynamic_index_in_dim(near, 1 - co, axis=1, keepdims=False)
     near = lax.ppermute(near, "co", swap)
     across = lax.dynamic_index_in_dim(far, 1 - co, axis=1, keepdims=False)
     across = lax.ppermute(across, "co", swap)
-
-    picked = jnp.where(co == 0, w_up, w_down).T
-    piece_n = picked.shape[0] // lat_n
-    piece = lax.dynamic_slice_in_dim(picked, lat * piece_n, piece_n, axis=0)
-    pieces = jnp.stack([piece] + [ring(piece, "ch", ch_n, d) for d in range(1, ch_n)])
-    weights = lax.all_gather(pieces, ("lat", "co"))
-    weights = weights.reshape(lat_n, co_n, ch_n, piece_n, full)
-
     forward, inverse = lon_tables(width, dests)
-    gain = lax.dynamic_slice_in_dim(gain_first, zh * BS, BS)
-    gain = jnp.broadcast_to(gain[:, None], (BS, cols))
-    at = jnp.stack([co, zh, lon]).astype(jnp.int32)
     wide_n = half * BS
     spec, base = call(
         functools.partial(forward_kernel, float(full)),
-        at,
-        (own, near, far, across, stats, gain, jnp.asarray(forward, BF16)),
+        place,
+        (own, near, far, across, chip_sums, partner_sums, block_gain, jnp.asarray(forward, BF16)),
         (
             jax.ShapeDtypeStruct((dests, 2 * KW // dests, wide_n), BF16),
             jax.ShapeDtypeStruct((wide_n, width), F32),
         ),
-        [pltpu.VMEM((wide_n, width), BF16)],
+        [
+            pltpu.VMEM((wide_n, width), BF16),
+            pltpu.VMEM((lon_n, rows, cols), F32),
+            pltpu.VMEM((lon_n, rows, cols), F32),
+        ],
         4 * KW * width * wide_n,
     )
     columns = lax.all_to_all(spec, ("lat", "co"), split_axis=0, concat_axis=0, tiled=True)
 
     modes = KW // dests
-    order = np.arange(height).reshape(lat_n, ch_n, co_n, trip).transpose(1, 3, 0, 2).reshape(-1)
-    left = lat_table(kept_lat, height, order)
-    kept = kept_lat.shape[0]
-    first_w = mode_weight(lax.dynamic_index_in_dim(mode_first, zh, axis=0, keepdims=False))
-    second_w = mode_weight(lax.dynamic_index_in_dim(mode_second, zh, axis=0, keepdims=False))
     (back,) = call(
         middle_kernel,
-        at,
-        (columns, left, left.T, first_w, second_w),
+        place,
+        (columns, left, first_w, second_w),
         (jax.ShapeDtypeStruct(columns.shape, BF16),),
         [
             pltpu.VMEM((wide_n // LANES, dests * 2 * modes, LANES), F32),
@@ -295,50 +331,49 @@
     )
     returned = lax.all_to_all(back, ("lat", "co"), split_axis=0, concat_axis=0, tiled=True)
 
-    at = jnp.stack([z, co]).astype(jnp.int32)
+    returned, weights = lax.optimization_barrier((returned, weights))
+    weights = weights.reshape(lat_n, co_n, ch_n // co_n, 2, piece_n, full)
     firsts = call(
         inverse_kernel,
-        at,
+        column,
         (returned.reshape(2 * KW, wide_n), jnp.asarray(inverse, BF16), base),
         tuple(jax.ShapeDtypeStruct((co_n, trip, BS, cols), BF16) for _ in range(z_n)),
         [pltpu.VMEM((wide_n, width), BF16)],
         4 * KW * width * wide_n,
-    )
-    mine = [firsts[0]] + [ring(firsts[d], ("zh", "ch"), z_n, d) for d in range(1, z_n)]
+        SMALL,
+    )
+    order = sorted(range(z_n), key=lambda d: (min(d, z_n - d), -d))
+    mine = [ring(firsts[d], ("zh", "ch"), z_n, d) if d else firsts[0] for d in order]
     theirs = jnp.stack(
         [lax.dynamic_index_in_dim(m, 1 - co, axis=0, keepdims=False) for m in mine]
     )
     theirs = lax.ppermute(theirs, "co", swap)
 
     tokens_n = co_n * trip * cols
-    gain = jnp.broadcast_to(gain_second[:, None], (full, tokens_n))
-    once = [whole(m.shape) for m in mine] + [whole(theirs.shape), whole(gain.shape)]
-    weight_block = (lat_n, None, None, piece_n, full)
+    once = [*mine, theirs, second_gain]
     results = pl.pallas_call(
-        token_kernel,
+        functools.partial(token_kernel, order),
         grid_spec=pltpu.PrefetchScalarGridSpec(
             num_scalar_prefetch=1,
-            grid=(ch_n,),
-            in_specs=once
-            + [
-                pl.BlockSpec(weight_block, lambda i, at: (0, 0, i, 0, 0)),
-                pl.BlockSpec(weight_block, lambda i, at: (0, 1, i, 0, 0)),
-            ],
+            grid=(1,),
+            in_specs=[whole(a.shape) for a in once] + [pl.BlockSpec(memory_space=pltpu.HBM)],
             out_specs=[whole((co_n * trip, chans, cols))] * ch_n,
             scratch_shapes=[
                 pltpu.VMEM((full, tokens_n), BF16),
                 pltpu.VMEM((full, tokens_n), BF16),
                 pltpu.VMEM((full, tokens_n), F32),
+                pltpu.VMEM((ch_n, lat_n, 2, piece_n, full), BF16),
+                pltpu.SemaphoreType.DMA((ch_n,)),
             ],
         ),
         out_shape=[jax.ShapeDtypeStruct((co_n * trip, chans, cols), BF16)] * ch_n,
-        compiler_params=pltpu.CompilerParams(vmem_limit_bytes=VMEM_LIMIT),
+        compiler_params=pltpu.CompilerParams(vmem_limit_bytes=LARGE),
         cost_estimate=pl.CostEstimate(
             flops=4 * full * full * ch_n * tokens_n,
             bytes_accessed=weights.size * 2,
             transcendentals=full * ch_n * tokens_n,
         ),
-    )(at, *mine, theirs, gain, weights, weights)
+    )(column, *once, weights)
     output = jnp.zeros((ch_n, co_n * trip, chans, cols), BF16)
     for d, piece in enumerate(results):
         piece = piece if d == 0 else ring(piece, "ch", ch_n, d)

time: 225 us -> 215 us (0.956); the launches traced: 221 us -> 215 us
  blocking collectives: 0 us -> 58.4 us
  waiting for transfers between devices: 96.6 us -> 71.3 us
  starting transfers between devices: 49.4 us -> 32.4 us
  local copies, waits for them, and re-layouts: 28.5 us -> 11.9 us
  other arithmetic: 10.5 us -> 4.19 us
    all_to_all x0 -> x2, blocking collectives: none -> 58.4 us  [the longest x1 35.9 us: on_device(): lax.all_to_all(spec, ('lat', 'co'), split_axis=0, concat_axis=0, tiled=True)]
    ppermute x3 -> x4, waiting for transfers between devices: 0.01 us -> 23.2 us  [the longest x1 22.7 us: on_device(): partner_sums = lax.ppermute(chip_sums, 'zh', swap)]
    all_to_all x2 -> x0, waiting for transfers between devices: 23.2 us -> none  [the longest x1 18.9 us: on_device(): lax.all_to_all(back, ('lat', 'co'), split_axis=0, concat_axis=0, tiled=True)]
    ppermute x16 -> x13, waiting for transfers between devices: 63.8 us -> 45.2 us  [ring(): lax.ppermute(array, axes, [(i, (i + step) % count) for i in range(count)])]
    all_to_all x2 -> x0, starting transfers between devices: 11.5 us -> none  [the longest x1 7.55 us: on_device(): lax.all_to_all(spec, ('lat', 'co'), split_axis=0, concat_axis=0, tiled=True)]
    unnamed x61 -> x65, local copies, waits for them, and re-layouts: 16.3 us -> 6.84 us
    ppermute x1, waiting for transfers between devices: 7.6 us -> 0.01 us  [on_device(): lax.ppermute(lax.dynamic_index_in_dim(own, 1 - zh, axis=3, keepdims=False...]
    ppermute x3 -> x4, starting transfers between devices: 5.87 us -> 1.94 us  [the longest x2 1.81 us: on_device(): lax.ppermute(piece, ('co', 'ch'), [(c * ch_n + i, c * ch_n + (i + 2 * c +...]
  transfers between devices with their start and end apart: 26 -> 22, of which waited for: 15 -> 13; matrix products, arithmetic and copies ran while one was open for 10% -> 3% of each run, Pallas kernels for 4% -> 3%
where the time goes in v3:
time: 215 us
  waiting for transfers between devices  71.3 us (33%)
  blocking collectives  58.4 us (27%)
  starting transfers between devices  32.4 us (15%)
  Pallas kernels  21.9 us (10%)
  between operations  13.8 us (6%)
  local copies, waits for them, and re-layouts  11.9 us (6%)
  other arithmetic  4.19 us (2%)
    ppermute x13, waiting for transfers between devices, ring(): lax.ppermute(array, axes, [(i, (i + step) % count) for i in range(count)])  45.2 us
    all_to_all x1, blocking collectives, on_device(): lax.all_to_all(spec, ('lat', 'co'), split_axis=0, concat_axis=0, tiled=True)  35.9 us
    ppermute x13, starting transfers between devices, ring(): lax.ppermute(array, axes, [(i, (i + step) % count) for i in range(count)])  23.7 us
    ppermute x1, waiting for transfers between devices, on_device(): partner_sums = lax.ppermute(chip_sums, 'zh', swap)  22.7 us
    all_to_all x1, blocking collectives, on_device(): lax.all_to_all(back, ('lat', 'co'), split_axis=0, concat_axis=0, tiled=True)  22.5 us
    pallas_call x1, Pallas kernels, on_device(): pl.pallas_call(functools.partial(token_kernel, order), grid_spec=pltpu.Pr...  13.4 us
    pallas_call x3, Pallas kernels, call(): pl.pallas_call(kernel, grid_spec=pltpu.PrefetchScalarGridSpec(num_scalar_...  8.53 us
    unnamed x65, local copies, waits for them, and re-layouts  6.84 us
  transfers between devices with their start and end apart: 22, of which 13 were waited for; matrix products, arithmetic and copies ran while one was open for 3% of the time, Pallas kernels for 3%

profile of v3, /device:TPU:96, one launch (start us, length us, event | category | flops | bytes accessed | tf_op | source)
XLA Modules:
  0.0 214.6 jit_solution(17181114944535512072)
XLA Ops:
  6.5 1.4 constant_dynamic-slice_fusion
  7.9 0.1 copy.15
  8.1 0.1 copy.16
  8.3 0.8 collective-permute-start
  9.1 1.0 collective-permute-start.1
  10.1 0.3 convert_reduce_fusion
  10.5 0.3 collective-permute-start.2
  10.7 2.4 %collective-permute-start.3 = (f32[2,24,128]{2,1,0:T(8,128)S(1)}, f32[2,24,128]{2,1,0:T(8,128)S(1)}, u32[]{:S(2)}, u32[]{:S(2)}) collective-permute-start(f32[2,24,128]{2,1,0:T(8,128)S(1)} %pad_maximum_fusion.4), channel_id=1, source_target_pairs={{0,2},{1,3},{2,0},{3,1},{4,6},{5,7},{6,4},{7,5},{8,10},{9,11},{10,... | collective-permute-start | bytes 73736 | tf_op jit(solution)/shard_map/ppermute | solution.py:245
  13.1 0.1 collective-permute-start.4
  13.2 0.1 pad_add_fusion.1.at
  13.3 0.1 pad_add_fusion.at
  13.3 0.1 dynamic_slice.55
  13.4 1.4 collective-permute-done.2
  14.8 4.6 %collective-permute-done.3 = f32[2,24,128]{2,1,0:T(8,128)S(1)} collective-permute-done((f32[2,24,128]{2,1,0:T(8,128)S(1)}, f32[2,24,128]{2,1,0:T(8,128)S(1)}, u32[]{:S(2)}, u32[]{:S(2)}) %collective-permute-start.3) | collective-permute-done | bytes 24608 | tf_op jit(solution)/shard_map/ppermute | solution.py:245
  19.5 0.6 add_add_fusion
  20.1 0.7 pad_maximum_fusion.1
  20.8 0.7 broadcast_in_dim.31.gain
  21.5 0.9 broadcast_in_dim.32.refs_9_
  22.5 0.4 dynamic-slice_reduce_fusion
  22.9 0.1 reshape.26
  23.0 0.1 reshape.27
  23.1 0.7 maximum_maximum_fusion.first_w
  23.8 0.7 convolution_convert_fusion
  24.5 0.9 dynamic-slice_bitcast_fusion
  25.4 6.2 %collective-permute-start.6 = (bf16[4,2,3,96,128]{4,3,2,1,0:T(8,128)(2,1)}, bf16[4,2,3,96,128]{4,3,2,1,0:T(8,128)(2,1)S(1)}, u32[]{:S(2)}, u32[]{:S(2)}) collective-permute-start(bf16[4,2,3,96,128]{4,3,2,1,0:T(8,128)(2,1)} %dynamic-slice_bitcast_fusion), channel_id=1, source_target_pairs={{0,8},{8,0},{1,9},{9,1},{2,10},{10,2},{3,11},{11,3},{4,12},{12,4},... | collective-permute-start | bytes 1769480 | tf_op jit(solution)/shard_map/ppermute | solution.py:278
  31.7 1.0 pad_maximum_fusion.left
  32.7 0.7 maximum_maximum_fusion.1.second_w
  33.3 0.5 collective-permute-done.7
  33.8 0.1 collective-permute-start.8
  34.0 0.2 collective-permute-start.5
  34.1 22.7 %collective-permute-done.8.partner = f32[2,2,24,128]{3,2,1,0:T(8,128)S(1)} collective-permute-done((f32[2,2,24,128]{3,2,1,0:T(8,128)S(1)}, f32[2,2,24,128]{3,2,1,0:T(8,128)S(1)}, u32[]{:S(2)}, u32[]{:S(2)}) %collective-permute-start.8) | collective-permute-done | bytes 49184 | tf_op jit(solution)/shard_map/ppermute | solution.py:282
  56.9 0.1 collective-permute-start.9
  57.0 0.7 copy-done.1
  57.7 0.9 collective-permute-done.9.across
  58.6 1.1 copy-done.2
  59.6 1.0 copy-done.5
  60.7 0.8 copy-done.6
  61.5 2.2 %shard_map.109 = (bf16[32,16,1152]{2,1,0:T(8,128)(2,1)S(1)}, f32[1152,512]{1,0:T(8,128)S(1)}) custom-call(s32[3]{0:T(128)S(1)} %pad_add_fusion.at, bf16[4,2,3,2,96,128]{5,4,3,2,1,0:T(8,128)(2,1)S(1)} %bitcast.50, bf16[4,3,96,128]{3,2,1,0:T(8,128)(2,1)S(1)} %collective-permute-done.5.near, bf16[4,2,3,96,128]{4,3,2,1,0:T(8,128)(2,1)S(1)} %copy-done.2, ...), custom_call_target="tpu_custom_call" | custom-call | flops 603979776 | bytes 6569984 | tf_op jit(solution)/shard_map/pallas_call | solution.py:33
  63.7 35.9 %all_to_all.10.columns = bf16[32,16,1152]{2,1,0:T(8,128)(2,1)S(1)} all-to-all(bf16[32,16,1152]{2,1,0:T(8,128)(2,1)S(1)} %get-tuple-element.42), channel_id=1, replica_groups=mesh['lat'=16,'zh'=2,'co'=2,'ch'=4] {'lat','co'}, dimensions={0} | all-to-all | bytes 2359296 | tf_op jit(solution)/shard_map/all_to_all | solution.py:317
  99.6 4.8 %shard_map.110 = bf16[32,16,1152]{2,1,0:T(8,128)(2,1)S(1)} custom-call(s32[3]{0:T(128)S(1)} %pad_add_fusion.at, bf16[32,16,1152]{2,1,0:T(8,128)(2,1)S(1)} %all_to_all.10.columns, bf16[576,768]{1,0:T(8,128)(2,1)S(1)} %copy-done.3, bf16[256,256]{1,0:T(8,128)(2,1)S(1)} %copy-done.7, bf16[256,256]{1,0:T(8,128)(2,1)S(1)} %copy-done.8), custom_call_target="tpu_custom_call" | custom-call | flops 1811939328 | bytes 3506176 | tf_op jit(solution)/shard_map/pallas_call | solution.py:33
  104.4 22.5 %all_to_all.11 = bf16[32,16,1152]{2,1,0:T(8,128)(2,1)S(1)} all-to-all(bf16[32,16,1152]{2,1,0:T(8,128)(2,1)S(1)} %shard_map.110), channel_id=1, replica_groups=mesh['lat'=16,'zh'=2,'co'=2,'ch'=4] {'lat','co'}, dimensions={0} | all-to-all | bytes 2359296 | tf_op jit(solution)/shard_map/all_to_all | solution.py:332
  126.9 1.0 copy-done.4
  127.9 1.6 shard_map.111
  129.5 0.6 collective-permute-start.10
  130.1 2.8 %collective-permute-start.11 = (bf16[2,3,96,128]{3,2,1,0:T(8,128)(2,1)S(1)}, bf16[2,3,96,128]{3,2,1,0:T(8,128)(2,1)S(1)}, u32[]{:S(2)}, u32[]{:S(2)}) collective-permute-start(bf16[2,3,96,128]{3,2,1,0:T(8,128)(2,1)S(1)} %get-tuple-element.51), channel_id=1, source_target_pairs={{0,1},{1,2},{2,3},{3,8},{8,9},{9,10},{10,11},{11,0},{4,5},{5,6},{6... | collective-permute-start | bytes 442376 | tf_op jit(solution)/shard_map/ppermute | solution.py:245
  132.8 4.1 %collective-permute-start.13 = (bf16[2,3,96,128]{3,2,1,0:T(8,128)(2,1)S(1)}, bf16[2,3,96,128]{3,2,1,0:T(8,128)(2,1)S(1)}, u32[]{:S(2)}, u32[]{:S(2)}) collective-permute-start(bf16[2,3,96,128]{3,2,1,0:T(8,128)(2,1)S(1)} %get-tuple-element.53), channel_id=1, source_target_pairs={{0,2},{1,3},{2,8},{3,9},{8,10},{9,11},{10,0},{11,1},{4,6},{5,7},{6... | collective-permute-start | bytes 442376 | tf_op jit(solution)/shard_map/ppermute | solution.py:245
  137.0 0.7 collective-permute-done.10.refs_1_
  137.7 4.3 %collective-permute-start.15 = (bf16[2,3,96,128]{3,2,1,0:T(8,128)(2,1)S(1)}, bf16[2,3,96,128]{3,2,1,0:T(8,128)(2,1)S(1)}, u32[]{:S(2)}, u32[]{:S(2)}) collective-permute-start(bf16[2,3,96,128]{3,2,1,0:T(8,128)(2,1)S(1)} %get-tuple-element.55), channel_id=1, source_target_pairs={{0,3},{1,8},{2,9},{3,10},{8,11},{9,0},{10,1},{11,2},{4,7},{5,12},{... | collective-permute-start | bytes 442376 | tf_op jit(solution)/shard_map/ppermute | solution.py:245
  142.1 3.1 %collective-permute-start.16 = (bf16[2,3,96,128]{3,2,1,0:T(8,128)(2,1)S(1)}, bf16[2,3,96,128]{3,2,1,0:T(8,128)(2,1)S(1)}, u32[]{:S(2)}, u32[]{:S(2)}) collective-permute-start(bf16[2,3,96,128]{3,2,1,0:T(8,128)(2,1)S(1)} %get-tuple-element.56), channel_id=1, source_target_pairs={{0,8},{1,9},{2,10},{3,11},{8,0},{9,1},{10,2},{11,3},{4,12},{5,13},... | collective-permute-start | bytes 442376 | tf_op jit(solution)/shard_map/ppermute | solution.py:245
  145.2 0.2 collective-permute-done.12.refs_3_
  145.4 0.1 collective-permute-done.13.refs_4_
  145.6 11.1 %collective-permute-done.14.refs_5_ = bf16[2,3,96,128]{3,2,1,0:T(8,128)(2,1)S(1)} collective-permute-done((bf16[2,3,96,128]{3,2,1,0:T(8,128)(2,1)S(1)}, bf16[2,3,96,128]{3,2,1,0:T(8,128)(2,1)S(1)}, u32[]{:S(2)}, u32[]{:S(2)}) %collective-permute-start.14) | collective-permute-done | bytes 147488 | tf_op jit(solution)/shard_map/ppermute | solution.py:245
  156.7 1.4 collective-permute-done.15.refs_6_
  158.2 0.3 collective-permute-start.17
  158.5 2.0 collective-permute-done.17.refs_8_
  160.5 0.8 copy-done.26
  161.3 13.4 %shard_map.112 = (bf16[6,192,128]{2,1,0:T(8,128)(2,1)}, bf16[6,192,128]{2,1,0:T(8,128)(2,1)}, bf16[6,192,128]{2,1,0:T(8,128)(2,1)}, bf16[6,192,128]{2,1,0:T(8,128)(2,1)}) custom-call(s32[2]{0:T(128)} %copy-done.10, bf16[2,3,96,128]{3,2,1,0:T(8,128)(2,1)} %copy-done.9, bf16[2,3,96,128]{3,2,1,0:T(8,128)(2,1)} %copy-done.15, ...), custom_call_target="tpu_custom_call" | custom-call | flops 7247757312 | bytes 9437184 | tf_op jit(solution)/shard_map/pallas_call | solution.py:354
  174.7 1.8 collective-permute-start.18
  176.5 4.0 %collective-permute-start.19 = (bf16[6,192,128]{2,1,0:T(8,128)(2,1)}, bf16[6,192,128]{2,1,0:T(8,128)(2,1)S(1)}, u32[]{:S(2)}, u32[]{:S(2)}) collective-permute-start(bf16[6,192,128]{2,1,0:T(8,128)(2,1)} %get-tuple-element.61), channel_id=1, source_target_pairs={{0,2},{1,3},{2,0},{3,1},{4,6},{5,7},{6,4},{7,5},{8,10},{9,11},{10,... | collective-permute-start | bytes 884744 | tf_op jit(solution)/shard_map/ppermute | solution.py:245
  180.5 0.3 collective-permute-start.20
  180.8 0.2 broadcast_in_dim.30
  181.1 5.5 %collective-permute-done.18 = bf16[6,192,128]{2,1,0:T(8,128)(2,1)S(1)} collective-permute-done((bf16[6,192,128]{2,1,0:T(8,128)(2,1)}, bf16[6,192,128]{2,1,0:T(8,128)(2,1)S(1)}, u32[]{:S(2)}, u32[]{:S(2)}) %collective-permute-start.18) | collective-permute-done | bytes 294944 | tf_op jit(solution)/shard_map/ppermute | solution.py:245
  186.6 20.1 %collective-permute-done.19 = bf16[6,192,128]{2,1,0:T(8,128)(2,1)S(1)} collective-permute-done((bf16[6,192,128]{2,1,0:T(8,128)(2,1)}, bf16[6,192,128]{2,1,0:T(8,128)(2,1)S(1)}, u32[]{:S(2)}, u32[]{:S(2)}) %collective-permute-start.19) | collective-permute-done | bytes 294944 | tf_op jit(solution)/shard_map/ppermute | solution.py:245
  206.8 1.0 copy-done.12
  (85 shorter events, 0.6 us)
Async XLA Ops:
  6.5 3.6 %copy-start = (bf16[24,192,128]{2,1,0:T(8,128)(2,1)S(1)}, bf16[24,192,128]{2,1,0:T(8,128)(2,1)}, u32[]{:S(2)}) copy-start(bf16[24,192,128]{2,1,0:T(8,128)(2,1)} %param.11) | copy-start | bytes 3538948
  6.5 120.3 %all-gather.3.cloned.1.call-start = ((), (), s32[]{:S(2)}) async-start(), calls=%async_computation.2 | async-start | bytes 9732096 | tf_op jit(solution)/shard_map/all_gather | solution.py:276
  7.9 5.4 %copy-start.27 = (f32[192]{0:T(256)S(1)}, f32[192]{0:T(256)}, u32[]{:S(2)}) copy-start(f32[192]{0:T(256)} %param.12) | copy-start | bytes 2308
  8.2 13.3 %copy-start.24 = (f32[768]{0:T(1024)S(1)}, f32[768]{0:T(1024)}, u32[]{:S(2)}) copy-start(f32[768]{0:T(1024)} %param.16) | copy-start | bytes 9220
  8.2 14.2 %copy-start.22 = (f32[2,18432]{1,0:T(2,128)S(1)}, f32[2,18432]{1,0:T(2,128)}, u32[]{:S(2)}) copy-start(f32[2,18432]{1,0:T(2,128)} %param.14) | copy-start | bytes 442372
  8.3 14.2 %copy-start.23 = (f32[2,18432]{1,0:T(2,128)S(1)}, f32[2,18432]{1,0:T(2,128)}, u32[]{:S(2)}) copy-start(f32[2,18432]{1,0:T(2,128)} %param.13) | copy-start | bytes 442372
  8.3 11.8 %collective-permute-start = (bf16[2,48,768]{2,1,0:T(8,128)(2,1)S(1)}, bf16[2,48,768]{2,1,0:T(8,128)(2,1)S(1)}, u32[]{:S(2)}, u32[]{:S(2)}) collective-permute-start(bf16[2,48,768]{2,1,0:T(8,128)(2,1)S(1)} %pad_maximum_fusion.2), channel_id=1, source_target_pairs={{0,0},{1,1},{2,2},{3,3},{4,6},{5,7},{6,4},{7,5},{8,8},{9,9},{10,10... | collective-permute-start | bytes 442376 | tf_op jit(solution)/shard_map/ppermute | solution.py:255
  9.1 11.0 %collective-permute-start.1 = (bf16[2,48,768]{2,1,0:T(8,128)(2,1)S(1)}, bf16[2,48,768]{2,1,0:T(8,128)(2,1)S(1)}, u32[]{:S(2)}, u32[]{:S(2)}) collective-permute-start(bf16[2,48,768]{2,1,0:T(8,128)(2,1)S(1)} %pad_maximum_fusion.2), channel_id=1, source_target_pairs={{0,1},{1,2},{2,3},{3,0},{4,7},{5,4},{6,5},{7,6},{8,9},{9,10},{10,1... | collective-permute-start | bytes 442376 | tf_op jit(solution)/shard_map/ppermute | solution.py:255
  10.5 4.4 %collective-permute-start.2 = (f32[2,24,128]{2,1,0:T(8,128)S(1)}, f32[2,24,128]{2,1,0:T(8,128)S(1)}, u32[]{:S(2)}, u32[]{:S(2)}) collective-permute-start(f32[2,24,128]{2,1,0:T(8,128)S(1)} %pad_maximum_fusion.4), channel_id=1, source_target_pairs={{0,1},{1,2},{2,3},{3,0},{4,5},{5,6},{6,7},{7,4},{8,9},{9,10},{10,1... | collective-permute-start | bytes 73736 | tf_op jit(solution)/shard_map/ppermute | solution.py:245
  10.7 8.7 %collective-permute-start.3 = (f32[2,24,128]{2,1,0:T(8,128)S(1)}, f32[2,24,128]{2,1,0:T(8,128)S(1)}, u32[]{:S(2)}, u32[]{:S(2)}) collective-permute-start(f32[2,24,128]{2,1,0:T(8,128)S(1)} %pad_maximum_fusion.4), channel_id=1, source_target_pairs={{0,2},{1,3},{2,0},{3,1},{4,6},{5,7},{6,4},{7,5},{8,10},{9,11},{10,... | collective-permute-start | bytes 73736 | tf_op jit(solution)/shard_map/ppermute | solution.py:245
  13.1 6.4 %collective-permute-start.4 = (f32[2,24,128]{2,1,0:T(8,128)S(1)}, f32[2,24,128]{2,1,0:T(8,128)S(1)}, u32[]{:S(2)}, u32[]{:S(2)}) collective-permute-start(f32[2,24,128]{2,1,0:T(8,128)S(1)} %pad_maximum_fusion.4), channel_id=1, source_target_pairs={{0,3},{1,0},{2,1},{3,2},{4,7},{5,4},{6,5},{7,6},{8,11},{9,8},{10,9... | collective-permute-start | bytes 73736 | tf_op jit(solution)/shard_map/ppermute | solution.py:245
  13.3 113.6 %copy-start.10 = (s32[2]{0:T(128)}, s32[2]{0:T(128)S(1)}, u32[]{:S(2)}) copy-start(s32[2]{0:T(128)S(1)} %pad_add_fusion.1.at) | copy-start | bytes 28
  20.8 3.0 %copy-start.11 = (bf16[384,1536]{1,0:T(8,128)(2,1)S(1)}, bf16[384,1536]{1,0:T(8,128)(2,1)}, u32[]{:S(2)}) copy-start(bf16[384,1536]{1,0:T(8,128)(2,1)} %constant.136.clone) | copy-start | bytes 3538948
  20.8 3.0 %copy-start.25 = (s32[288]{0:T(512)S(1)}, s32[288]{0:T(512)}, u32[]{:S(2)}) copy-start(s32[288]{0:T(512)} %param.15) | copy-start | bytes 3460
  25.4 7.2 %copy-start.14 = (f32[2,24,128]{2,1,0:T(8,128)S(1)}, f32[2,24,128]{2,1,0:T(8,128)}, u32[]{:S(2)}) copy-start(f32[2,24,128]{2,1,0:T(8,128)} %add_add_fusion) | copy-start | bytes 73732
  25.4 31.4 %collective-permute-start.6 = (bf16[4,2,3,96,128]{4,3,2,1,0:T(8,128)(2,1)}, bf16[4,2,3,96,128]{4,3,2,1,0:T(8,128)(2,1)S(1)}, u32[]{:S(2)}, u32[]{:S(2)}) collective-permute-start(bf16[4,2,3,96,128]{4,3,2,1,0:T(8,128)(2,1)} %dynamic-slice_bitcast_fusion), channel_id=1, source_target_pairs={{0,8},{8,0},{1,9},{9,1},{2,10},{10,2},{3,11},{11,3},{4,12},{12,4},... | collective-permute-start | bytes 1769480 | tf_op jit(solution)/shard_map/ppermute | solution.py:278
  32.6 1.2 collective-permute-start.7
  33.8 23.0 %collective-permute-start.8 = (f32[2,2,24,128]{3,2,1,0:T(8,128)S(1)}, f32[2,2,24,128]{3,2,1,0:T(8,128)S(1)}, u32[]{:S(2)}, u32[]{:S(2)}) collective-permute-start(f32[2,2,24,128]{3,2,1,0:T(8,128)S(1)} %pad_maximum_fusion.3.chip), channel_id=1, source_target_pairs={{0,8},{8,0},{1,9},{9,1},{2,10},{10,2},{3,11},{11,3},{4,12},{12,4},... | collective-permute-start | bytes 147464 | tf_op jit(solution)/shard_map/ppermute | solution.py:282
  34.0 23.0 %collective-permute-start.5 = (bf16[4,3,96,128]{3,2,1,0:T(8,128)(2,1)S(1)}, bf16[4,3,96,128]{3,2,1,0:T(8,128)(2,1)S(1)}, u32[]{:S(2)}, u32[]{:S(2)}) collective-permute-start(bf16[4,3,96,128]{3,2,1,0:T(8,128)(2,1)S(1)} %dynamic-slice_bitcast_fusion.2), channel_id=1, source_target_pairs={{0,4},{4,0},{1,5},{5,1},{2,6},{6,2},{3,7},{7,3},{8,12},{12,8},{9,1... | collective-permute-start | bytes 884744 | tf_op jit(solution)/shard_map/ppermute | solution.py:297
  56.9 0.8 copy-start.1
  56.9 1.7 collective-permute-start.9
  58.6 1.1 copy-start.2
  59.6 1.0 copy-start.5
  60.7 0.8 copy-start.6
  63.7 35.9 %copy-start.3 = (bf16[576,768]{1,0:T(8,128)(2,1)S(1)}, bf16[576,768]{1,0:T(8,128)(2,1)}, u32[]{:S(2)}) copy-start(bf16[576,768]{1,0:T(8,128)(2,1)} %pad_maximum_fusion.left) | copy-start | bytes 2654212
  63.7 35.9 %copy-start.7 = (bf16[256,256]{1,0:T(8,128)(2,1)S(1)}, bf16[256,256]{1,0:T(8,128)(2,1)}, u32[]{:S(2)}) copy-start(bf16[256,256]{1,0:T(8,128)(2,1)} %maximum_maximum_fusion.first_w) | copy-start | bytes 393220
  63.7 35.9 %copy-start.8 = (bf16[256,256]{1,0:T(8,128)(2,1)S(1)}, bf16[256,256]{1,0:T(8,128)(2,1)}, u32[]{:S(2)}) copy-start(bf16[256,256]{1,0:T(8,128)(2,1)} %maximum_maximum_fusion.1.second_w) | copy-start | bytes 393220
  126.9 1.0 copy-start.4
  129.5 31.0 %copy-start.9 = (bf16[2,3,96,128]{3,2,1,0:T(8,128)(2,1)}, bf16[2,3,96,128]{3,2,1,0:T(8,128)(2,1)S(1)}, u32[]{:S(2)}) copy-start(bf16[2,3,96,128]{3,2,1,0:T(8,128)(2,1)S(1)} %get-tuple-element.49.refs_0_) | copy-start | bytes 442372
  129.5 8.2 %collective-permute-start.10 = (bf16[2,3,96,128]{3,2,1,0:T(8,128)(2,1)S(1)}, bf16[2,3,96,128]{3,2,1,0:T(8,128)(2,1)S(1)}, u32[]{:S(2)}, u32[]{:S(2)}) collective-permute-start(bf16[2,3,96,128]{3,2,1,0:T(8,128)(2,1)S(1)} %get-tuple-element.50), channel_id=1, source_target_pairs={{0,11},{1,0},{2,1},{3,2},{8,3},{9,8},{10,9},{11,10},{4,15},{5,4},{... | collective-permute-start | bytes 442376 | tf_op jit(solution)/shard_map/ppermute | solution.py:245
  130.1 12.0 %collective-permute-start.11 = (bf16[2,3,96,128]{3,2,1,0:T(8,128)(2,1)S(1)}, bf16[2,3,96,128]{3,2,1,0:T(8,128)(2,1)S(1)}, u32[]{:S(2)}, u32[]{:S(2)}) collective-permute-start(bf16[2,3,96,128]{3,2,1,0:T(8,128)(2,1)S(1)} %get-tuple-element.51), channel_id=1, source_target_pairs={{0,1},{1,2},{2,3},{3,8},{8,9},{9,10},{10,11},{11,0},{4,5},{5,6},{6... | collective-permute-start | bytes 442376 | tf_op jit(solution)/shard_map/ppermute | solution.py:245
  132.8 12.6 %collective-permute-start.12 = (bf16[2,3,96,128]{3,2,1,0:T(8,128)(2,1)S(1)}, bf16[2,3,96,128]{3,2,1,0:T(8,128)(2,1)S(1)}, u32[]{:S(2)}, u32[]{:S(2)}) collective-permute-start(bf16[2,3,96,128]{3,2,1,0:T(8,128)(2,1)S(1)} %get-tuple-element.52), channel_id=1, source_target_pairs={{0,10},{1,11},{2,0},{3,1},{8,2},{9,3},{10,8},{11,9},{4,14},{5,15},... | collective-permute-start | bytes 442376 | tf_op jit(solution)/shard_map/ppermute | solution.py:245
  132.8 12.7 %collective-permute-start.13 = (bf16[2,3,96,128]{3,2,1,0:T(8,128)(2,1)S(1)}, bf16[2,3,96,128]{3,2,1,0:T(8,128)(2,1)S(1)}, u32[]{:S(2)}, u32[]{:S(2)}) collective-permute-start(bf16[2,3,96,128]{3,2,1,0:T(8,128)(2,1)S(1)} %get-tuple-element.53), channel_id=1, source_target_pairs={{0,2},{1,3},{2,8},{3,9},{8,10},{9,11},{10,0},{11,1},{4,6},{5,7},{6... | collective-permute-start | bytes 442376 | tf_op jit(solution)/shard_map/ppermute | solution.py:245
  137.0 19.7 %collective-permute-start.14 = (bf16[2,3,96,128]{3,2,1,0:T(8,128)(2,1)S(1)}, bf16[2,3,96,128]{3,2,1,0:T(8,128)(2,1)S(1)}, u32[]{:S(2)}, u32[]{:S(2)}) collective-permute-start(bf16[2,3,96,128]{3,2,1,0:T(8,128)(2,1)S(1)} %get-tuple-element.54), channel_id=1, source_target_pairs={{0,9},{1,10},{2,11},{3,0},{8,1},{9,2},{10,3},{11,8},{4,13},{5,14},... | collective-permute-start | bytes 442376 | tf_op jit(solution)/shard_map/ppermute | solution.py:245
  137.7 22.8 %copy-start.15 = (bf16[2,3,96,128]{3,2,1,0:T(8,128)(2,1)}, bf16[2,3,96,128]{3,2,1,0:T(8,128)(2,1)S(1)}, u32[]{:S(2)}) copy-start(bf16[2,3,96,128]{3,2,1,0:T(8,128)(2,1)S(1)} %collective-permute-done.10.refs_1_) | copy-start | bytes 442372
  137.7 20.4 %collective-permute-start.15 = (bf16[2,3,96,128]{3,2,1,0:T(8,128)(2,1)S(1)}, bf16[2,3,96,128]{3,2,1,0:T(8,128)(2,1)S(1)}, u32[]{:S(2)}, u32[]{:S(2)}) collective-permute-start(bf16[2,3,96,128]{3,2,1,0:T(8,128)(2,1)S(1)} %get-tuple-element.55), channel_id=1, source_target_pairs={{0,3},{1,8},{2,9},{3,10},{8,11},{9,0},{10,1},{11,2},{4,7},{5,12},{... | collective-permute-start | bytes 442376 | tf_op jit(solution)/shard_map/ppermute | solution.py:245
  142.0 18.5 %copy-start.16 = (bf16[2,3,96,128]{3,2,1,0:T(8,128)(2,1)}, bf16[2,3,96,128]{3,2,1,0:T(8,128)(2,1)S(1)}, u32[]{:S(2)}) copy-start(bf16[2,3,96,128]{3,2,1,0:T(8,128)(2,1)S(1)} %collective-permute-done.11.refs_2_) | copy-start | bytes 442372
  142.1 16.1 %collective-permute-start.16 = (bf16[2,3,96,128]{3,2,1,0:T(8,128)(2,1)S(1)}, bf16[2,3,96,128]{3,2,1,0:T(8,128)(2,1)S(1)}, u32[]{:S(2)}, u32[]{:S(2)}) collective-permute-start(bf16[2,3,96,128]{3,2,1,0:T(8,128)(2,1)S(1)} %get-tuple-element.56), channel_id=1, source_target_pairs={{0,8},{1,9},{2,10},{3,11},{8,0},{9,1},{10,2},{11,3},{4,12},{5,13},... | collective-permute-start | bytes 442376 | tf_op jit(solution)/shard_map/ppermute | solution.py:245
  145.4 15.1 %copy-start.17 = (bf16[2,3,96,128]{3,2,1,0:T(8,128)(2,1)}, bf16[2,3,96,128]{3,2,1,0:T(8,128)(2,1)S(1)}, u32[]{:S(2)}) copy-start(bf16[2,3,96,128]{3,2,1,0:T(8,128)(2,1)S(1)} %collective-permute-done.12.refs_3_) | copy-start | bytes 442372
  145.6 14.9 %copy-start.18 = (bf16[2,3,96,128]{3,2,1,0:T(8,128)(2,1)}, bf16[2,3,96,128]{3,2,1,0:T(8,128)(2,1)S(1)}, u32[]{:S(2)}) copy-start(bf16[2,3,96,128]{3,2,1,0:T(8,128)(2,1)S(1)} %collective-permute-done.13.refs_4_) | copy-start | bytes 442372
  156.7 3.8 %copy-start.19 = (bf16[2,3,96,128]{3,2,1,0:T(8,128)(2,1)}, bf16[2,3,96,128]{3,2,1,0:T(8,128)(2,1)S(1)}, u32[]{:S(2)}) copy-start(bf16[2,3,96,128]{3,2,1,0:T(8,128)(2,1)S(1)} %collective-permute-done.14.refs_5_) | copy-start | bytes 442372
  158.1 2.4 %copy-start.20 = (bf16[2,3,96,128]{3,2,1,0:T(8,128)(2,1)}, bf16[2,3,96,128]{3,2,1,0:T(8,128)(2,1)S(1)}, u32[]{:S(2)}) copy-start(bf16[2,3,96,128]{3,2,1,0:T(8,128)(2,1)S(1)} %collective-permute-done.15.refs_6_) | copy-start | bytes 442372
  158.1 2.4 %copy-start.21 = (bf16[2,3,96,128]{3,2,1,0:T(8,128)(2,1)}, bf16[2,3,96,128]{3,2,1,0:T(8,128)(2,1)S(1)}, u32[]{:S(2)}) copy-start(bf16[2,3,96,128]{3,2,1,0:T(8,128)(2,1)S(1)} %collective-permute-done.16.refs_7_) | copy-start | bytes 442372
  158.2 2.3 %collective-permute-start.17 = (bf16[8,3,96,128]{3,2,1,0:T(8,128)(2,1)S(1)}, bf16[8,3,96,128]{3,2,1,0:T(8,128)(2,1)S(1)}, u32[]{:S(2)}, u32[]{:S(2)}) collective-permute-start(bf16[8,3,96,128]{3,2,1,0:T(8,128)(2,1)S(1)} %dynamic-slice_dynamic-update-slice_fusion), channel_id=1, source_target_pairs={{0,4},{4,0},{1,5},{5,1},{2,6},{6,2},{3,7},{7,3},{8,12},{12,8},{9,1... | collective-permute-start | bytes 1769480 | tf_op jit(solution)/shard_map/ppermute | solution.py:350
  160.5 0.8 copy-start.26
  174.7 6.3 %copy-start.13 = (bf16[6,192,128]{2,1,0:T(8,128)(2,1)S(1)}, bf16[6,192,128]{2,1,0:T(8,128)(2,1)}, u32[]{:S(2)}) copy-start(bf16[6,192,128]{2,1,0:T(8,128)(2,1)} %get-tuple-element.59) | copy-start | bytes 884740
  174.7 11.9 %collective-permute-start.18 = (bf16[6,192,128]{2,1,0:T(8,128)(2,1)}, bf16[6,192,128]{2,1,0:T(8,128)(2,1)S(1)}, u32[]{:S(2)}, u32[]{:S(2)}) collective-permute-start(bf16[6,192,128]{2,1,0:T(8,128)(2,1)} %get-tuple-element.60), channel_id=1, source_target_pairs={{0,1},{1,2},{2,3},{3,0},{4,5},{5,6},{6,7},{7,4},{8,9},{9,10},{10,1... | collective-permute-start | bytes 884744 | tf_op jit(solution)/shard_map/ppermute | solution.py:245
  176.5 30.2 %collective-permute-start.19 = (bf16[6,192,128]{2,1,0:T(8,128)(2,1)}, bf16[6,192,128]{2,1,0:T(8,128)(2,1)S(1)}, u32[]{:S(2)}, u32[]{:S(2)}) collective-permute-start(bf16[6,192,128]{2,1,0:T(8,128)(2,1)} %get-tuple-element.61), channel_id=1, source_target_pairs={{0,2},{1,3},{2,0},{3,1},{4,6},{5,7},{6,4},{7,5},{8,10},{9,11},{10,... | collective-permute-start | bytes 884744 | tf_op jit(solution)/shard_map/ppermute | solution.py:245
  180.5 26.2 %collective-permute-start.20 = (bf16[6,192,128]{2,1,0:T(8,128)(2,1)}, bf16[6,192,128]{2,1,0:T(8,128)(2,1)S(1)}, u32[]{:S(2)}, u32[]{:S(2)}) collective-permute-start(bf16[6,192,128]{2,1,0:T(8,128)(2,1)} %get-tuple-element.62), channel_id=1, source_target_pairs={{0,3},{1,0},{2,1},{3,2},{4,7},{5,4},{6,5},{7,6},{8,11},{9,8},{10,9... | collective-permute-start | bytes 884744 | tf_op jit(solution)/shard_map/ppermute | solution.py:245
  206.8 1.0 copy-start.12
Sparse Core Ops, SparseCore 0:
  22.6 76.2 all-gather.2

commit v4 on v3

--- a/solution.py
+++ b/solution.py
@@ -78,53 +78,53 @@
     ).astype(BF16)
 
 
-def strips(at, own, near, far, across):
-    core, high, lon = at[0], at[1], at[2]
-    trip = near.shape[1]
-    parts = (
-        lambda c, t: own[c, core, t, high],
-        lambda c, t: near[c, t],
-        lambda c, t: far[c, core, t],
-        lambda c, t: across[c, t],
-    )
-    for d, part in enumerate(parts):
-        lanes = pl.ds(pl.multiple_of((lon ^ d) * LANES, LANES), LANES)
-        for r in range(near.shape[0] * trip):
-            yield r, lanes, part(r // trip, r % trip).astype(F32)
-
-
-def forward_kernel(full, at, own, near, far, across, chip, partner, gain, table, *refs):
+def forward_kernel(full, start, at, own, near, far, across, chip, partner, gain, table, *refs):
     spec, base, normed, mean, scale = refs
     for d in range(4):
         stats = (chip if d < 2 else partner)[d % 2] / full
         mean[d] = stats[0]
         scale[d] = lax.rsqrt(stats[1] - stats[0] * stats[0] + EPSILON)
-    count, trip = near.shape[0] * near.shape[1], near.shape[1]
-    for i, (r, lanes, values) in enumerate(strips(at, own, near, far, across)):
-        d = i // count
-        low = r + (r // trip) * trip
-        picked = []
-        for ref in (mean, scale):
-            rows = ref[d, low : low + 1], ref[d, low + trip : low + trip + 1]
-            picked.append(jnp.where(at[0] == 0, *rows))
-        value = ((values - picked[0]) * picked[1] * gain[...]).astype(BF16)
-        rows = slice(r * BS, (r + 1) * BS)
-        normed[rows, lanes] = value
-        base[rows, lanes] = values + value.astype(F32)
+    core, high, lon = at[0], at[1], at[2]
+    trip, count = own.shape[2], near.shape[1]
+    parts = (
+        lambda c, t: own[c, core, start + t, high],
+        lambda c, t: near[c, t],
+        lambda c, t: far[c, core, t],
+        lambda c, t: across[c, t],
+    )
+    for d, part in enumerate(parts):
+        lanes = pl.ds(pl.multiple_of((lon ^ d) * LANES, LANES), LANES)
+        for c in range(near.shape[0]):
+            for t in range(count):
+                low = 2 * c * trip + start + t
+                picked = []
+                for ref in (mean, scale):
+                    rows = ref[d, low : low + 1], ref[d, low + trip : low + trip + 1]
+                    picked.append(jnp.where(core == 0, *rows))
+                values = part(c, t).astype(F32)
+                value = ((values - picked[0]) * picked[1] * gain[...]).astype(BF16)
+                rows = slice((c * count + t) * BS, (c * count + t + 1) * BS)
+                normed[rows, lanes] = value
+                base[rows, lanes] = values + value.astype(F32)
     result = dot(table[...], normed[...], ((1,), (1,)))
     spec[...] = result.astype(BF16).reshape(spec.shape)
 
 
-def middle_kernel(at, columns, left, first_w, second_w, out, wide, stacked, mid):
-    srcs, pairs, inner = columns.shape
+def middle_kernel(parts, at, *refs):
+    columns, (left, first_w, second_w) = refs[:parts], refs[parts : parts + 3]
+    out, wide, stacked, mid = refs[parts + 3 :]
+    srcs, pairs, inner = out.shape
     modes = pairs // 2
     local = inner // BS
     height = srcs * local
     kept = left.shape[0] // 2
     tiles = inner // LANES
-    for j in range(tiles):
-        part = columns[:, :, j * LANES : (j + 1) * LANES]
-        wide[j] = part.reshape(srcs * pairs, LANES).astype(F32)
+    j = 0
+    for column in columns:
+        for k in range(column.shape[2] // LANES):
+            part = column[:, :, k * LANES : (k + 1) * LANES]
+            wide[j] = part.reshape(srcs * pairs, LANES).astype(F32)
+            j += 1
     blank = jnp.zeros((srcs, LANES), F32)
     for t in range(2):
         for k in range(modes):
@@ -165,20 +165,26 @@
         out[:, :, j * LANES : (j + 1) * LANES] = part
 
 
-def inverse_kernel(at, returned, table, base, *refs):
-    outs, first = refs[:-1], refs[-1]
+def inverse_kernel(chunks, at, returned, table, *refs):
+    bases, outs, first = refs[: len(chunks)], refs[len(chunks) : -1], refs[-1]
     field = dot(returned[...], table[...], ((0,), (0,))).astype(BF16).astype(F32)
-    first[...] = (base[...] + field).astype(BF16)
+    ahead = 0
+    for base in bases:
+        size = base.shape[0]
+        first[ahead : ahead + size] = (base[...] + field[ahead : ahead + size]).astype(BF16)
+        ahead += size
     count = len(outs)
     cores, trip = outs[0].shape[0], outs[0].shape[1]
     groups = first.shape[0] // (trip * BS)
     for d, out in enumerate(outs):
         place = lax.rem(at[0] + d, count)
         high, low = place // groups, lax.rem(place, groups)
-        rows = pl.ds(pl.multiple_of(low * (trip * BS), trip * BS), trip * BS)
-        for c in range(cores):
-            lanes = pl.ds(pl.multiple_of((high * cores + c) * LANES, LANES), LANES)
-            out[c] = first[rows, lanes].reshape(trip, BS, LANES)
+        for start, many in chunks:
+            row = start * groups * BS + low * (many * BS)
+            rows = pl.ds(pl.multiple_of(row, BS), many * BS)
+            for c in range(cores):
+                lanes = pl.ds(pl.multiple_of((high * cores + c) * LANES, LANES), LANES)
+                out[c, start : start + many] = first[rows, lanes].reshape(many, BS, LANES)
 
 
 def token_kernel(order, at, *refs):
@@ -275,53 +281,68 @@
     )
     weights = lax.all_gather(pieces, ("lat", "co"))
     own = sent.reshape(ch_n, co_n, trip, zh_n, BS, cols)
-    far = lax.ppermute(
-        lax.dynamic_index_in_dim(own, 1 - zh, axis=3, keepdims=False), "zh", swap
-    )
+    chunks = ((0, 1), (1, trip - 1))
+    sizes = [ch_n * count * BS for _, count in chunks]
+
+    def to_far(array, chunk):
+        array = lax.slice_in_dim(array, chunk[0], chunk[0] + chunk[1], axis=2)
+        return lax.ppermute(
+            lax.dynamic_index_in_dim(array, 1 - zh, axis=3, keepdims=False), "zh", swap
+        )
+
+    def to_near(array):
+        return lax.ppermute(
+            lax.dynamic_index_in_dim(array, 1 - co, axis=1, keepdims=False), "co", swap
+        )
+
+    far = to_far(own, chunks[0])
     chip_sums = jnp.stack([sums, lax.ppermute(sums, "co", swap)])
     partner_sums = lax.ppermute(chip_sums, "zh", swap)
-    order = np.arange(height).reshape(lat_n, ch_n, co_n, trip).transpose(1, 3, 0, 2).reshape(-1)
+    order = np.arange(height).reshape(lat_n, ch_n, co_n, trip).transpose(1, 3, 0, 2)
+    order = np.concatenate([order[:, a : a + n].reshape(-1) for a, n in chunks])
     left = lat_table(kept_lat, height, order)
     kept = kept_lat.shape[0]
     first_w = mode_weight(lax.dynamic_index_in_dim(mode_first, zh, axis=0, keepdims=False))
     second_w = mode_weight(lax.dynamic_index_in_dim(mode_second, zh, axis=0, keepdims=False))
-    (far, chip_sums, partner_sums), tables = lax.optimization_barrier(
-        (
-            (far, chip_sums, partner_sums),
-            (left, first_w, second_w),
+    (far, chip_sums, partner_sums, own), tables = lax.optimization_barrier(
+        ((far, chip_sums, partner_sums, own), (left, first_w, second_w))
+    )
+    left, first_w, second_w = tables
+    fars = [far, to_far(own, chunks[1])]
+
+    forward, inverse = lon_tables(width, dests)
+    forward = jnp.asarray(forward, BF16)
+    wide_n = half * BS
+    columns, bases = [], []
+    for chunk, size, far in zip(chunks, sizes, fars):
+        near = lax.slice_in_dim(own, chunk[0], chunk[0] + chunk[1], axis=2)
+        near = to_near(lax.dynamic_index_in_dim(near, zh, axis=3, keepdims=False))
+        spec, base = call(
+            functools.partial(forward_kernel, float(full), chunk[0]),
+            place,
+            (own, near, far, to_near(far), chip_sums, partner_sums, block_gain, forward),
+            (
+                jax.ShapeDtypeStruct((dests, 2 * KW // dests, size), BF16),
+                jax.ShapeDtypeStruct((size, width), F32),
+            ),
+            [
+                pltpu.VMEM((size, width), BF16),
+                pltpu.VMEM((lon_n, rows, cols), F32),
+                pltpu.VMEM((lon_n, rows, cols), F32),
+            ],
+            4 * KW * width * size,
         )
-    )
-    left, first_w, second_w = tables
-    near = lax.dynamic_index_in_dim(own, zh, axis=3, keepdims=False)
-    near = lax.dynamic_index_in_dim(near, 1 - co, axis=1, keepdims=False)
-    near = lax.ppermute(near, "co", swap)
-    across = lax.dynamic_index_in_dim(far, 1 - co, axis=1, keepdims=False)
-    across = lax.ppermute(across, "co", swap)
-    forward, inverse = lon_tables(width, dests)
-    wide_n = half * BS
-    spec, base = call(
-        functools.partial(forward_kernel, float(full)),
-        place,
-        (own, near, far, across, chip_sums, partner_sums, block_gain, jnp.asarray(forward, BF16)),
-        (
-            jax.ShapeDtypeStruct((dests, 2 * KW // dests, wide_n), BF16),
-            jax.ShapeDtypeStruct((wide_n, width), F32),
-        ),
-        [
-            pltpu.VMEM((wide_n, width), BF16),
-            pltpu.VMEM((lon_n, rows, cols), F32),
-            pltpu.VMEM((lon_n, rows, cols), F32),
-        ],
-        4 * KW * width * wide_n,
-    )
-    columns = lax.all_to_all(spec, ("lat", "co"), split_axis=0, concat_axis=0, tiled=True)
+        columns.append(
+            lax.all_to_all(spec, ("lat", "co"), split_axis=0, concat_axis=0, tiled=True)
+        )
+        bases.append(base)
 
     modes = KW // dests
     (back,) = call(
-        middle_kernel,
+        functools.partial(middle_kernel, len(columns)),
         place,
-        (columns, left, first_w, second_w),
-        (jax.ShapeDtypeStruct(columns.shape, BF16),),
+        (*columns, left, first_w, second_w),
+        (jax.ShapeDtypeStruct((dests, 2 * modes, wide_n), BF16),),
         [
             pltpu.VMEM((wide_n // LANES, dests * 2 * modes, LANES), F32),
             pltpu.VMEM((2 * height, modes * LANES), BF16),
@@ -334,9 +355,9 @@
     returned, weights = lax.optimization_barrier((returned, weights))
     weights = weights.reshape(lat_n, co_n, ch_n // co_n, 2, piece_n, full)
     firsts = call(
-        inverse_kernel,
+        functools.partial(inverse_kernel, chunks),
         column,
-        (returned.reshape(2 * KW, wide_n), jnp.asarray(inverse, BF16), base),
+        (returned.reshape(2 * KW, wide_n), jnp.asarray(inverse, BF16), *bases),
         tuple(jax.ShapeDtypeStruct((co_n, trip, BS, cols), BF16) for _ in range(z_n)),
         [pltpu.VMEM((wide_n, width), BF16)],
         4 * KW * width * wide_n,

time: 215 us -> 214 us (level)
  starting transfers between devices: 32.4 us -> 45.9 us
  blocking collectives: 58.4 us -> 45.2 us
  waiting for transfers between devices: 71.3 us -> 66.9 us
  Pallas kernels: 21.9 us -> 24.3 us
    ppermute x1, waiting for transfers between devices: 22.7 us -> 6.58 us  [on_device(): partner_sums = lax.ppermute(chip_sums, 'zh', swap)]
    all_to_all x1, blocking collectives: 35.9 us -> 23 us  [on_device(): lax.all_to_all(spec, ('lat', 'co'), split_axis=0, concat_axis=0, tiled=True)]
    ppermute x3 -> x6, starting transfers between devices: 6.48 us -> 14.8 us  [the longest x2 13.5 us: to_far(): lax.ppermute(lax.dynamic_index_in_dim(array, 1 - zh, axis=3, keepdims=Fal...]
    all_to_all x0 -> x1, waiting for transfers between devices: none -> 8.35 us  [on_device(): lax.all_to_all(spec, ('lat', 'co'), split_axis=0, concat_axis=0, tiled=True)]
    all_to_all x0 -> x1, starting transfers between devices: none -> 7.45 us  [on_device(): lax.all_to_all(spec, ('lat', 'co'), split_axis=0, concat_axis=0, tiled=True)]
    ppermute x13, starting transfers between devices: 23.7 us -> 19.6 us  [ring(): lax.ppermute(array, axes, [(i, (i + step) % count) for i in range(count)])]
    pallas_call x3 -> x4, Pallas kernels: 8.53 us -> 10.9 us  [call(): pl.pallas_call(kernel, grid_spec=pltpu.PrefetchScalarGridSpec(num_scalar_...]
    ppermute x13, waiting for transfers between devices: 45.2 us -> 47.4 us  [ring(): lax.ppermute(array, axes, [(i, (i + step) % count) for i in range(count)])]
  transfers between devices with their start and end apart: 22 -> 26, of which waited for: 13 -> 16; matrix products, arithmetic and copies ran while one was open for 3% -> 3% of each run, Pallas kernels for 3% -> 4%
where the time goes in v4:
time: 214 us; the launch traced here: 213 us
  waiting for transfers between devices  66.9 us (31%)
  starting transfers between devices  45.9 us (21%)
  blocking collectives  45.2 us (21%)
  Pallas kernels  24.3 us (11%)
  between operations  14 us (7%)
  local copies, waits for them, and re-layouts  11.3 us (5%)
  other arithmetic  3.47 us (2%)
    ppermute x13, waiting for transfers between devices, ring(): lax.ppermute(array, axes, [(i, (i + step) % count) for i in range(count)])  47.4 us
    all_to_all x1, blocking collectives, on_device(): lax.all_to_all(spec, ('lat', 'co'), split_axis=0, concat_axis=0, tiled=True)  23 us
    all_to_all x1, blocking collectives, on_device(): lax.all_to_all(back, ('lat', 'co'), split_axis=0, concat_axis=0, tiled=True)  22.3 us
    ppermute x13, starting transfers between devices, ring(): lax.ppermute(array, axes, [(i, (i + step) % count) for i in range(count)])  19.6 us
    ppermute x2, starting transfers between devices, to_far(): lax.ppermute(lax.dynamic_index_in_dim(array, 1 - zh, axis=3, keepdims=Fal...  13.5 us
    pallas_call x1, Pallas kernels, on_device(): pl.pallas_call(functools.partial(token_kernel, order), grid_spec=pltpu.Pr...  13.3 us
    pallas_call x4, Pallas kernels, call(): pl.pallas_call(kernel, grid_spec=pltpu.PrefetchScalarGridSpec(num_scalar_...  10.9 us
    all_to_all x1, waiting for transfers between devices, on_device(): lax.all_to_all(spec, ('lat', 'co'), split_axis=0, concat_axis=0, tiled=True)  8.35 us
  transfers between devices with their start and end apart: 26, of which 16 were waited for; matrix products, arithmetic and copies ran while one was open for 3% of the time, Pallas kernels for 4%

profile of v4, /device:TPU:96, one launch (start us, length us, event | category | flops | bytes accessed | tf_op | source)
XLA Modules:
  0.0 213.0 jit_solution(13234755303735161914)
XLA Ops:
  6.5 1.4 constant_dynamic-slice_fusion
  7.9 0.1 copy.15
  8.1 0.1 copy.16
  8.3 0.8 collective-permute-start
  9.1 1.0 collective-permute-start.1
  10.1 0.3 convert_reduce_fusion
  10.5 0.3 collective-permute-start.2
  10.7 2.4 %collective-permute-start.3 = (f32[2,24,128]{2,1,0:T(8,128)S(1)}, f32[2,24,128]{2,1,0:T(8,128)S(1)}, u32[]{:S(2)}, u32[]{:S(2)}) collective-permute-start(f32[2,24,128]{2,1,0:T(8,128)S(1)} %pad_maximum_fusion.4), channel_id=1, source_target_pairs={{0,2},{1,3},{2,0},{3,1},{4,6},{5,7},{6,4},{7,5},{8,10},{9,11},{10,... | collective-permute-start | bytes 73736 | tf_op jit(solution)/shard_map/ppermute | solution.py:251
  13.1 0.1 collective-permute-start.4
  13.2 0.6 pad_add_fusion.1.at
  13.9 0.9 collective-permute-done.2
  14.8 4.6 %collective-permute-done.3 = f32[2,24,128]{2,1,0:T(8,128)S(1)} collective-permute-done((f32[2,24,128]{2,1,0:T(8,128)S(1)}, f32[2,24,128]{2,1,0:T(8,128)S(1)}, u32[]{:S(2)}, u32[]{:S(2)}) %collective-permute-start.3) | collective-permute-done | bytes 24608 | tf_op jit(solution)/shard_map/ppermute | solution.py:251
  19.5 0.8 pad_maximum_fusion.1
  20.3 0.9 broadcast_in_dim.32.refs_9_
  21.3 0.4 dynamic-slice_reduce_fusion
  22.0 1.9 convolution_convert_fusion
  24.0 1.0 pad_maximum_fusion.refs_2_
  25.0 1.0 collective-permute-start.6
  26.1 5.5 %collective-permute-start.5 = (bf16[4,2,1,96,128]{4,3,2,1,0:T(8,128)(2,1)S(1)}, bf16[4,2,1,96,128]{4,3,2,1,0:T(8,128)(2,1)S(1)}, u32[]{:S(2)}, u32[]{:S(2)}) collective-permute-start(bf16[4,2,1,96,128]{4,3,2,1,0:T(8,128)(2,1)S(1)} %dynamic-slice_bitcast_fusion.3), channel_id=1, source_target_pairs={{0,8},{8,0},{1,9},{9,1},{2,10},{10,2},{3,11},{11,3},{4,12},{12,4},... | collective-permute-start | bytes 589832 | tf_op jit(solution)/shard_map/ppermute | solution.py:289
  31.6 0.8 collective-permute-start.7
  32.4 0.7 maximum_maximum_fusion.1.refs_4_
  33.1 6.6 %collective-permute-done.7.partner = f32[2,2,24,128]{3,2,1,0:T(8,128)S(1)} collective-permute-done((f32[2,2,24,128]{3,2,1,0:T(8,128)S(1)}, f32[2,2,24,128]{3,2,1,0:T(8,128)S(1)}, u32[]{:S(2)}, u32[]{:S(2)}) %collective-permute-start.7) | collective-permute-done | bytes 49184 | tf_op jit(solution)/shard_map/ppermute | solution.py:300
  39.8 0.8 dynamic-slice_bitcast_fusion
  40.6 8.0 %collective-permute-start.11 = (bf16[4,2,2,96,128]{4,3,2,1,0:T(8,128)(2,1)}, bf16[4,2,2,96,128]{4,3,2,1,0:T(8,128)(2,1)S(1)}, u32[]{:S(2)}, u32[]{:S(2)}) collective-permute-start(bf16[4,2,2,96,128]{4,3,2,1,0:T(8,128)(2,1)} %dynamic-slice_bitcast_fusion), channel_id=1, source_target_pairs={{0,8},{8,0},{1,9},{9,1},{2,10},{10,2},{3,11},{11,3},{4,12},{12,4},... | collective-permute-start | bytes 1179656 | tf_op jit(solution)/shard_map/ppermute | solution.py:289
  48.7 0.6 collective-permute-start.9
  49.3 0.7 collective-permute-done.8.near
  50.0 0.2 collective-permute-done.9.across
  50.2 2.0 shard_map.109
  52.3 0.9 copy-done.5
  53.2 7.4 %all-to-all-start = ((bf16[32,16,384]{2,1,0:T(8,128)(2,1)}), bf16[32,16,384]{2,1,0:T(8,128)(2,1)}, u32[]{:S(2)}, u32[]{:S(2)}) async-start(bf16[32,16,384]{2,1,0:T(8,128)(2,1)} %get-tuple-element.46), calls=%async_computation | async-start | bytes 786432 | tf_op jit(solution)/shard_map/all_to_all | solution.py:336
  60.7 0.3 collective-permute-start.10
  61.0 0.4 collective-permute-start.12
  61.4 1.1 collective-permute-done.10.near
  62.5 0.6 collective-permute-done.12.across
  63.0 1.0 copy-done.4
  64.0 0.6 copy-done.12
  64.7 1.6 shard_map.110
  66.3 0.9 copy-done.7
  67.2 8.3 %all-to-all-done.refs_0_ = bf16[32,16,384]{2,1,0:T(8,128)(2,1)} async-done(((bf16[32,16,384]{2,1,0:T(8,128)(2,1)}), bf16[32,16,384]{2,1,0:T(8,128)(2,1)}, u32[]{:S(2)}, u32[]{:S(2)}) %all-to-all-start) | async-done | bytes 393248 | tf_op jit(solution)/shard_map/all_to_all | solution.py:336
  75.5 23.0 %all_to_all.15.refs_1_ = bf16[32,16,768]{2,1,0:T(8,128)(2,1)S(1)} all-to-all(bf16[32,16,768]{2,1,0:T(8,128)(2,1)} %copy-done.7), channel_id=1, replica_groups=mesh['lat'=16,'zh'=2,'co'=2,'ch'=4] {'lat','co'}, dimensions={0} | all-to-all | bytes 1572864 | tf_op jit(solution)/shard_map/all_to_all | solution.py:336
  98.5 5.7 %shard_map.111 = bf16[32,16,1152]{2,1,0:T(8,128)(2,1)S(1)} custom-call(s32[3]{0:T(128)S(1)} %copy-done.13, bf16[32,16,384]{2,1,0:T(8,128)(2,1)} %all-to-all-done.refs_0_, bf16[32,16,768]{2,1,0:T(8,128)(2,1)S(1)} %all_to_all.15.refs_1_, bf16[576,768]{1,0:T(8,128)(2,1)S(1)} %copy-done.2, bf16[256,256]{1,0:T(8,128)(2,1)S(1)} %maximum_maximum_fusion.refs_3_, ...), custom_call_target="tpu_custom_call" | custom-call | flops 1811939328 | bytes 3506176 | tf_op jit(solution)/shard_map/pallas_call | solution.py:33
  104.3 22.3 %all_to_all.16 = bf16[32,16,1152]{2,1,0:T(8,128)(2,1)S(1)} all-to-all(bf16[32,16,1152]{2,1,0:T(8,128)(2,1)S(1)} %shard_map.111), channel_id=1, replica_groups=mesh['lat'=16,'zh'=2,'co'=2,'ch'=4] {'lat','co'}, dimensions={0} | all-to-all | bytes 2359296 | tf_op jit(solution)/shard_map/all_to_all | solution.py:353
  126.5 1.1 copy-done.6
  127.6 1.6 shard_map.112
  129.2 0.6 collective-permute-start.13
  129.8 2.7 %collective-permute-start.14 = (bf16[2,3,96,128]{3,2,1,0:T(8,128)(2,1)S(1)}, bf16[2,3,96,128]{3,2,1,0:T(8,128)(2,1)S(1)}, u32[]{:S(2)}, u32[]{:S(2)}) collective-permute-start(bf16[2,3,96,128]{3,2,1,0:T(8,128)(2,1)S(1)} %get-tuple-element.57), channel_id=1, source_target_pairs={{0,1},{1,2},{2,3},{3,8},{8,9},{9,10},{10,11},{11,0},{4,5},{5,6},{6... | collective-permute-start | bytes 442376 | tf_op jit(solution)/shard_map/ppermute | solution.py:251
  132.6 4.1 %collective-permute-start.16 = (bf16[2,3,96,128]{3,2,1,0:T(8,128)(2,1)S(1)}, bf16[2,3,96,128]{3,2,1,0:T(8,128)(2,1)S(1)}, u32[]{:S(2)}, u32[]{:S(2)}) collective-permute-start(bf16[2,3,96,128]{3,2,1,0:T(8,128)(2,1)S(1)} %get-tuple-element.59), channel_id=1, source_target_pairs={{0,2},{1,3},{2,8},{3,9},{8,10},{9,11},{10,0},{11,1},{4,6},{5,7},{6... | collective-permute-start | bytes 442376 | tf_op jit(solution)/shard_map/ppermute | solution.py:251
  136.7 0.9 collective-permute-done.13.refs_1_
  137.6 4.2 %collective-permute-start.18 = (bf16[2,3,96,128]{3,2,1,0:T(8,128)(2,1)S(1)}, bf16[2,3,96,128]{3,2,1,0:T(8,128)(2,1)S(1)}, u32[]{:S(2)}, u32[]{:S(2)}) collective-permute-start(bf16[2,3,96,128]{3,2,1,0:T(8,128)(2,1)S(1)} %get-tuple-element.61), channel_id=1, source_target_pairs={{0,3},{1,8},{2,9},{3,10},{8,11},{9,0},{10,1},{11,2},{4,7},{5,12},{... | collective-permute-start | bytes 442376 | tf_op jit(solution)/shard_map/ppermute | solution.py:251
  141.8 0.1 collective-permute-start.19
  141.9 3.2 %collective-permute-done.15.refs_3_ = bf16[2,3,96,128]{3,2,1,0:T(8,128)(2,1)S(1)} collective-permute-done((bf16[2,3,96,128]{3,2,1,0:T(8,128)(2,1)S(1)}, bf16[2,3,96,128]{3,2,1,0:T(8,128)(2,1)S(1)}, u32[]{:S(2)}, u32[]{:S(2)}) %collective-permute-start.15) | collective-permute-done | bytes 147488 | tf_op jit(solution)/shard_map/ppermute | solution.py:251
  145.1 1.5 collective-permute-done.16.refs_4_
  146.6 7.8 %collective-permute-done.17.refs_5_ = bf16[2,3,96,128]{3,2,1,0:T(8,128)(2,1)S(1)} collective-permute-done((bf16[2,3,96,128]{3,2,1,0:T(8,128)(2,1)S(1)}, bf16[2,3,96,128]{3,2,1,0:T(8,128)(2,1)S(1)}, u32[]{:S(2)}, u32[]{:S(2)}) %collective-permute-start.17) | collective-permute-done | bytes 147488 | tf_op jit(solution)/shard_map/ppermute | solution.py:251
  154.4 3.4 %collective-permute-done.18.refs_6_ = bf16[2,3,96,128]{3,2,1,0:T(8,128)(2,1)S(1)} collective-permute-done((bf16[2,3,96,128]{3,2,1,0:T(8,128)(2,1)S(1)}, bf16[2,3,96,128]{3,2,1,0:T(8,128)(2,1)S(1)}, u32[]{:S(2)}, u32[]{:S(2)}) %collective-permute-start.18) | collective-permute-done | bytes 147488 | tf_op jit(solution)/shard_map/ppermute | solution.py:251
  157.9 0.3 collective-permute-start.20
  158.2 2.0 collective-permute-done.20.refs_8_
  160.2 0.8 copy-done.28
  161.0 13.3 %shard_map.113 = (bf16[6,192,128]{2,1,0:T(8,128)(2,1)}, bf16[6,192,128]{2,1,0:T(8,128)(2,1)}, bf16[6,192,128]{2,1,0:T(8,128)(2,1)}, bf16[6,192,128]{2,1,0:T(8,128)(2,1)}) custom-call(s32[2]{0:T(128)} %pad_add_fusion.1.at, bf16[2,3,96,128]{3,2,1,0:T(8,128)(2,1)} %copy-done.10, bf16[2,3,96,128]{3,2,1,0:T(8,128)(2,1)} %copy-done.17, ...), custom_call_target="tpu_custom_call" | custom-call | flops 7247757312 | bytes 9437184 | tf_op jit(solution)/shard_map/pallas_call | solution.py:375
  174.5 4.4 %collective-permute-start.22 = (bf16[6,192,128]{2,1,0:T(8,128)(2,1)}, bf16[6,192,128]{2,1,0:T(8,128)(2,1)S(1)}, u32[]{:S(2)}, u32[]{:S(2)}) collective-permute-start(bf16[6,192,128]{2,1,0:T(8,128)(2,1)} %get-tuple-element.67), channel_id=1, source_target_pairs={{0,2},{1,3},{2,0},{3,1},{4,6},{5,7},{6,4},{7,5},{8,10},{9,11},{10,... | collective-permute-start | bytes 884744 | tf_op jit(solution)/shard_map/ppermute | solution.py:251
  178.9 0.7 collective-permute-start.23
  179.6 0.2 broadcast_in_dim.30
  179.9 5.1 %collective-permute-done.21 = bf16[6,192,128]{2,1,0:T(8,128)(2,1)S(1)} collective-permute-done((bf16[6,192,128]{2,1,0:T(8,128)(2,1)}, bf16[6,192,128]{2,1,0:T(8,128)(2,1)S(1)}, u32[]{:S(2)}, u32[]{:S(2)}) %collective-permute-start.21) | collective-permute-done | bytes 294944 | tf_op jit(solution)/shard_map/ppermute | solution.py:251
  185.0 20.1 %collective-permute-done.22 = bf16[6,192,128]{2,1,0:T(8,128)(2,1)S(1)} collective-permute-done((bf16[6,192,128]{2,1,0:T(8,128)(2,1)}, bf16[6,192,128]{2,1,0:T(8,128)(2,1)S(1)}, u32[]{:S(2)}, u32[]{:S(2)}) %collective-permute-start.22) | collective-permute-done | bytes 294944 | tf_op jit(solution)/shard_map/ppermute | solution.py:251
  205.2 1.0 copy-done.15
  (104 shorter events, 1.4 us)
Async XLA Ops:
  6.5 3.6 %copy-start = (bf16[24,192,128]{2,1,0:T(8,128)(2,1)S(1)}, bf16[24,192,128]{2,1,0:T(8,128)(2,1)}, u32[]{:S(2)}) copy-start(bf16[24,192,128]{2,1,0:T(8,128)(2,1)} %param.11) | copy-start | bytes 3538948
  6.5 120.0 %all-gather.3.cloned.1.call-start = ((), (), s32[]{:S(2)}) async-start(), calls=%async_computation.3 | async-start | bytes 9732096 | tf_op jit(solution)/shard_map/all_gather | solution.py:282
  7.9 5.9 %copy-start.29 = (f32[192]{0:T(256)S(1)}, f32[192]{0:T(256)}, u32[]{:S(2)}) copy-start(f32[192]{0:T(256)} %param.12) | copy-start | bytes 2308
  8.2 12.1 %copy-start.26 = (f32[768]{0:T(1024)S(1)}, f32[768]{0:T(1024)}, u32[]{:S(2)}) copy-start(f32[768]{0:T(1024)} %param.16) | copy-start | bytes 9220
  8.2 13.0 %copy-start.24 = (f32[2,18432]{1,0:T(2,128)S(1)}, f32[2,18432]{1,0:T(2,128)}, u32[]{:S(2)}) copy-start(f32[2,18432]{1,0:T(2,128)} %param.14) | copy-start | bytes 442372
  8.3 13.0 %copy-start.25 = (f32[2,18432]{1,0:T(2,128)S(1)}, f32[2,18432]{1,0:T(2,128)}, u32[]{:S(2)}) copy-start(f32[2,18432]{1,0:T(2,128)} %param.13) | copy-start | bytes 442372
  8.3 11.2 %collective-permute-start = (bf16[2,48,768]{2,1,0:T(8,128)(2,1)S(1)}, bf16[2,48,768]{2,1,0:T(8,128)(2,1)S(1)}, u32[]{:S(2)}, u32[]{:S(2)}) collective-permute-start(bf16[2,48,768]{2,1,0:T(8,128)(2,1)S(1)} %pad_maximum_fusion.2), channel_id=1, source_target_pairs={{0,0},{1,1},{2,2},{3,3},{4,6},{5,7},{6,4},{7,5},{8,8},{9,9},{10,10... | collective-permute-start | bytes 442376 | tf_op jit(solution)/shard_map/ppermute | solution.py:261
  9.1 10.4 %collective-permute-start.1 = (bf16[2,48,768]{2,1,0:T(8,128)(2,1)S(1)}, bf16[2,48,768]{2,1,0:T(8,128)(2,1)S(1)}, u32[]{:S(2)}, u32[]{:S(2)}) collective-permute-start(bf16[2,48,768]{2,1,0:T(8,128)(2,1)S(1)} %pad_maximum_fusion.2), channel_id=1, source_target_pairs={{0,1},{1,2},{2,3},{3,0},{4,7},{5,4},{6,5},{7,6},{8,9},{9,10},{10,1... | collective-permute-start | bytes 442376 | tf_op jit(solution)/shard_map/ppermute | solution.py:261
  10.5 4.4 %collective-permute-start.2 = (f32[2,24,128]{2,1,0:T(8,128)S(1)}, f32[2,24,128]{2,1,0:T(8,128)S(1)}, u32[]{:S(2)}, u32[]{:S(2)}) collective-permute-start(f32[2,24,128]{2,1,0:T(8,128)S(1)} %pad_maximum_fusion.4), channel_id=1, source_target_pairs={{0,1},{1,2},{2,3},{3,0},{4,5},{5,6},{6,7},{7,4},{8,9},{9,10},{10,1... | collective-permute-start | bytes 73736 | tf_op jit(solution)/shard_map/ppermute | solution.py:251
  10.7 8.7 %collective-permute-start.3 = (f32[2,24,128]{2,1,0:T(8,128)S(1)}, f32[2,24,128]{2,1,0:T(8,128)S(1)}, u32[]{:S(2)}, u32[]{:S(2)}) collective-permute-start(f32[2,24,128]{2,1,0:T(8,128)S(1)} %pad_maximum_fusion.4), channel_id=1, source_target_pairs={{0,2},{1,3},{2,0},{3,1},{4,6},{5,7},{6,4},{7,5},{8,10},{9,11},{10,... | collective-permute-start | bytes 73736 | tf_op jit(solution)/shard_map/ppermute | solution.py:251
  13.1 6.4 %collective-permute-start.4 = (f32[2,24,128]{2,1,0:T(8,128)S(1)}, f32[2,24,128]{2,1,0:T(8,128)S(1)}, u32[]{:S(2)}, u32[]{:S(2)}) collective-permute-start(f32[2,24,128]{2,1,0:T(8,128)S(1)} %pad_maximum_fusion.4), channel_id=1, source_target_pairs={{0,3},{1,0},{2,1},{3,2},{4,7},{5,4},{6,5},{7,6},{8,11},{9,8},{10,9... | collective-permute-start | bytes 73736 | tf_op jit(solution)/shard_map/ppermute | solution.py:251
  13.8 36.4 %copy-start.11 = (s32[3]{0:T(128)}, s32[3]{0:T(128)S(1)}, u32[]{:S(2)}) copy-start(s32[3]{0:T(128)S(1)} %pad_add_fusion.at) | copy-start | bytes 40
  20.3 1.7 copy-start.27
  25.0 6.6 %collective-permute-start.6 = (f32[2,24,128]{2,1,0:T(8,128)S(1)}, f32[2,24,128]{2,1,0:T(8,128)S(1)}, u32[]{:S(2)}, u32[]{:S(2)}) collective-permute-start(f32[2,24,128]{2,1,0:T(8,128)S(1)} %add_add_fusion), channel_id=1, source_target_pairs={{0,4},{4,0},{1,5},{5,1},{2,6},{6,2},{3,7},{7,3},{8,12},{12,8},{9,1... | collective-permute-start | bytes 73736 | tf_op jit(solution)/shard_map/ppermute | solution.py:299
  26.1 13.6 %collective-permute-start.5 = (bf16[4,2,1,96,128]{4,3,2,1,0:T(8,128)(2,1)S(1)}, bf16[4,2,1,96,128]{4,3,2,1,0:T(8,128)(2,1)S(1)}, u32[]{:S(2)}, u32[]{:S(2)}) collective-permute-start(bf16[4,2,1,96,128]{4,3,2,1,0:T(8,128)(2,1)S(1)} %dynamic-slice_bitcast_fusion.3), channel_id=1, source_target_pairs={{0,8},{8,0},{1,9},{9,1},{2,10},{10,2},{3,11},{11,3},{4,12},{12,4},... | collective-permute-start | bytes 589832 | tf_op jit(solution)/shard_map/ppermute | solution.py:289
  31.6 8.1 %collective-permute-start.7 = (f32[2,2,24,128]{3,2,1,0:T(8,128)S(1)}, f32[2,2,24,128]{3,2,1,0:T(8,128)S(1)}, u32[]{:S(2)}, u32[]{:S(2)}) collective-permute-start(f32[2,2,24,128]{3,2,1,0:T(8,128)S(1)} %pad_maximum_fusion.3.chip), channel_id=1, source_target_pairs={{0,8},{8,0},{1,9},{9,1},{2,10},{10,2},{3,11},{11,3},{4,12},{12,4},... | collective-permute-start | bytes 147464 | tf_op jit(solution)/shard_map/ppermute | solution.py:300
  39.7 10.5 %copy-start.1 = (bf16[512,512]{1,0:T(8,128)(2,1)S(1)}, bf16[512,512]{1,0:T(8,128)(2,1)}, u32[]{:S(2)}) copy-start(bf16[512,512]{1,0:T(8,128)(2,1)} %constant.177.clone.table) | copy-start | bytes 1572868
  40.6 20.4 %collective-permute-start.11 = (bf16[4,2,2,96,128]{4,3,2,1,0:T(8,128)(2,1)}, bf16[4,2,2,96,128]{4,3,2,1,0:T(8,128)(2,1)S(1)}, u32[]{:S(2)}, u32[]{:S(2)}) collective-permute-start(bf16[4,2,2,96,128]{4,3,2,1,0:T(8,128)(2,1)} %dynamic-slice_bitcast_fusion), channel_id=1, source_target_pairs={{0,8},{8,0},{1,9},{9,1},{2,10},{10,2},{3,11},{11,3},{4,12},{12,4},... | collective-permute-start | bytes 1179656 | tf_op jit(solution)/shard_map/ppermute | solution.py:289
  48.6 1.4 collective-permute-start.8
  48.7 1.5 collective-permute-start.9
  52.3 0.9 copy-start.5
  53.2 22.4 %all-to-all-start = ((bf16[32,16,384]{2,1,0:T(8,128)(2,1)}), bf16[32,16,384]{2,1,0:T(8,128)(2,1)}, u32[]{:S(2)}, u32[]{:S(2)}) async-start(bf16[32,16,384]{2,1,0:T(8,128)(2,1)} %get-tuple-element.46), calls=%async_computation | async-start | bytes 786432 | tf_op jit(solution)/shard_map/all_to_all | solution.py:336
  60.7 1.8 collective-permute-start.10
  61.0 1.5 copy-start.3
  61.0 2.0 collective-permute-start.12
  63.0 1.0 copy-start.4
  64.0 0.6 copy-start.12
  66.3 0.9 copy-start.7
  67.2 31.3 %copy-start.2 = (bf16[576,768]{1,0:T(8,128)(2,1)S(1)}, bf16[576,768]{1,0:T(8,128)(2,1)}, u32[]{:S(2)}) copy-start(bf16[576,768]{1,0:T(8,128)(2,1)} %pad_maximum_fusion.refs_2_) | copy-start | bytes 2654212
  67.2 31.3 %copy-start.9 = (bf16[256,256]{1,0:T(8,128)(2,1)S(1)}, bf16[256,256]{1,0:T(8,128)(2,1)}, u32[]{:S(2)}) copy-start(bf16[256,256]{1,0:T(8,128)(2,1)} %maximum_maximum_fusion.1.refs_4_) | copy-start | bytes 393220
  67.2 31.3 %copy-start.13 = (s32[3]{0:T(128)S(1)}, s32[3]{0:T(128)}, u32[]{:S(2)}) copy-start(s32[3]{0:T(128)} %copy-done.11) | copy-start | bytes 40
  104.2 22.3 %copy-start.8 = (bf16[512,512]{1,0:T(8,128)(2,1)S(1)}, bf16[512,512]{1,0:T(8,128)(2,1)}, u32[]{:S(2)}) copy-start(bf16[512,512]{1,0:T(8,128)(2,1)} %constant.178.clone.table) | copy-start | bytes 1572868
  104.2 22.3 %copy-start.14 = (s32[2]{0:T(128)S(1)}, s32[2]{0:T(128)}, u32[]{:S(2)}) copy-start(s32[2]{0:T(128)} %pad_add_fusion.1.at) | copy-start | bytes 28
  126.5 1.1 copy-start.6
  129.2 30.9 %copy-start.10 = (bf16[2,3,96,128]{3,2,1,0:T(8,128)(2,1)}, bf16[2,3,96,128]{3,2,1,0:T(8,128)(2,1)S(1)}, u32[]{:S(2)}) copy-start(bf16[2,3,96,128]{3,2,1,0:T(8,128)(2,1)S(1)} %get-tuple-element.55.refs_0_) | copy-start | bytes 442372
  129.2 8.3 %collective-permute-start.13 = (bf16[2,3,96,128]{3,2,1,0:T(8,128)(2,1)S(1)}, bf16[2,3,96,128]{3,2,1,0:T(8,128)(2,1)S(1)}, u32[]{:S(2)}, u32[]{:S(2)}) collective-permute-start(bf16[2,3,96,128]{3,2,1,0:T(8,128)(2,1)S(1)} %get-tuple-element.56), channel_id=1, source_target_pairs={{0,11},{1,0},{2,1},{3,2},{8,3},{9,8},{10,9},{11,10},{4,15},{5,4},{... | collective-permute-start | bytes 442376 | tf_op jit(solution)/shard_map/ppermute | solution.py:251
  129.8 11.9 %collective-permute-start.14 = (bf16[2,3,96,128]{3,2,1,0:T(8,128)(2,1)S(1)}, bf16[2,3,96,128]{3,2,1,0:T(8,128)(2,1)S(1)}, u32[]{:S(2)}, u32[]{:S(2)}) collective-permute-start(bf16[2,3,96,128]{3,2,1,0:T(8,128)(2,1)S(1)} %get-tuple-element.57), channel_id=1, source_target_pairs={{0,1},{1,2},{2,3},{3,8},{8,9},{9,10},{10,11},{11,0},{4,5},{5,6},{6... | collective-permute-start | bytes 442376 | tf_op jit(solution)/shard_map/ppermute | solution.py:251
  132.6 12.5 %collective-permute-start.15 = (bf16[2,3,96,128]{3,2,1,0:T(8,128)(2,1)S(1)}, bf16[2,3,96,128]{3,2,1,0:T(8,128)(2,1)S(1)}, u32[]{:S(2)}, u32[]{:S(2)}) collective-permute-start(bf16[2,3,96,128]{3,2,1,0:T(8,128)(2,1)S(1)} %get-tuple-element.58), channel_id=1, source_target_pairs={{0,10},{1,11},{2,0},{3,1},{8,2},{9,3},{10,8},{11,9},{4,14},{5,15},... | collective-permute-start | bytes 442376 | tf_op jit(solution)/shard_map/ppermute | solution.py:251
  132.6 14.0 %collective-permute-start.16 = (bf16[2,3,96,128]{3,2,1,0:T(8,128)(2,1)S(1)}, bf16[2,3,96,128]{3,2,1,0:T(8,128)(2,1)S(1)}, u32[]{:S(2)}, u32[]{:S(2)}) collective-permute-start(bf16[2,3,96,128]{3,2,1,0:T(8,128)(2,1)S(1)} %get-tuple-element.59), channel_id=1, source_target_pairs={{0,2},{1,3},{2,8},{3,9},{8,10},{9,11},{10,0},{11,1},{4,6},{5,7},{6... | collective-permute-start | bytes 442376 | tf_op jit(solution)/shard_map/ppermute | solution.py:251
  136.7 17.7 %collective-permute-start.17 = (bf16[2,3,96,128]{3,2,1,0:T(8,128)(2,1)S(1)}, bf16[2,3,96,128]{3,2,1,0:T(8,128)(2,1)S(1)}, u32[]{:S(2)}, u32[]{:S(2)}) collective-permute-start(bf16[2,3,96,128]{3,2,1,0:T(8,128)(2,1)S(1)} %get-tuple-element.60), channel_id=1, source_target_pairs={{0,9},{1,10},{2,11},{3,0},{8,1},{9,2},{10,3},{11,8},{4,13},{5,14},... | collective-permute-start | bytes 442376 | tf_op jit(solution)/shard_map/ppermute | solution.py:251
  137.6 22.6 %copy-start.17 = (bf16[2,3,96,128]{3,2,1,0:T(8,128)(2,1)}, bf16[2,3,96,128]{3,2,1,0:T(8,128)(2,1)S(1)}, u32[]{:S(2)}) copy-start(bf16[2,3,96,128]{3,2,1,0:T(8,128)(2,1)S(1)} %collective-permute-done.13.refs_1_) | copy-start | bytes 442372
  137.6 20.2 %collective-permute-start.18 = (bf16[2,3,96,128]{3,2,1,0:T(8,128)(2,1)S(1)}, bf16[2,3,96,128]{3,2,1,0:T(8,128)(2,1)S(1)}, u32[]{:S(2)}, u32[]{:S(2)}) collective-permute-start(bf16[2,3,96,128]{3,2,1,0:T(8,128)(2,1)S(1)} %get-tuple-element.61), channel_id=1, source_target_pairs={{0,3},{1,8},{2,9},{3,10},{8,11},{9,0},{10,1},{11,2},{4,7},{5,12},{... | collective-permute-start | bytes 442376 | tf_op jit(solution)/shard_map/ppermute | solution.py:251
  141.8 18.4 %copy-start.18 = (bf16[2,3,96,128]{3,2,1,0:T(8,128)(2,1)}, bf16[2,3,96,128]{3,2,1,0:T(8,128)(2,1)S(1)}, u32[]{:S(2)}) copy-start(bf16[2,3,96,128]{3,2,1,0:T(8,128)(2,1)S(1)} %collective-permute-done.14.refs_2_) | copy-start | bytes 442372
  141.8 16.0 %collective-permute-start.19 = (bf16[2,3,96,128]{3,2,1,0:T(8,128)(2,1)S(1)}, bf16[2,3,96,128]{3,2,1,0:T(8,128)(2,1)S(1)}, u32[]{:S(2)}, u32[]{:S(2)}) collective-permute-start(bf16[2,3,96,128]{3,2,1,0:T(8,128)(2,1)S(1)} %get-tuple-element.62), channel_id=1, source_target_pairs={{0,8},{1,9},{2,10},{3,11},{8,0},{9,1},{10,2},{11,3},{4,12},{5,13},... | collective-permute-start | bytes 442376 | tf_op jit(solution)/shard_map/ppermute | solution.py:251
  145.1 15.1 %copy-start.19 = (bf16[2,3,96,128]{3,2,1,0:T(8,128)(2,1)}, bf16[2,3,96,128]{3,2,1,0:T(8,128)(2,1)S(1)}, u32[]{:S(2)}) copy-start(bf16[2,3,96,128]{3,2,1,0:T(8,128)(2,1)S(1)} %collective-permute-done.15.refs_3_) | copy-start | bytes 442372
  146.6 13.6 %copy-start.20 = (bf16[2,3,96,128]{3,2,1,0:T(8,128)(2,1)}, bf16[2,3,96,128]{3,2,1,0:T(8,128)(2,1)S(1)}, u32[]{:S(2)}) copy-start(bf16[2,3,96,128]{3,2,1,0:T(8,128)(2,1)S(1)} %collective-permute-done.16.refs_4_) | copy-start | bytes 442372
  154.4 5.9 %copy-start.21 = (bf16[2,3,96,128]{3,2,1,0:T(8,128)(2,1)}, bf16[2,3,96,128]{3,2,1,0:T(8,128)(2,1)S(1)}, u32[]{:S(2)}) copy-start(bf16[2,3,96,128]{3,2,1,0:T(8,128)(2,1)S(1)} %collective-permute-done.17.refs_5_) | copy-start | bytes 442372
  157.8 2.4 %copy-start.22 = (bf16[2,3,96,128]{3,2,1,0:T(8,128)(2,1)}, bf16[2,3,96,128]{3,2,1,0:T(8,128)(2,1)S(1)}, u32[]{:S(2)}) copy-start(bf16[2,3,96,128]{3,2,1,0:T(8,128)(2,1)S(1)} %collective-permute-done.18.refs_6_) | copy-start | bytes 442372
  157.8 2.4 %copy-start.23 = (bf16[2,3,96,128]{3,2,1,0:T(8,128)(2,1)}, bf16[2,3,96,128]{3,2,1,0:T(8,128)(2,1)S(1)}, u32[]{:S(2)}) copy-start(bf16[2,3,96,128]{3,2,1,0:T(8,128)(2,1)S(1)} %collective-permute-done.19.refs_7_) | copy-start | bytes 442372
  157.9 2.3 %collective-permute-start.20 = (bf16[8,3,96,128]{3,2,1,0:T(8,128)(2,1)S(1)}, bf16[8,3,96,128]{3,2,1,0:T(8,128)(2,1)S(1)}, u32[]{:S(2)}, u32[]{:S(2)}) collective-permute-start(bf16[8,3,96,128]{3,2,1,0:T(8,128)(2,1)S(1)} %dynamic-slice_dynamic-update-slice_fusion), channel_id=1, source_target_pairs={{0,4},{4,0},{1,5},{5,1},{2,6},{6,2},{3,7},{7,3},{8,12},{12,8},{9,1... | collective-permute-start | bytes 1769480 | tf_op jit(solution)/shard_map/ppermute | solution.py:371
  160.2 0.8 copy-start.28
  174.3 5.5 %copy-start.16 = (bf16[6,192,128]{2,1,0:T(8,128)(2,1)S(1)}, bf16[6,192,128]{2,1,0:T(8,128)(2,1)}, u32[]{:S(2)}) copy-start(bf16[6,192,128]{2,1,0:T(8,128)(2,1)} %get-tuple-element.65) | copy-start | bytes 884740
  174.4 10.6 %collective-permute-start.21 = (bf16[6,192,128]{2,1,0:T(8,128)(2,1)}, bf16[6,192,128]{2,1,0:T(8,128)(2,1)S(1)}, u32[]{:S(2)}, u32[]{:S(2)}) collective-permute-start(bf16[6,192,128]{2,1,0:T(8,128)(2,1)} %get-tuple-element.66), channel_id=1, source_target_pairs={{0,1},{1,2},{2,3},{3,0},{4,5},{5,6},{6,7},{7,4},{8,9},{9,10},{10,1... | collective-permute-start | bytes 884744 | tf_op jit(solution)/shard_map/ppermute | solution.py:251
  174.5 30.6 %collective-permute-start.22 = (bf16[6,192,128]{2,1,0:T(8,128)(2,1)}, bf16[6,192,128]{2,1,0:T(8,128)(2,1)S(1)}, u32[]{:S(2)}, u32[]{:S(2)}) collective-permute-start(bf16[6,192,128]{2,1,0:T(8,128)(2,1)} %get-tuple-element.67), channel_id=1, source_target_pairs={{0,2},{1,3},{2,0},{3,1},{4,6},{5,7},{6,4},{7,5},{8,10},{9,11},{10,... | collective-permute-start | bytes 884744 | tf_op jit(solution)/shard_map/ppermute | solution.py:251
  178.9 26.2 %collective-permute-start.23 = (bf16[6,192,128]{2,1,0:T(8,128)(2,1)}, bf16[6,192,128]{2,1,0:T(8,128)(2,1)S(1)}, u32[]{:S(2)}, u32[]{:S(2)}) collective-permute-start(bf16[6,192,128]{2,1,0:T(8,128)(2,1)} %get-tuple-element.68), channel_id=1, source_target_pairs={{0,3},{1,0},{2,1},{3,2},{4,7},{5,4},{6,5},{7,6},{8,11},{9,8},{10,9... | collective-permute-start | bytes 884744 | tf_op jit(solution)/shard_map/ppermute | solution.py:251
  205.2 1.0 copy-start.15
Sparse Core Ops, SparseCore 0:
  21.4 75.7 all-gather.2

commit v5 on v4

--- a/solution.py
+++ b/solution.py
@@ -331,6 +331,7 @@
                 pltpu.VMEM((lon_n, rows, cols), F32),
             ],
             4 * KW * width * size,
+            LARGE,
         )
         columns.append(
             lax.all_to_all(spec, ("lat", "co"), split_axis=0, concat_axis=0, tiled=True)

time: 214 us -> 213 us (level)
  Pallas kernels: 24.3 us -> 27.9 us
    pallas_call x4, Pallas kernels: 10.9 us -> 14.6 us  [call(): pl.pallas_call(kernel, grid_spec=pltpu.PrefetchScalarGridSpec(num_scalar_...]
    unnamed x69 -> x73, local copies, waits for them, and re-layouts: 6.75 us -> 5.63 us
  transfers between devices with their start and end apart: 26 -> 26, of which waited for: 16 -> 15; matrix products, arithmetic and copies ran while one was open for 3% -> 2% of each run, Pallas kernels for 4% -> 6%
where the time goes in v5:
time: 213 us; the launch traced here: 212 us
  waiting for transfers between devices  65.9 us (31%)
  starting transfers between devices  46.1 us (22%)
  blocking collectives  45.9 us (22%)
  Pallas kernels  27.9 us (13%)
  between operations  14 us (7%)
  local copies, waits for them, and re-layouts  10 us (5%)
    ppermute x13, waiting for transfers between devices, ring(): lax.ppermute(array, axes, [(i, (i + step) % count) for i in range(count)])  47.3 us
    all_to_all x1, blocking collectives, on_device(): lax.all_to_all(spec, ('lat', 'co'), split_axis=0, concat_axis=0, tiled=True)  23.7 us
    all_to_all x1, blocking collectives, on_device(): lax.all_to_all(back, ('lat', 'co'), split_axis=0, concat_axis=0, tiled=True)  22.2 us
    ppermute x13, starting transfers between devices, ring(): lax.ppermute(array, axes, [(i, (i + step) % count) for i in range(count)])  19.7 us
    pallas_call x4, Pallas kernels, call(): pl.pallas_call(kernel, grid_spec=pltpu.PrefetchScalarGridSpec(num_scalar_...  14.6 us
    ppermute x2, starting transfers between devices, to_far(): lax.ppermute(lax.dynamic_index_in_dim(array, 1 - zh, axis=3, keepdims=Fal...  13.6 us
    pallas_call x1, Pallas kernels, on_device(): pl.pallas_call(functools.partial(token_kernel, order), grid_spec=pltpu.Pr...  13.4 us
    all_to_all x1, starting transfers between devices, on_device(): lax.all_to_all(spec, ('lat', 'co'), split_axis=0, concat_axis=0, tiled=True)  7.32 us
  transfers between devices with their start and end apart: 26, of which 15 were waited for; matrix products, arithmetic and copies ran while one was open for 2% of the time, Pallas kernels for 6%

profile of v5, /device:TPU:96, one launch (start us, length us, event | category | flops | bytes accessed | tf_op | source)
XLA Modules:
  0.0 212.4 jit_solution(6282324070803905912)
XLA Ops:
  6.5 1.4 constant_dynamic-slice_fusion
  7.9 0.1 copy.15
  8.1 0.1 copy.16
  8.3 0.8 collective-permute-start
  9.1 1.0 collective-permute-start.1
  10.1 0.3 convert_reduce_fusion
  10.5 0.3 collective-permute-start.2
  10.7 2.4 %collective-permute-start.3 = (f32[2,24,128]{2,1,0:T(8,128)S(1)}, f32[2,24,128]{2,1,0:T(8,128)S(1)}, u32[]{:S(2)}, u32[]{:S(2)}) collective-permute-start(f32[2,24,128]{2,1,0:T(8,128)S(1)} %pad_maximum_fusion.4), channel_id=1, source_target_pairs={{0,2},{1,3},{2,0},{3,1},{4,6},{5,7},{6,4},{7,5},{8,10},{9,11},{10,... | collective-permute-start | bytes 73736 | tf_op jit(solution)/shard_map/ppermute | solution.py:251
  13.1 0.1 collective-permute-start.4
  13.3 0.6 pad_add_fusion.at
  14.0 0.9 collective-permute-done.2
  14.8 4.6 %collective-permute-done.3 = f32[2,24,128]{2,1,0:T(8,128)S(1)} collective-permute-done((f32[2,24,128]{2,1,0:T(8,128)S(1)}, f32[2,24,128]{2,1,0:T(8,128)S(1)}, u32[]{:S(2)}, u32[]{:S(2)}) %collective-permute-start.3) | collective-permute-done | bytes 24608 | tf_op jit(solution)/shard_map/ppermute | solution.py:251
  19.5 0.7 pad_maximum_fusion.1
  20.2 0.7 broadcast_in_dim.31.gain
  20.9 0.9 broadcast_in_dim.32.refs_9_
  21.9 0.4 dynamic-slice_reduce_fusion
  22.3 0.1 reshape.28
  22.4 0.1 reshape.29
  22.6 0.7 convolution_convert_fusion
  23.5 1.1 collective-permute-start.6
  24.7 5.5 %collective-permute-start.5 = (bf16[4,2,1,96,128]{4,3,2,1,0:T(8,128)(2,1)S(1)}, bf16[4,2,1,96,128]{4,3,2,1,0:T(8,128)(2,1)S(1)}, u32[]{:S(2)}, u32[]{:S(2)}) collective-permute-start(bf16[4,2,1,96,128]{4,3,2,1,0:T(8,128)(2,1)S(1)} %dynamic-slice_bitcast_fusion.3), channel_id=1, source_target_pairs={{0,8},{8,0},{1,9},{9,1},{2,10},{10,2},{3,11},{11,3},{4,12},{12,4},... | collective-permute-start | bytes 589832 | tf_op jit(solution)/shard_map/ppermute | solution.py:289
  30.1 0.8 collective-permute-start.7
  31.0 7.2 %collective-permute-done.7.partner = f32[2,2,24,128]{3,2,1,0:T(8,128)S(1)} collective-permute-done((f32[2,2,24,128]{3,2,1,0:T(8,128)S(1)}, f32[2,2,24,128]{3,2,1,0:T(8,128)S(1)}, u32[]{:S(2)}, u32[]{:S(2)}) %collective-permute-start.7) | collective-permute-done | bytes 49184 | tf_op jit(solution)/shard_map/ppermute | solution.py:300
  38.2 0.7 copy-done.10
  39.1 8.1 %collective-permute-start.11 = (bf16[4,2,2,96,128]{4,3,2,1,0:T(8,128)(2,1)S(1)}, bf16[4,2,2,96,128]{4,3,2,1,0:T(8,128)(2,1)S(1)}, u32[]{:S(2)}, u32[]{:S(2)}) collective-permute-start(bf16[4,2,2,96,128]{4,3,2,1,0:T(8,128)(2,1)S(1)} %dynamic-slice_bitcast_fusion), channel_id=1, source_target_pairs={{0,8},{8,0},{1,9},{9,1},{2,10},{10,2},{3,11},{11,3},{4,12},{12,4},... | collective-permute-start | bytes 1179656 | tf_op jit(solution)/shard_map/ppermute | solution.py:289
  47.2 0.1 collective-permute-start.8
  47.3 0.6 collective-permute-start.9
  47.9 0.7 collective-permute-done.8.near
  48.6 0.3 collective-permute-done.9.across
  48.8 0.4 copy-done.17
  49.2 0.6 copy-done.18
  49.8 3.8 %shard_map.109 = (bf16[32,16,384]{2,1,0:T(8,128)(2,1)}, f32[384,512]{1,0:T(8,128)}) custom-call(s32[3]{0:T(128)} %pad_add_fusion.at, bf16[4,2,3,2,96,128]{5,4,3,2,1,0:T(8,128)(2,1)} %bitcast.55, bf16[4,1,96,128]{3,2,1,0:T(8,128)(2,1)} %copy-done.17, bf16[4,2,1,96,128]{4,3,2,1,0:T(8,128)(2,1)} %copy-done.10, bf16[4,1,96,128]{3,2,1,0:T(8,128)(2,1)} %copy-done.18, ...), custom_call_target="tpu_custom_call" | custom-call | flops 201326592 | bytes 3424256 | tf_op jit(solution)/shard_map/pallas_call | solution.py:33
  53.6 7.3 %all-to-all-start = ((bf16[32,16,384]{2,1,0:T(8,128)(2,1)}), bf16[32,16,384]{2,1,0:T(8,128)(2,1)S(1)}, u32[]{:S(2)}, u32[]{:S(2)}) async-start(bf16[32,16,384]{2,1,0:T(8,128)(2,1)} %get-tuple-element.46), calls=%async_computation | async-start | bytes 786432 | tf_op jit(solution)/shard_map/all_to_all | solution.py:337
  61.0 0.4 collective-permute-start.10
  61.4 0.3 collective-permute-start.12
  61.7 0.8 collective-permute-done.10.near
  62.5 0.7 collective-permute-done.12.across
  63.2 0.7 copy-done.15
  63.9 4.4 %shard_map.110 = (bf16[32,16,768]{2,1,0:T(8,128)(2,1)}, f32[768,512]{1,0:T(8,128)}) custom-call(s32[3]{0:T(128)} %pad_add_fusion.at, bf16[4,2,3,2,96,128]{5,4,3,2,1,0:T(8,128)(2,1)} %bitcast.56, bf16[4,2,96,128]{3,2,1,0:T(8,128)(2,1)} %copy-done.14, bf16[4,2,2,96,128]{4,3,2,1,0:T(8,128)(2,1)} %copy-done.9, bf16[4,2,96,128]{3,2,1,0:T(8,128)(2,1)} %copy-done.15, ...), custom_call_target="tpu_custom_call" | custom-call | flops 402653184 | bytes 4997120 | tf_op jit(solution)/shard_map/pallas_call | solution.py:33
  68.3 6.9 %all-to-all-done.refs_0_ = bf16[32,16,384]{2,1,0:T(8,128)(2,1)S(1)} async-done(((bf16[32,16,384]{2,1,0:T(8,128)(2,1)}), bf16[32,16,384]{2,1,0:T(8,128)(2,1)S(1)}, u32[]{:S(2)}, u32[]{:S(2)}) %all-to-all-start) | async-done | bytes 393248 | tf_op jit(solution)/shard_map/all_to_all | solution.py:337
  75.2 23.7 %all_to_all.15.refs_1_ = bf16[32,16,768]{2,1,0:T(8,128)(2,1)S(1)} all-to-all(bf16[32,16,768]{2,1,0:T(8,128)(2,1)} %get-tuple-element.47), channel_id=1, replica_groups=mesh['lat'=16,'zh'=2,'co'=2,'ch'=4] {'lat','co'}, dimensions={0} | all-to-all | bytes 1572864 | tf_op jit(solution)/shard_map/all_to_all | solution.py:337
  98.9 4.8 %shard_map.111 = bf16[32,16,1152]{2,1,0:T(8,128)(2,1)S(1)} custom-call(s32[3]{0:T(128)S(1)} %copy-done.4, bf16[32,16,384]{2,1,0:T(8,128)(2,1)S(1)} %all-to-all-done.refs_0_, bf16[32,16,768]{2,1,0:T(8,128)(2,1)S(1)} %all_to_all.15.refs_1_, bf16[576,768]{1,0:T(8,128)(2,1)S(1)} %pad_maximum_fusion.refs_2_, bf16[256,256]{1,0:T(8,128)(2,1)S(1)} %maximum_maximum_fusion.refs_3_, ...), custom_call_target="tpu_custom_call" | custom-call | flops 1811939328 | bytes 3506176 | tf_op jit(solution)/shard_map/pallas_call | solution.py:33
  103.7 22.2 %all_to_all.16 = bf16[32,16,1152]{2,1,0:T(8,128)(2,1)S(1)} all-to-all(bf16[32,16,1152]{2,1,0:T(8,128)(2,1)S(1)} %shard_map.111), channel_id=1, replica_groups=mesh['lat'=16,'zh'=2,'co'=2,'ch'=4] {'lat','co'}, dimensions={0} | all-to-all | bytes 2359296 | tf_op jit(solution)/shard_map/all_to_all | solution.py:354
  126.0 1.0 copy-done.2
  127.0 1.6 shard_map.112
  128.6 0.8 collective-permute-start.13
  129.4 2.5 %collective-permute-start.14 = (bf16[2,3,96,128]{3,2,1,0:T(8,128)(2,1)S(1)}, bf16[2,3,96,128]{3,2,1,0:T(8,128)(2,1)S(1)}, u32[]{:S(2)}, u32[]{:S(2)}) collective-permute-start(bf16[2,3,96,128]{3,2,1,0:T(8,128)(2,1)S(1)} %get-tuple-element.57), channel_id=1, source_target_pairs={{0,1},{1,2},{2,3},{3,8},{8,9},{9,10},{10,11},{11,0},{4,5},{5,6},{6... | collective-permute-start | bytes 442376 | tf_op jit(solution)/shard_map/ppermute | solution.py:251
  132.0 4.1 %collective-permute-start.16 = (bf16[2,3,96,128]{3,2,1,0:T(8,128)(2,1)S(1)}, bf16[2,3,96,128]{3,2,1,0:T(8,128)(2,1)S(1)}, u32[]{:S(2)}, u32[]{:S(2)}) collective-permute-start(bf16[2,3,96,128]{3,2,1,0:T(8,128)(2,1)S(1)} %get-tuple-element.59), channel_id=1, source_target_pairs={{0,2},{1,3},{2,8},{3,9},{8,10},{9,11},{10,0},{11,1},{4,6},{5,7},{6... | collective-permute-start | bytes 442376 | tf_op jit(solution)/shard_map/ppermute | solution.py:251
  136.1 0.8 collective-permute-done.13.refs_1_
  136.9 4.2 %collective-permute-start.18 = (bf16[2,3,96,128]{3,2,1,0:T(8,128)(2,1)S(1)}, bf16[2,3,96,128]{3,2,1,0:T(8,128)(2,1)S(1)}, u32[]{:S(2)}, u32[]{:S(2)}) collective-permute-start(bf16[2,3,96,128]{3,2,1,0:T(8,128)(2,1)S(1)} %get-tuple-element.61), channel_id=1, source_target_pairs={{0,3},{1,8},{2,9},{3,10},{8,11},{9,0},{10,1},{11,2},{4,7},{5,12},{... | collective-permute-start | bytes 442376 | tf_op jit(solution)/shard_map/ppermute | solution.py:251
  141.2 0.2 collective-permute-start.19
  141.4 3.6 %collective-permute-done.15.refs_3_ = bf16[2,3,96,128]{3,2,1,0:T(8,128)(2,1)S(1)} collective-permute-done((bf16[2,3,96,128]{3,2,1,0:T(8,128)(2,1)S(1)}, bf16[2,3,96,128]{3,2,1,0:T(8,128)(2,1)S(1)}, u32[]{:S(2)}, u32[]{:S(2)}) %collective-permute-start.15) | collective-permute-done | bytes 147488 | tf_op jit(solution)/shard_map/ppermute | solution.py:251
  145.1 8.7 %collective-permute-done.17.refs_5_ = bf16[2,3,96,128]{3,2,1,0:T(8,128)(2,1)S(1)} collective-permute-done((bf16[2,3,96,128]{3,2,1,0:T(8,128)(2,1)S(1)}, bf16[2,3,96,128]{3,2,1,0:T(8,128)(2,1)S(1)}, u32[]{:S(2)}, u32[]{:S(2)}) %collective-permute-start.17) | collective-permute-done | bytes 147488 | tf_op jit(solution)/shard_map/ppermute | solution.py:251
  153.8 3.5 %collective-permute-done.18.refs_6_ = bf16[2,3,96,128]{3,2,1,0:T(8,128)(2,1)S(1)} collective-permute-done((bf16[2,3,96,128]{3,2,1,0:T(8,128)(2,1)S(1)}, bf16[2,3,96,128]{3,2,1,0:T(8,128)(2,1)S(1)}, u32[]{:S(2)}, u32[]{:S(2)}) %collective-permute-start.18) | collective-permute-done | bytes 147488 | tf_op jit(solution)/shard_map/ppermute | solution.py:251
  157.3 0.3 collective-permute-start.20
  157.6 2.0 collective-permute-done.20.refs_8_
  159.7 0.8 copy-done.30
  160.4 13.4 %shard_map.113 = (bf16[6,192,128]{2,1,0:T(8,128)(2,1)}, bf16[6,192,128]{2,1,0:T(8,128)(2,1)}, bf16[6,192,128]{2,1,0:T(8,128)(2,1)}, bf16[6,192,128]{2,1,0:T(8,128)(2,1)}) custom-call(s32[2]{0:T(128)} %copy-done.5, bf16[2,3,96,128]{3,2,1,0:T(8,128)(2,1)} %copy-done.3, bf16[2,3,96,128]{3,2,1,0:T(8,128)(2,1)} %copy-done.19, bf16[2,3,96,128]{3,2,1,0:T(8,128)(2,1)} %copy-done.20, ...), custom_call_target="tpu_custom_call" | custom-call | flops 7247757312 | bytes 9437184 | tf_op jit(solution)/shard_map/pallas_call | solution.py:376
  173.9 4.4 %collective-permute-start.22 = (bf16[6,192,128]{2,1,0:T(8,128)(2,1)}, bf16[6,192,128]{2,1,0:T(8,128)(2,1)S(1)}, u32[]{:S(2)}, u32[]{:S(2)}) collective-permute-start(bf16[6,192,128]{2,1,0:T(8,128)(2,1)} %get-tuple-element.67), channel_id=1, source_target_pairs={{0,2},{1,3},{2,0},{3,1},{4,6},{5,7},{6,4},{7,5},{8,10},{9,11},{10,... | collective-permute-start | bytes 884744 | tf_op jit(solution)/shard_map/ppermute | solution.py:251
  178.3 0.7 collective-permute-start.23
  179.0 0.2 broadcast_in_dim.30
  179.3 5.1 %collective-permute-done.21 = bf16[6,192,128]{2,1,0:T(8,128)(2,1)S(1)} collective-permute-done((bf16[6,192,128]{2,1,0:T(8,128)(2,1)}, bf16[6,192,128]{2,1,0:T(8,128)(2,1)S(1)}, u32[]{:S(2)}, u32[]{:S(2)}) %collective-permute-start.21) | collective-permute-done | bytes 294944 | tf_op jit(solution)/shard_map/ppermute | solution.py:251
  184.4 20.1 %collective-permute-done.22 = bf16[6,192,128]{2,1,0:T(8,128)(2,1)S(1)} collective-permute-done((bf16[6,192,128]{2,1,0:T(8,128)(2,1)}, bf16[6,192,128]{2,1,0:T(8,128)(2,1)S(1)}, u32[]{:S(2)}, u32[]{:S(2)}) %collective-permute-start.22) | collective-permute-done | bytes 294944 | tf_op jit(solution)/shard_map/ppermute | solution.py:251
  204.6 1.0 copy-done.8
  (108 shorter events, 1.2 us)
Async XLA Ops:
  6.5 3.6 %copy-start.6 = (bf16[24,192,128]{2,1,0:T(8,128)(2,1)S(1)}, bf16[24,192,128]{2,1,0:T(8,128)(2,1)}, u32[]{:S(2)}) copy-start(bf16[24,192,128]{2,1,0:T(8,128)(2,1)} %param.11) | copy-start | bytes 3538948
  6.5 119.4 %all-gather.3.cloned.1.call-start = ((), (), s32[]{:S(2)}) async-start(), calls=%async_computation.3 | async-start | bytes 9732096 | tf_op jit(solution)/shard_map/all_gather | solution.py:282
  7.9 6.0 %copy-start.31 = (f32[192]{0:T(256)S(1)}, f32[192]{0:T(256)}, u32[]{:S(2)}) copy-start(f32[192]{0:T(256)} %param.12) | copy-start | bytes 2308
  8.2 12.7 %copy-start.28 = (f32[768]{0:T(1024)S(1)}, f32[768]{0:T(1024)}, u32[]{:S(2)}) copy-start(f32[768]{0:T(1024)} %param.16) | copy-start | bytes 9220
  8.2 13.7 %copy-start.26 = (f32[2,18432]{1,0:T(2,128)S(1)}, f32[2,18432]{1,0:T(2,128)}, u32[]{:S(2)}) copy-start(f32[2,18432]{1,0:T(2,128)} %param.14) | copy-start | bytes 442372
  8.3 13.6 %copy-start.27 = (f32[2,18432]{1,0:T(2,128)S(1)}, f32[2,18432]{1,0:T(2,128)}, u32[]{:S(2)}) copy-start(f32[2,18432]{1,0:T(2,128)} %param.13) | copy-start | bytes 442372
  8.3 11.2 %collective-permute-start = (bf16[2,48,768]{2,1,0:T(8,128)(2,1)S(1)}, bf16[2,48,768]{2,1,0:T(8,128)(2,1)S(1)}, u32[]{:S(2)}, u32[]{:S(2)}) collective-permute-start(bf16[2,48,768]{2,1,0:T(8,128)(2,1)S(1)} %pad_maximum_fusion.2), channel_id=1, source_target_pairs={{0,0},{1,1},{2,2},{3,3},{4,6},{5,7},{6,4},{7,5},{8,8},{9,9},{10,10... | collective-permute-start | bytes 442376 | tf_op jit(solution)/shard_map/ppermute | solution.py:261
  9.1 10.4 %collective-permute-start.1 = (bf16[2,48,768]{2,1,0:T(8,128)(2,1)S(1)}, bf16[2,48,768]{2,1,0:T(8,128)(2,1)S(1)}, u32[]{:S(2)}, u32[]{:S(2)}) collective-permute-start(bf16[2,48,768]{2,1,0:T(8,128)(2,1)S(1)} %pad_maximum_fusion.2), channel_id=1, source_target_pairs={{0,1},{1,2},{2,3},{3,0},{4,7},{5,4},{6,5},{7,6},{8,9},{9,10},{10,1... | collective-permute-start | bytes 442376 | tf_op jit(solution)/shard_map/ppermute | solution.py:261
  10.5 4.4 %collective-permute-start.2 = (f32[2,24,128]{2,1,0:T(8,128)S(1)}, f32[2,24,128]{2,1,0:T(8,128)S(1)}, u32[]{:S(2)}, u32[]{:S(2)}) collective-permute-start(f32[2,24,128]{2,1,0:T(8,128)S(1)} %pad_maximum_fusion.4), channel_id=1, source_target_pairs={{0,1},{1,2},{2,3},{3,0},{4,5},{5,6},{6,7},{7,4},{8,9},{9,10},{10,1... | collective-permute-start | bytes 73736 | tf_op jit(solution)/shard_map/ppermute | solution.py:251
  10.7 8.7 %collective-permute-start.3 = (f32[2,24,128]{2,1,0:T(8,128)S(1)}, f32[2,24,128]{2,1,0:T(8,128)S(1)}, u32[]{:S(2)}, u32[]{:S(2)}) collective-permute-start(f32[2,24,128]{2,1,0:T(8,128)S(1)} %pad_maximum_fusion.4), channel_id=1, source_target_pairs={{0,2},{1,3},{2,0},{3,1},{4,6},{5,7},{6,4},{7,5},{8,10},{9,11},{10,... | collective-permute-start | bytes 73736 | tf_op jit(solution)/shard_map/ppermute | solution.py:251
  13.1 6.4 %collective-permute-start.4 = (f32[2,24,128]{2,1,0:T(8,128)S(1)}, f32[2,24,128]{2,1,0:T(8,128)S(1)}, u32[]{:S(2)}, u32[]{:S(2)}) collective-permute-start(f32[2,24,128]{2,1,0:T(8,128)S(1)} %pad_maximum_fusion.4), channel_id=1, source_target_pairs={{0,3},{1,0},{2,1},{3,2},{4,7},{5,4},{6,5},{7,6},{8,11},{9,8},{10,9... | collective-permute-start | bytes 73736 | tf_op jit(solution)/shard_map/ppermute | solution.py:251
  13.3 112.7 %copy-start.5 = (s32[2]{0:T(128)}, s32[2]{0:T(128)S(1)}, u32[]{:S(2)}) copy-start(s32[2]{0:T(128)S(1)} %pad_add_fusion.1.at) | copy-start | bytes 28
  20.2 2.4 %copy-start.7 = (bf16[384,1536]{1,0:T(8,128)(2,1)S(1)}, bf16[384,1536]{1,0:T(8,128)(2,1)}, u32[]{:S(2)}) copy-start(bf16[384,1536]{1,0:T(8,128)(2,1)} %constant.176.clone) | copy-start | bytes 3538948
  20.2 2.4 %copy-start.29 = (s32[288]{0:T(512)S(1)}, s32[288]{0:T(512)}, u32[]{:S(2)}) copy-start(s32[288]{0:T(512)} %param.15) | copy-start | bytes 3460
  23.5 6.7 %collective-permute-start.6 = (f32[2,24,128]{2,1,0:T(8,128)S(1)}, f32[2,24,128]{2,1,0:T(8,128)S(1)}, u32[]{:S(2)}, u32[]{:S(2)}) collective-permute-start(f32[2,24,128]{2,1,0:T(8,128)S(1)} %add_add_fusion), channel_id=1, source_target_pairs={{0,4},{4,0},{1,5},{5,1},{2,6},{6,2},{3,7},{7,3},{8,12},{12,8},{9,1... | collective-permute-start | bytes 73736 | tf_op jit(solution)/shard_map/ppermute | solution.py:299
  24.7 13.6 %collective-permute-start.5 = (bf16[4,2,1,96,128]{4,3,2,1,0:T(8,128)(2,1)S(1)}, bf16[4,2,1,96,128]{4,3,2,1,0:T(8,128)(2,1)S(1)}, u32[]{:S(2)}, u32[]{:S(2)}) collective-permute-start(bf16[4,2,1,96,128]{4,3,2,1,0:T(8,128)(2,1)S(1)} %dynamic-slice_bitcast_fusion.3), channel_id=1, source_target_pairs={{0,8},{8,0},{1,9},{9,1},{2,10},{10,2},{3,11},{11,3},{4,12},{12,4},... | collective-permute-start | bytes 589832 | tf_op jit(solution)/shard_map/ppermute | solution.py:289
  30.1 8.1 %copy-start.12 = (f32[2,2,24,128]{3,2,1,0:T(8,128)}, f32[2,2,24,128]{3,2,1,0:T(8,128)S(1)}, u32[]{:S(2)}) copy-start(f32[2,2,24,128]{3,2,1,0:T(8,128)S(1)} %pad_maximum_fusion.3.chip) | copy-start | bytes 147460
  30.1 8.1 %collective-permute-start.7 = (f32[2,2,24,128]{3,2,1,0:T(8,128)S(1)}, f32[2,2,24,128]{3,2,1,0:T(8,128)S(1)}, u32[]{:S(2)}, u32[]{:S(2)}) collective-permute-start(f32[2,2,24,128]{3,2,1,0:T(8,128)S(1)} %pad_maximum_fusion.3.chip), channel_id=1, source_target_pairs={{0,8},{8,0},{1,9},{9,1},{2,10},{10,2},{3,11},{11,3},{4,12},{12,4},... | collective-permute-start | bytes 147464 | tf_op jit(solution)/shard_map/ppermute | solution.py:300
  38.2 10.6 %copy-start.16 = (f32[2,2,24,128]{3,2,1,0:T(8,128)}, f32[2,2,24,128]{3,2,1,0:T(8,128)S(1)}, u32[]{:S(2)}) copy-start(f32[2,2,24,128]{3,2,1,0:T(8,128)S(1)} %collective-permute-done.7.partner) | copy-start | bytes 147460
  38.2 0.7 copy-start.10
  39.0 8.3 %copy-start.11 = (bf16[4,2,1,96,128]{4,3,2,1,0:T(8,128)(2,1)S(1)}, bf16[4,2,1,96,128]{4,3,2,1,0:T(8,128)(2,1)}, u32[]{:S(2)}) copy-start(bf16[4,2,1,96,128]{4,3,2,1,0:T(8,128)(2,1)} %copy-done.10) | copy-start | bytes 589828
  39.1 22.3 %collective-permute-start.11 = (bf16[4,2,2,96,128]{4,3,2,1,0:T(8,128)(2,1)S(1)}, bf16[4,2,2,96,128]{4,3,2,1,0:T(8,128)(2,1)S(1)}, u32[]{:S(2)}, u32[]{:S(2)}) collective-permute-start(bf16[4,2,2,96,128]{4,3,2,1,0:T(8,128)(2,1)S(1)} %dynamic-slice_bitcast_fusion), channel_id=1, source_target_pairs={{0,8},{8,0},{1,9},{9,1},{2,10},{10,2},{3,11},{11,3},{4,12},{12,4},... | collective-permute-start | bytes 1179656 | tf_op jit(solution)/shard_map/ppermute | solution.py:289
  47.2 1.4 collective-permute-start.8
  47.3 1.5 collective-permute-start.9
  48.6 0.6 copy-start.17
  49.2 0.6 copy-start.18
  53.6 21.6 %all-to-all-start = ((bf16[32,16,384]{2,1,0:T(8,128)(2,1)}), bf16[32,16,384]{2,1,0:T(8,128)(2,1)S(1)}, u32[]{:S(2)}, u32[]{:S(2)}) async-start(bf16[32,16,384]{2,1,0:T(8,128)(2,1)} %get-tuple-element.46), calls=%async_computation | async-start | bytes 786432 | tf_op jit(solution)/shard_map/all_to_all | solution.py:337
  61.0 1.5 collective-permute-start.10
  61.4 1.8 copy-start.9
  61.4 1.8 collective-permute-start.12
  62.5 0.7 copy-start.14
  63.2 0.7 copy-start.15
  68.3 30.6 %copy-start.4 = (s32[3]{0:T(128)S(1)}, s32[3]{0:T(128)}, u32[]{:S(2)}) copy-start(s32[3]{0:T(128)} %pad_add_fusion.at) | copy-start | bytes 40
  103.7 22.3 %copy-start = (f32[768,512]{1,0:T(8,128)S(1)}, f32[768,512]{1,0:T(8,128)}, u32[]{:S(2)}) copy-start(f32[768,512]{1,0:T(8,128)} %get-tuple-element.54.refs_1_) | copy-start | bytes 4718596
  103.7 22.3 %copy-start.1 = (f32[384,512]{1,0:T(8,128)S(1)}, f32[384,512]{1,0:T(8,128)}, u32[]{:S(2)}) copy-start(f32[384,512]{1,0:T(8,128)} %get-tuple-element.53.refs_0_) | copy-start | bytes 2359300
  126.0 1.0 copy-start.2
  128.6 31.0 %copy-start.3 = (bf16[2,3,96,128]{3,2,1,0:T(8,128)(2,1)}, bf16[2,3,96,128]{3,2,1,0:T(8,128)(2,1)S(1)}, u32[]{:S(2)}) copy-start(bf16[2,3,96,128]{3,2,1,0:T(8,128)(2,1)S(1)} %get-tuple-element.55.refs_0_) | copy-start | bytes 442372
  128.6 8.3 %collective-permute-start.13 = (bf16[2,3,96,128]{3,2,1,0:T(8,128)(2,1)S(1)}, bf16[2,3,96,128]{3,2,1,0:T(8,128)(2,1)S(1)}, u32[]{:S(2)}, u32[]{:S(2)}) collective-permute-start(bf16[2,3,96,128]{3,2,1,0:T(8,128)(2,1)S(1)} %get-tuple-element.56), channel_id=1, source_target_pairs={{0,11},{1,0},{2,1},{3,2},{8,3},{9,8},{10,9},{11,10},{4,15},{5,4},{... | collective-permute-start | bytes 442376 | tf_op jit(solution)/shard_map/ppermute | solution.py:251
  129.4 11.7 %collective-permute-start.14 = (bf16[2,3,96,128]{3,2,1,0:T(8,128)(2,1)S(1)}, bf16[2,3,96,128]{3,2,1,0:T(8,128)(2,1)S(1)}, u32[]{:S(2)}, u32[]{:S(2)}) collective-permute-start(bf16[2,3,96,128]{3,2,1,0:T(8,128)(2,1)S(1)} %get-tuple-element.57), channel_id=1, source_target_pairs={{0,1},{1,2},{2,3},{3,8},{8,9},{9,10},{10,11},{11,0},{4,5},{5,6},{6... | collective-permute-start | bytes 442376 | tf_op jit(solution)/shard_map/ppermute | solution.py:251
  132.0 13.0 %collective-permute-start.15 = (bf16[2,3,96,128]{3,2,1,0:T(8,128)(2,1)S(1)}, bf16[2,3,96,128]{3,2,1,0:T(8,128)(2,1)S(1)}, u32[]{:S(2)}, u32[]{:S(2)}) collective-permute-start(bf16[2,3,96,128]{3,2,1,0:T(8,128)(2,1)S(1)} %get-tuple-element.58), channel_id=1, source_target_pairs={{0,10},{1,11},{2,0},{3,1},{8,2},{9,3},{10,8},{11,9},{4,14},{5,15},... | collective-permute-start | bytes 442376 | tf_op jit(solution)/shard_map/ppermute | solution.py:251
  132.0 13.1 %collective-permute-start.16 = (bf16[2,3,96,128]{3,2,1,0:T(8,128)(2,1)S(1)}, bf16[2,3,96,128]{3,2,1,0:T(8,128)(2,1)S(1)}, u32[]{:S(2)}, u32[]{:S(2)}) collective-permute-start(bf16[2,3,96,128]{3,2,1,0:T(8,128)(2,1)S(1)} %get-tuple-element.59), channel_id=1, source_target_pairs={{0,2},{1,3},{2,8},{3,9},{8,10},{9,11},{10,0},{11,1},{4,6},{5,7},{6... | collective-permute-start | bytes 442376 | tf_op jit(solution)/shard_map/ppermute | solution.py:251
  136.1 17.7 %collective-permute-start.17 = (bf16[2,3,96,128]{3,2,1,0:T(8,128)(2,1)S(1)}, bf16[2,3,96,128]{3,2,1,0:T(8,128)(2,1)S(1)}, u32[]{:S(2)}, u32[]{:S(2)}) collective-permute-start(bf16[2,3,96,128]{3,2,1,0:T(8,128)(2,1)S(1)} %get-tuple-element.60), channel_id=1, source_target_pairs={{0,9},{1,10},{2,11},{3,0},{8,1},{9,2},{10,3},{11,8},{4,13},{5,14},... | collective-permute-start | bytes 442376 | tf_op jit(solution)/shard_map/ppermute | solution.py:251
  136.9 22.7 %copy-start.19 = (bf16[2,3,96,128]{3,2,1,0:T(8,128)(2,1)}, bf16[2,3,96,128]{3,2,1,0:T(8,128)(2,1)S(1)}, u32[]{:S(2)}) copy-start(bf16[2,3,96,128]{3,2,1,0:T(8,128)(2,1)S(1)} %collective-permute-done.13.refs_1_) | copy-start | bytes 442372
  136.9 20.3 %collective-permute-start.18 = (bf16[2,3,96,128]{3,2,1,0:T(8,128)(2,1)S(1)}, bf16[2,3,96,128]{3,2,1,0:T(8,128)(2,1)S(1)}, u32[]{:S(2)}, u32[]{:S(2)}) collective-permute-start(bf16[2,3,96,128]{3,2,1,0:T(8,128)(2,1)S(1)} %get-tuple-element.61), channel_id=1, source_target_pairs={{0,3},{1,8},{2,9},{3,10},{8,11},{9,0},{10,1},{11,2},{4,7},{5,12},{... | collective-permute-start | bytes 442376 | tf_op jit(solution)/shard_map/ppermute | solution.py:251
  141.2 18.5 %copy-start.20 = (bf16[2,3,96,128]{3,2,1,0:T(8,128)(2,1)}, bf16[2,3,96,128]{3,2,1,0:T(8,128)(2,1)S(1)}, u32[]{:S(2)}) copy-start(bf16[2,3,96,128]{3,2,1,0:T(8,128)(2,1)S(1)} %collective-permute-done.14.refs_2_) | copy-start | bytes 442372
  141.2 16.1 %collective-permute-start.19 = (bf16[2,3,96,128]{3,2,1,0:T(8,128)(2,1)S(1)}, bf16[2,3,96,128]{3,2,1,0:T(8,128)(2,1)S(1)}, u32[]{:S(2)}, u32[]{:S(2)}) collective-permute-start(bf16[2,3,96,128]{3,2,1,0:T(8,128)(2,1)S(1)} %get-tuple-element.62), channel_id=1, source_target_pairs={{0,8},{1,9},{2,10},{3,11},{8,0},{9,1},{10,2},{11,3},{4,12},{5,13},... | collective-permute-start | bytes 442376 | tf_op jit(solution)/shard_map/ppermute | solution.py:251
  145.0 14.6 %copy-start.21 = (bf16[2,3,96,128]{3,2,1,0:T(8,128)(2,1)}, bf16[2,3,96,128]{3,2,1,0:T(8,128)(2,1)S(1)}, u32[]{:S(2)}) copy-start(bf16[2,3,96,128]{3,2,1,0:T(8,128)(2,1)S(1)} %collective-permute-done.15.refs_3_) | copy-start | bytes 442372
  145.0 14.6 %copy-start.22 = (bf16[2,3,96,128]{3,2,1,0:T(8,128)(2,1)}, bf16[2,3,96,128]{3,2,1,0:T(8,128)(2,1)S(1)}, u32[]{:S(2)}) copy-start(bf16[2,3,96,128]{3,2,1,0:T(8,128)(2,1)S(1)} %collective-permute-done.16.refs_4_) | copy-start | bytes 442372
  153.8 5.9 %copy-start.23 = (bf16[2,3,96,128]{3,2,1,0:T(8,128)(2,1)}, bf16[2,3,96,128]{3,2,1,0:T(8,128)(2,1)S(1)}, u32[]{:S(2)}) copy-start(bf16[2,3,96,128]{3,2,1,0:T(8,128)(2,1)S(1)} %collective-permute-done.17.refs_5_) | copy-start | bytes 442372
  157.2 2.4 %copy-start.24 = (bf16[2,3,96,128]{3,2,1,0:T(8,128)(2,1)}, bf16[2,3,96,128]{3,2,1,0:T(8,128)(2,1)S(1)}, u32[]{:S(2)}) copy-start(bf16[2,3,96,128]{3,2,1,0:T(8,128)(2,1)S(1)} %collective-permute-done.18.refs_6_) | copy-start | bytes 442372
  157.3 2.4 %copy-start.25 = (bf16[2,3,96,128]{3,2,1,0:T(8,128)(2,1)}, bf16[2,3,96,128]{3,2,1,0:T(8,128)(2,1)S(1)}, u32[]{:S(2)}) copy-start(bf16[2,3,96,128]{3,2,1,0:T(8,128)(2,1)S(1)} %collective-permute-done.19.refs_7_) | copy-start | bytes 442372
  157.3 2.3 %collective-permute-start.20 = (bf16[8,3,96,128]{3,2,1,0:T(8,128)(2,1)S(1)}, bf16[8,3,96,128]{3,2,1,0:T(8,128)(2,1)S(1)}, u32[]{:S(2)}, u32[]{:S(2)}) collective-permute-start(bf16[8,3,96,128]{3,2,1,0:T(8,128)(2,1)S(1)} %dynamic-slice_dynamic-update-slice_fusion), channel_id=1, source_target_pairs={{0,4},{4,0},{1,5},{5,1},{2,6},{6,2},{3,7},{7,3},{8,12},{12,8},{9,1... | collective-permute-start | bytes 1769480 | tf_op jit(solution)/shard_map/ppermute | solution.py:372
  159.6 0.8 copy-start.30
  173.8 5.4 %copy-start.13 = (bf16[6,192,128]{2,1,0:T(8,128)(2,1)S(1)}, bf16[6,192,128]{2,1,0:T(8,128)(2,1)}, u32[]{:S(2)}) copy-start(bf16[6,192,128]{2,1,0:T(8,128)(2,1)} %get-tuple-element.65) | copy-start | bytes 884740
  173.8 10.5 %collective-permute-start.21 = (bf16[6,192,128]{2,1,0:T(8,128)(2,1)}, bf16[6,192,128]{2,1,0:T(8,128)(2,1)S(1)}, u32[]{:S(2)}, u32[]{:S(2)}) collective-permute-start(bf16[6,192,128]{2,1,0:T(8,128)(2,1)} %get-tuple-element.66), channel_id=1, source_target_pairs={{0,1},{1,2},{2,3},{3,0},{4,5},{5,6},{6,7},{7,4},{8,9},{9,10},{10,1... | collective-permute-start | bytes 884744 | tf_op jit(solution)/shard_map/ppermute | solution.py:251
  173.9 30.6 %collective-permute-start.22 = (bf16[6,192,128]{2,1,0:T(8,128)(2,1)}, bf16[6,192,128]{2,1,0:T(8,128)(2,1)S(1)}, u32[]{:S(2)}, u32[]{:S(2)}) collective-permute-start(bf16[6,192,128]{2,1,0:T(8,128)(2,1)} %get-tuple-element.67), channel_id=1, source_target_pairs={{0,2},{1,3},{2,0},{3,1},{4,6},{5,7},{6,4},{7,5},{8,10},{9,11},{10,... | collective-permute-start | bytes 884744 | tf_op jit(solution)/shard_map/ppermute | solution.py:251
  178.3 26.2 %collective-permute-start.23 = (bf16[6,192,128]{2,1,0:T(8,128)(2,1)}, bf16[6,192,128]{2,1,0:T(8,128)(2,1)S(1)}, u32[]{:S(2)}, u32[]{:S(2)}) collective-permute-start(bf16[6,192,128]{2,1,0:T(8,128)(2,1)} %get-tuple-element.68), channel_id=1, source_target_pairs={{0,3},{1,0},{2,1},{3,2},{4,7},{5,4},{6,5},{7,6},{8,11},{9,8},{10,9... | collective-permute-start | bytes 884744 | tf_op jit(solution)/shard_map/ppermute | solution.py:251
  204.6 1.0 copy-start.8
Sparse Core Ops, SparseCore 0:
  22.0 75.8 all-gather.2
